TPU v7x, 32 devices: a whole 2x2x4 slice. The times are simulated.
32 devices in a mesh: band: 4 (over y, x), grid: 8 (over z, core).
Axes of the slice: x: 2, y: 2, z: 4, core: 2. Of those that a mesh axis runs over, the one named last changes fastest.
Arguments:
- valence: bfloat16 [64, 96, 9216], P('band', 'grid'), may hold values from -6 to 6
- conduction: bfloat16 [32, 96, 9216], P('band', 'grid'), may hold values from -6 to 6
- screened: bfloat16 [6144, 6144], P('grid'), may hold values from -0.0007324219 to 0.0007324219
- blocks: int32 [2], replicated, may hold values from 0 to 7
- gsphere: int32 [6144], P('grid'), may hold values from 0 to 4095, as said below
Outputs:
- kernel: float32 [4, 64, 64], P('band', 'grid')
Inputs may be any that keep to these rules, and one draw needn't show every extreme that they name: `gsphere`: distinct within each aligned block of 768 entries.
All inputs are finite; a program needn't handle non-finite values.
Results may differ from a plain program's by a relative error of at most 0.0093.
Values may be sent and summed in bfloat16 or wider, within the bound.
No kernel may reach another device: no remote copies, remote signals or barrier semaphores. Data moves between devices by JAX's collectives and lax.ppermute only.
A program may use at most 128 MiB of HBM per device.

v0:
```python
import functools
import math

import jax
import jax.numpy as jnp
from jax import lax
from jax.experimental import pallas as pl
from jax.experimental.pallas import tpu as pltpu
from jax.sharding import PartitionSpec as P

GRID_N = 96
KF = 32
BLK = 8
XG = 4
LANES = XG * GRID_N
F32 = jnp.float32
BF16 = jnp.bfloat16


def fourier_parts(length, kept):
    positions = jnp.arange(length, dtype=jnp.int32)
    freqs = jnp.arange(kept, dtype=jnp.int32) - kept // 2
    phase = positions[:, None] * freqs[None, :] % length
    phases = phase.astype(F32) * (2.0 * math.pi / length)
    factor = 1.0 / math.sqrt(length)
    return (jnp.cos(phases) * factor).astype(BF16), (jnp.sin(phases) * factor).astype(BF16)


def y_table(cosine, sine):
    one = jnp.concatenate([cosine.T, -sine.T], axis=0)
    zero = jnp.zeros_like(one)
    return jnp.concatenate(
        [jnp.concatenate([one, zero], axis=1), jnp.concatenate([zero, one], axis=1)], axis=0
    )


def z_table(cosine, sine):
    from_real = jnp.stack([cosine, -sine], axis=1)
    from_imag = jnp.stack([sine, cosine], axis=1)
    both = jnp.stack([from_real, from_imag])
    same = jnp.eye(XG, dtype=BF16)
    table = same[None, :, None, :, None, None] * both[:, None, :, None, :, :]
    return table.reshape(2 * LANES, XG * 2 * KF)


def planes(orbitals):
    count, slab, _ = orbitals.shape
    groups = -(-slab // XG)
    orbitals = jnp.pad(orbitals, ((0, 0), (0, groups * XG - slab), (0, 0)))
    orbitals = orbitals.reshape(count, groups, XG, GRID_N, GRID_N)
    return jnp.transpose(orbitals, (0, 1, 3, 2, 4)).reshape(count, groups, GRID_N, LANES)


def front_kernel(here, val, cond, ytab, ztab, pick, wave, even, odd, mixed, section):
    conds, groups = cond.shape[0], cond.shape[1]
    cols = pick.shape[1]
    own_y = cols // KF
    for pair in range(conds // 2):
        for group in range(groups):
            orbital = val[0, group]
            density = jnp.concatenate(
                [orbital * cond[2 * pair, group], orbital * cond[2 * pair + 1, group]], axis=0
            )
            out = jnp.dot(ytab[...], density, preferred_element_type=F32).astype(BF16)
            for half in range(2):
                row = (2 * pair + half) * KF
                base = half * 2 * KF
                mixed[group, row:row + KF, :LANES] = out[base:base + KF]
                mixed[group, row:row + KF, LANES:] = out[base + KF:base + 2 * KF]
    for group in range(groups):
        value = jnp.dot(mixed[group], ztab[...], preferred_element_type=F32)
        section[2 * group] = value[:, :128]
        section[2 * group + 1] = value[:, 128:]

    def one_target(step, parity, out_ref):
        order = 2 * step + parity
        target = here[0] ^ order
        first = target * own_y
        parts = []
        for group in range(groups):
            for half in range(2):
                rows = [
                    section[2 * group + half, pl.ds(first + y, conds, stride=KF), :]
                    for y in range(own_y)
                ]
                for piece in range(4):
                    cut = slice(KF * piece, KF * piece + KF)
                    parts.append(jnp.concatenate([row[:, cut] for row in rows], axis=1))
        left = jnp.concatenate(parts, axis=0).astype(BF16)
        found = jnp.dot(left, pick[order], preferred_element_type=F32)
        real = imag = None
        count = XG * groups
        for x in range(count):
            cosine = wave[order, x:x + 1, :]
            sine = wave[order, count + x:count + x + 1, :]
            re = found[2 * x * conds:(2 * x + 1) * conds]
            im = found[(2 * x + 1) * conds:(2 * x + 2) * conds]
            add_real = re * cosine + im * sine
            add_imag = im * cosine - re * sine
            real = add_real if real is None else real + add_real
            imag = add_imag if imag is None else imag + add_imag
        out_ref[step] = jnp.concatenate([real, imag], axis=0).astype(BF16)

    def body(step, carry):
        one_target(step, 0, even)
        one_target(step, 1, odd)
        return carry

    lax.fori_loop(0, even.shape[0], body, 0)


def front(here, vals, cond, ytab, ztab, pick, wave):
    count, groups = vals.shape[:2]
    conds = cond.shape[0]
    targets, cols, own = pick.shape
    rows = 2 * conds
    shape = jax.ShapeDtypeStruct((targets // 2, count * rows, own), BF16)
    whole = lambda a: pl.BlockSpec(a.shape, lambda v, h: (0,) * a.ndim)
    spec = pltpu.PrefetchScalarGridSpec(
        num_scalar_prefetch=1,
        grid=(count,),
        in_specs=[
            pl.BlockSpec((1,) + vals.shape[1:], lambda v, h: (v, 0, 0, 0)),
            whole(cond), whole(ytab), whole(ztab), whole(pick), whole(wave),
        ],
        out_specs=[pl.BlockSpec((targets // 2, rows, own), lambda v, h: (0, v, 0))] * 2,
        scratch_shapes=[
            pltpu.VMEM((groups, conds * KF, 2 * LANES), BF16),
            pltpu.VMEM((2 * groups, conds * KF, XG * KF), F32),
        ],
    )
    return pl.pallas_call(
        front_kernel,
        grid_spec=spec,
        out_shape=[shape, shape],
        compiler_params=pltpu.CompilerParams(vmem_limit_bytes=48 * 1024 * 1024),
        cost_estimate=pl.CostEstimate(flops=count * 900_000_000, bytes_accessed=count * 2_000_000, transcendentals=0),
        name="front",
    )(here, vals, cond, ytab, ztab, pick, wave)


def screen_kernel(here, *refs):
    *pieces, w_even, w_odd, even, odd, side = refs

    @pl.when(pl.program_id(0) == 0)
    def _():
        total = pieces[0][...].astype(F32)
        for piece in pieces[1:]:
            total = total + piece[...].astype(F32)
        side[...] = total.astype(BF16)

    even[0] = jnp.dot(side[...], w_even[...], preferred_element_type=F32).astype(BF16)
    odd[0] = jnp.dot(side[...], w_odd[...], preferred_element_type=F32).astype(BF16)


def screen(here, pieces, screened, targets):
    rows, own = pieces[0].shape
    if own % 128:
        side = sum(p.astype(F32) for p in pieces).astype(BF16)
        part = jnp.dot(side, screened, preferred_element_type=F32).astype(BF16)
        part = jnp.transpose(part.reshape(rows, targets, own), (1, 0, 2))
        part = jnp.take(part, here[0] ^ jnp.arange(targets), axis=0)
        return part[0::2], part[1::2]
    shape = jax.ShapeDtypeStruct((targets // 2, rows, own), BF16)
    spec = pltpu.PrefetchScalarGridSpec(
        num_scalar_prefetch=1,
        grid=(targets // 2,),
        in_specs=[pl.BlockSpec((rows, own), lambda r, h: (0, 0))] * len(pieces) + [
            pl.BlockSpec((own, own), lambda r, h: (0, h[0] ^ (2 * r))),
            pl.BlockSpec((own, own), lambda r, h: (0, h[0] ^ (2 * r + 1))),
        ],
        out_specs=[pl.BlockSpec((1, rows, own), lambda r, h: (r, 0, 0))] * 2,
        scratch_shapes=[pltpu.VMEM((rows, own), BF16)],
    )
    return pl.pallas_call(
        screen_kernel,
        grid_spec=spec,
        out_shape=[shape, shape],
        compiler_params=pltpu.CompilerParams(vmem_limit_bytes=32 * 1024 * 1024),
        cost_estimate=pl.CostEstimate(flops=2 * rows * own * own * targets, bytes_accessed=2 * own * own * targets, transcendentals=0),
        name="screen",
    )(here, *pieces, screened, screened)


def close_kernel(count, first, *refs):
    ins, out = refs[:-1], refs[-1]
    sides = []
    for group in (ins[:count], ins[count:]):
        total = group[0][...].astype(F32)
        for piece in group[1:]:
            total = total + piece[...].astype(F32)
        rows, own = total.shape
        total = total.reshape(rows // (2 * first), 2, first, own)
        sides.append([total[:, part].reshape(rows // 2, own).astype(BF16) for part in range(2)])
    product = None
    for left, right in zip(*sides, strict=True):
        term = lax.dot_general(left, right, (((1,), (1,)), ((), ())), preferred_element_type=F32)
        product = term if product is None else product + term
    out[...] = product


def close(u_pieces, b_pieces, conds):
    rows = u_pieces[0].shape[0] // 2
    return pl.pallas_call(
        functools.partial(close_kernel, len(u_pieces), conds),
        out_shape=jax.ShapeDtypeStruct((rows, rows), F32),
        name="close",
    )(*u_pieces, *b_pieces)


def swap(array, axis, mask, size):
    return lax.ppermute(array, axis, [(i, i ^ mask) for i in range(size)])


def gather_sums(even, odd, targets):
    total = (even.astype(F32) + swap(odd, "grid", 1, targets).astype(F32)).astype(even.dtype)
    return [total[0]] + [swap(total[r], "grid", 2 * r, targets) for r in range(1, targets // 2)]


def ring_order(size):
    return [0, 1, 3, 2] if size == 4 else list(range(size))


def round_ring(own, holder, size, reverse):
    order = ring_order(size)
    if reverse:
        order = order[::-1]
    pairs = [(order[i], order[(i + 1) % size]) for i in range(size)]
    place = [0] * size
    for i, device in enumerate(order):
        place[device] = i
    place = jnp.array(place, jnp.int32)
    away = (place[lax.axis_index("band")] - place[holder]) % size
    chunks = len(own)
    got = []
    for step in range(chunks + size - 2):
        mine = own[min(step, chunks - 1)]
        sent = mine if step == 0 else jnp.where(away == 0, mine, got[-1])
        got.append(lax.ppermute(sent, "band", pairs))
    out = []
    for j in range(chunks):
        value = own[j]
        for hop in range(1, size):
            value = jnp.where(away == hop, got[j + hop - 1], value)
        out.append(value)
    return out


def per_device(sizes, valence, conduction, screened, blocks, gsphere):
    n_band, n_grid = sizes
    held = valence.shape[0] // BLK
    conds, slab = conduction.shape[:2]
    cols = KF // n_grid * KF
    here = lax.axis_index("grid").astype(jnp.int32)
    at = here[None]

    cosine, sine = fourier_parts(GRID_N, KF)
    ytab, ztab = y_table(cosine, sine), z_table(cosine, sine)
    targets = here ^ jnp.arange(n_grid, dtype=jnp.int32)
    points = jnp.take(lax.all_gather(gsphere, "grid", axis=0), targets, axis=0)
    pick = (jnp.arange(cols, dtype=jnp.int32)[None, :, None] == (points % cols)[:, None, :]).astype(BF16)
    turn = (jnp.arange(KF, dtype=jnp.int32)[None, :, None] == (points // cols)[:, None, :]).astype(BF16)
    fill = -slab % XG
    local = lambda t: jnp.pad(lax.dynamic_slice_in_dim(t, here * slab, slab, 0), ((0, fill), (0, 0)))
    phase = jnp.concatenate([local(cosine), local(sine)], axis=0)
    wave = jnp.einsum("xq,rqn->rxn", phase, turn, preferred_element_type=F32)

    cond = planes(conduction)

    def chosen(block):
        mine = planes(lax.dynamic_slice_in_dim(valence, block % held * BLK, BLK, 0))
        holder = block // held
        half = BLK // 2
        right = round_ring([mine[j] for j in range(half)], holder, n_band, False)
        left = round_ring([mine[j] for j in range(half, BLK)], holder, n_band, True)
        return jnp.stack(right + left)

    side_a = gather_sums(*front(at, chosen(blocks[0]), cond, ytab, ztab, pick, wave), n_grid)
    part_b = front(at, chosen(blocks[1]), cond, ytab, ztab, pick, wave)
    part_u = screen(at, side_a, screened, n_grid)
    side_b = gather_sums(*part_b, n_grid)
    side_u = gather_sums(*part_u, n_grid)
    share = close(side_u, side_b, conds)
    share = jnp.take(share.reshape(n_grid, -1, share.shape[1]), targets, axis=0)
    pieces = gather_sums(share[0::2], share[1::2], n_grid)
    return sum(pieces)[None]


def solution(mesh):
    sizes = (mesh.shape["band"], mesh.shape["grid"])
    in_specs = (P("band", "grid", None), P("band", "grid", None), P("grid", None), P(), P("grid"))
    out_specs = P("band", "grid", None)
    return jax.shard_map(
        functools.partial(per_device, sizes), mesh=mesh, in_specs=in_specs, out_specs=out_specs, check_vma=False
    )
```

profile of v0, /device:TPU:0, one launch (start us, length us, event | category | flops | bytes accessed | tf_op | source)
XLA Modules:
  0.0 265.8 jit_solution(4701818281880127969)
XLA Ops:
  5.0 4.0 %constant_dynamic-slice_fusion = (bf16[8,12,9216]{2,0,1:T(8,128)(2,1)}, bf16[8,12,9216]{2,0,1:T(8,128)(2,1)}) fusion(bf16[16,12,9216]{2,0,1:T(8,128)(2,1)} %param.9, s32[]{:T(128)S(6)} %select_n.517, s32[]{:T(128)S(6)} %select_n.461), kind=kLoop, calls=%fused_computation.127 | loop fusion | bytes 7077896 | tf_op jit(solution)/shard_map/dynamic_slice | solution.py:271
  9.0 3.7 %reshape.254 = bf16[8,3,4,96,96]{4,3,0,2,1:T(8,128)(2,1)S(1)} reshape(bf16[8,12,9216]{2,0,1:T(8,128)(2,1)} %get-tuple-element.18) | data formatting | bytes 3538944 | tf_op jit(solution)/shard_map/reshape | solution.py:50
  14.9 2.9 %collective-permute-start = (bf16[3,96,384]{2,1,0:T(8,128)(2,1)}, bf16[3,96,384]{2,1,0:T(8,128)(2,1)}, u32[]{:S(2)}, u32[]{:S(2)}) collective-permute-start(bf16[3,96,384]{2,1,0:T(8,128)(2,1)} %squeeze.113), channel_id=1, source_target_pairs={{0,8},{8,24},{24,16},{16,0},{1,9},{9,25},{25,17},{17,1},{2,10},{10... | collective-permute-start | bytes 663560 | tf_op jit(solution)/shard_map/ppermute | solution.py:239
  19.9 3.7 %reshape.257 = bf16[8,3,4,96,96]{4,3,0,2,1:T(8,128)(2,1)S(1)} reshape(bf16[8,12,9216]{2,0,1:T(8,128)(2,1)} %get-tuple-element.17) | data formatting | bytes 3538944 | tf_op jit(solution)/shard_map/reshape | solution.py:50
  26.0 2.0 collective-permute-start.20
  43.1 3.3 %reshape.255 = bf16[8,3,4,96,96]{4,3,0,2,1:T(8,128)(2,1)} reshape(bf16[8,12,9216]{2,0,1:T(8,128)(2,1)S(1)} %copy-done.15) | data formatting | bytes 3538944 | tf_op jit(solution)/shard_map/reshape | solution.py:50
  46.5 3.5 %copy.97 = bf16[8,3,4,96,96]{4,2,3,1,0:T(4,128)(2,1)S(1)} copy(bf16[8,3,4,96,96]{4,3,0,2,1:T(8,128)(2,1)} %reshape.255) | data formatting | bytes 3538944 | tf_op jit(solution)/shard_map/reshape | solution.py:50
  49.9 2.7 %reshape.256.cond = bf16[8,3,96,384]{3,2,1,0:T(8,128)(2,1)} reshape(bf16[8,3,96,4,96]{4,3,2,1,0:T(4,128)(2,1)S(1)} %bitcast.113) | data formatting | bytes 3538944 | tf_op jit(solution)/shard_map/reshape | solution.py:51
  53.7 14.8 %all-gather.1 = s32[8,1,768]{2,1,0:T(1,128)S(1)} all-gather(s32[1,1,768]{2,1,0:T(1,128)S(1)} %reshape.276), channel_id=2, replica_groups=mesh['band'=4,'grid'=8] {'grid'}, dimensions={0}, use_global_device_ids=true | all-gather | bytes 27648 | tf_op jit(solution)/shard_map/all_gather | solution.py:260
  70.8 1.9 squeeze.128
  73.6 1.9 squeeze.129
  75.5 1.9 copy.86
  77.3 1.9 squeeze.131
  79.2 1.8 copy.87
  81.1 1.9 squeeze.132
  83.9 1.9 squeeze.133
  136.9 24.0 %front.2 = (bf16[4,128,768]{2,1,0:T(8,128)(2,1)S(1)}, bf16[4,128,768]{2,1,0:T(8,128)(2,1)}) custom-call(s32[1]{0:T(128)} %bitcast.here, bf16[8,3,96,384]{3,2,1,0:T(8,128)(2,1)S(1)} %bitcast_dynamic-update-slice_fusion.8.val, bf16[8,3,96,384]{3,2,1,0:T(8,128)(2,1)} %reshape.256.cond, bf16[128,192]{1,0:T(8,128)(2,1)S(1)} %fusion.4.ytab, ...), custom_call_target="tpu_custom_call" | custom-call | flops 7200000000 | bytes 16000000 | tf_op jit(solution)/shard_map/front/pallas_call | solution.py:132
  163.8 24.3 %front.3 = (bf16[4,128,768]{2,1,0:T(8,128)(2,1)S(1)}, bf16[4,128,768]{2,1,0:T(8,128)(2,1)}) custom-call(s32[1]{0:T(128)} %bitcast.here, bf16[8,3,96,384]{3,2,1,0:T(8,128)(2,1)S(1)} %bitcast_dynamic-update-slice_fusion.val, bf16[8,3,96,384]{3,2,1,0:T(8,128)(2,1)} %reshape.256.cond, bf16[128,192]{1,0:T(8,128)(2,1)S(1)} %fusion.4.ytab, ...), custom_call_target="tpu_custom_call" | custom-call | flops 7200000000 | bytes 16000000 | tf_op jit(solution)/shard_map/front/pallas_call | solution.py:132
  191.8 2.3 collective-permute-start.14
  194.6 5.7 %collective-permute-done.13.refs_1_ = bf16[128,768]{1,0:T(8,128)(2,1)S(1)} collective-permute-done((bf16[128,768]{1,0:T(8,128)(2,1)S(1)}, bf16[128,768]{1,0:T(8,128)(2,1)S(1)}, u32[]{:S(2)}, u32[]{:S(2)}) %collective-permute-start.13) | collective-permute-done | bytes 196640 | tf_op jit(solution)/shard_map/ppermute | solution.py:212
  200.3 8.7 %collective-permute-done.14.refs_2_ = bf16[128,768]{1,0:T(8,128)(2,1)S(1)} collective-permute-done((bf16[128,768]{1,0:T(8,128)(2,1)S(1)}, bf16[128,768]{1,0:T(8,128)(2,1)S(1)}, u32[]{:S(2)}, u32[]{:S(2)}) %collective-permute-start.14) | collective-permute-done | bytes 196640 | tf_op jit(solution)/shard_map/ppermute | solution.py:212
  209.0 2.8 %screen.1 = (bf16[4,128,768]{2,1,0:T(8,128)(2,1)S(1)}, bf16[4,128,768]{2,1,0:T(8,128)(2,1)S(1)}) custom-call(s32[1]{0:T(128)} %bitcast.here, bf16[128,768]{1,0:T(8,128)(2,1)S(1)} %get-tuple-element.46.refs_0_, bf16[128,768]{1,0:T(8,128)(2,1)S(1)} %collective-permute-done.13.refs_1_, bf16[128,768]{1,0:T(8,128)(2,1)S(1)} %collective-permute-done.14.refs_2_, ...), custom_call_target="tpu_custom_call" | custom-call | flops 1207959552 | bytes 9437184 | tf_op jit(solution)/shard_map/screen/pallas_call | solution.py:175
  212.8 3.5 %collective-permute-start.33 = (bf16[128,768]{1,0:T(8,128)(2,1)S(1)}, bf16[128,768]{1,0:T(8,128)(2,1)S(1)}, u32[]{:S(2)}, u32[]{:S(2)}) collective-permute-start(bf16[128,768]{1,0:T(8,128)(2,1)S(1)} %get-tuple-element.37), channel_id=1, source_target_pairs={{0,2},{1,3},{2,0},{3,1},{4,6},{5,7},{6,4},{7,5},{8,10},{9,11},{10,... | collective-permute-start | bytes 589832 | tf_op jit(solution)/shard_map/ppermute | solution.py:212
  216.9 1.8 collective-permute-start.35
  222.2 3.4 %collective-permute-done.33.refs_5_ = bf16[128,768]{1,0:T(8,128)(2,1)S(1)} collective-permute-done((bf16[128,768]{1,0:T(8,128)(2,1)S(1)}, bf16[128,768]{1,0:T(8,128)(2,1)S(1)}, u32[]{:S(2)}, u32[]{:S(2)}) %collective-permute-start.33) | collective-permute-done | bytes 196640 | tf_op jit(solution)/shard_map/ppermute | solution.py:212
  225.7 1.9 collective-permute-start.19
  227.6 5.9 %collective-permute-done.34.refs_6_ = bf16[128,768]{1,0:T(8,128)(2,1)S(1)} collective-permute-done((bf16[128,768]{1,0:T(8,128)(2,1)S(1)}, bf16[128,768]{1,0:T(8,128)(2,1)S(1)}, u32[]{:S(2)}, u32[]{:S(2)}) %collective-permute-start.34) | collective-permute-done | bytes 196640 | tf_op jit(solution)/shard_map/ppermute | solution.py:212
  234.6 15.8 %collective-permute-done.18.refs_2_ = bf16[128,768]{1,0:T(8,128)(2,1)S(1)} collective-permute-done((bf16[128,768]{1,0:T(8,128)(2,1)S(1)}, bf16[128,768]{1,0:T(8,128)(2,1)S(1)}, u32[]{:S(2)}, u32[]{:S(2)}) %collective-permute-start.18) | collective-permute-done | bytes 196640 | tf_op jit(solution)/shard_map/ppermute | solution.py:212
  251.1 2.4 close.1
  256.1 2.0 collective-permute-start.39
  258.2 3.4 %collective-permute-start.38 = (f32[8,64]{1,0:T(8,128)S(1)}, f32[8,64]{1,0:T(8,128)S(1)}, u32[]{:S(2)}, u32[]{:S(2)}) collective-permute-start(f32[8,64]{1,0:T(8,128)S(1)} %get-tuple-element.51), channel_id=1, source_target_pairs={{0,4},{1,5},{2,6},{3,7},{4,0},{5,1},{6,2},{7,3},{8,12},{9,13},{10,... | collective-permute-start | bytes 6152 | tf_op jit(solution)/shard_map/ppermute | solution.py:212
  263.2 2.0 collective-permute-done.37
  (239 shorter events, 90.9 us)
Async XLA Ops:
  14.9 71.8 %collective-permute-start = (bf16[3,96,384]{2,1,0:T(8,128)(2,1)}, bf16[3,96,384]{2,1,0:T(8,128)(2,1)}, u32[]{:S(2)}, u32[]{:S(2)}) collective-permute-start(bf16[3,96,384]{2,1,0:T(8,128)(2,1)} %squeeze.113), channel_id=1, source_target_pairs={{0,8},{8,24},{24,16},{16,0},{1,9},{9,25},{25,17},{17,1},{2,10},{10... | collective-permute-start | bytes 663560 | tf_op jit(solution)/shard_map/ppermute | solution.py:239
  19.9 69.7 %collective-permute-start.6 = (bf16[3,96,384]{2,1,0:T(8,128)(2,1)}, bf16[3,96,384]{2,1,0:T(8,128)(2,1)}, u32[]{:S(2)}, u32[]{:S(2)}) collective-permute-start(bf16[3,96,384]{2,1,0:T(8,128)(2,1)} %squeeze.117), channel_id=1, source_target_pairs={{16,24},{24,8},{8,0},{0,16},{17,25},{25,9},{9,1},{1,17},{18,26},{2... | collective-permute-start | bytes 663560 | tf_op jit(solution)/shard_map/ppermute | solution.py:239
  26.0 65.1 %collective-permute-start.20 = (bf16[3,96,384]{2,1,0:T(8,128)(2,1)}, bf16[3,96,384]{2,1,0:T(8,128)(2,1)}, u32[]{:S(2)}, u32[]{:S(2)}) collective-permute-start(bf16[3,96,384]{2,1,0:T(8,128)(2,1)} %squeeze.130), channel_id=1, source_target_pairs={{0,8},{8,24},{24,16},{16,0},{1,9},{9,25},{25,17},{17,1},{2,10},{10... | collective-permute-start | bytes 663560 | tf_op jit(solution)/shard_map/ppermute | solution.py:239
  30.0 63.6 %collective-permute-start.26 = (bf16[3,96,384]{2,1,0:T(8,128)(2,1)}, bf16[3,96,384]{2,1,0:T(8,128)(2,1)}, u32[]{:S(2)}, u32[]{:S(2)}) collective-permute-start(bf16[3,96,384]{2,1,0:T(8,128)(2,1)} %squeeze.134), channel_id=1, source_target_pairs={{16,24},{24,8},{8,0},{0,16},{17,25},{25,9},{9,1},{1,17},{18,26},{2... | collective-permute-start | bytes 663560 | tf_op jit(solution)/shard_map/ppermute | solution.py:239
  92.1 9.0 %collective-permute-start.21 = (bf16[3,96,384]{2,1,0:T(8,128)(2,1)S(1)}, bf16[3,96,384]{2,1,0:T(8,128)(2,1)S(1)}, u32[]{:S(2)}, u32[]{:S(2)}) collective-permute-start(bf16[3,96,384]{2,1,0:T(8,128)(2,1)S(1)} %broadcast_select_fusion.9), channel_id=1, source_target_pairs={{0,8},{8,24},{24,16},{16,0},{1,9},{9,25},{25,17},{17,1},{2,10},{10... | collective-permute-start | bytes 663560 | tf_op jit(solution)/shard_map/ppermute | solution.py:239
  94.6 9.0 %collective-permute-start.27 = (bf16[3,96,384]{2,1,0:T(8,128)(2,1)S(1)}, bf16[3,96,384]{2,1,0:T(8,128)(2,1)S(1)}, u32[]{:S(2)}, u32[]{:S(2)}) collective-permute-start(bf16[3,96,384]{2,1,0:T(8,128)(2,1)S(1)} %broadcast_select_fusion.4), channel_id=1, source_target_pairs={{16,24},{24,8},{8,0},{0,16},{17,25},{25,9},{9,1},{1,17},{18,26},{2... | collective-permute-start | bytes 663560 | tf_op jit(solution)/shard_map/ppermute | solution.py:239
  96.3 9.4 %collective-permute-start.2 = (bf16[3,96,384]{2,1,0:T(8,128)(2,1)S(1)}, bf16[3,96,384]{2,1,0:T(8,128)(2,1)S(1)}, u32[]{:S(2)}, u32[]{:S(2)}) collective-permute-start(bf16[3,96,384]{2,1,0:T(8,128)(2,1)S(1)} %broadcast_select_fusion.18), channel_id=1, source_target_pairs={{0,8},{8,24},{24,16},{16,0},{1,9},{9,25},{25,17},{17,1},{2,10},{10... | collective-permute-start | bytes 663560 | tf_op jit(solution)/shard_map/ppermute | solution.py:239
  98.9 9.4 %collective-permute-start.8 = (bf16[3,96,384]{2,1,0:T(8,128)(2,1)S(1)}, bf16[3,96,384]{2,1,0:T(8,128)(2,1)S(1)}, u32[]{:S(2)}, u32[]{:S(2)}) collective-permute-start(bf16[3,96,384]{2,1,0:T(8,128)(2,1)S(1)} %broadcast_select_fusion.13), channel_id=1, source_target_pairs={{16,24},{24,8},{8,0},{0,16},{17,25},{25,9},{9,1},{1,17},{18,26},{2... | collective-permute-start | bytes 663560 | tf_op jit(solution)/shard_map/ppermute | solution.py:239
  101.1 9.4 %collective-permute-start.22 = (bf16[3,96,384]{2,1,0:T(8,128)(2,1)S(1)}, bf16[3,96,384]{2,1,0:T(8,128)(2,1)S(1)}, u32[]{:S(2)}, u32[]{:S(2)}) collective-permute-start(bf16[3,96,384]{2,1,0:T(8,128)(2,1)S(1)} %broadcast_select_fusion.8), channel_id=1, source_target_pairs={{0,8},{8,24},{24,16},{16,0},{1,9},{9,25},{25,17},{17,1},{2,10},{10... | collective-permute-start | bytes 663560 | tf_op jit(solution)/shard_map/ppermute | solution.py:239
  103.6 9.4 %collective-permute-start.28 = (bf16[3,96,384]{2,1,0:T(8,128)(2,1)S(1)}, bf16[3,96,384]{2,1,0:T(8,128)(2,1)S(1)}, u32[]{:S(2)}, u32[]{:S(2)}) collective-permute-start(bf16[3,96,384]{2,1,0:T(8,128)(2,1)S(1)} %broadcast_select_fusion.3), channel_id=1, source_target_pairs={{16,24},{24,8},{8,0},{0,16},{17,25},{25,9},{9,1},{1,17},{18,26},{2... | collective-permute-start | bytes 663560 | tf_op jit(solution)/shard_map/ppermute | solution.py:239
  105.8 10.1 %collective-permute-start.3 = (bf16[3,96,384]{2,1,0:T(8,128)(2,1)S(1)}, bf16[3,96,384]{2,1,0:T(8,128)(2,1)S(1)}, u32[]{:S(2)}, u32[]{:S(2)}) collective-permute-start(bf16[3,96,384]{2,1,0:T(8,128)(2,1)S(1)} %broadcast_select_fusion.17), channel_id=1, source_target_pairs={{0,8},{8,24},{24,16},{16,0},{1,9},{9,25},{25,17},{17,1},{2,10},{10... | collective-permute-start | bytes 663560 | tf_op jit(solution)/shard_map/ppermute | solution.py:239
  108.4 9.4 %collective-permute-start.9 = (bf16[3,96,384]{2,1,0:T(8,128)(2,1)S(1)}, bf16[3,96,384]{2,1,0:T(8,128)(2,1)S(1)}, u32[]{:S(2)}, u32[]{:S(2)}) collective-permute-start(bf16[3,96,384]{2,1,0:T(8,128)(2,1)S(1)} %broadcast_select_fusion.12), channel_id=1, source_target_pairs={{16,24},{24,8},{8,0},{0,16},{17,25},{25,9},{9,1},{1,17},{18,26},{2... | collective-permute-start | bytes 663560 | tf_op jit(solution)/shard_map/ppermute | solution.py:239
  110.5 9.4 %collective-permute-start.23 = (bf16[3,96,384]{2,1,0:T(8,128)(2,1)S(1)}, bf16[3,96,384]{2,1,0:T(8,128)(2,1)S(1)}, u32[]{:S(2)}, u32[]{:S(2)}) collective-permute-start(bf16[3,96,384]{2,1,0:T(8,128)(2,1)S(1)} %broadcast_select_fusion.7), channel_id=1, source_target_pairs={{0,8},{8,24},{24,16},{16,0},{1,9},{9,25},{25,17},{17,1},{2,10},{10... | collective-permute-start | bytes 663560 | tf_op jit(solution)/shard_map/ppermute | solution.py:239
  113.1 9.4 %collective-permute-start.29 = (bf16[3,96,384]{2,1,0:T(8,128)(2,1)S(1)}, bf16[3,96,384]{2,1,0:T(8,128)(2,1)S(1)}, u32[]{:S(2)}, u32[]{:S(2)}) collective-permute-start(bf16[3,96,384]{2,1,0:T(8,128)(2,1)S(1)} %broadcast_select_fusion.2), channel_id=1, source_target_pairs={{16,24},{24,8},{8,0},{0,16},{17,25},{25,9},{9,1},{1,17},{18,26},{2... | collective-permute-start | bytes 663560 | tf_op jit(solution)/shard_map/ppermute | solution.py:239
  117.8 9.4 %collective-permute-start.10 = (bf16[3,96,384]{2,1,0:T(8,128)(2,1)S(1)}, bf16[3,96,384]{2,1,0:T(8,128)(2,1)S(1)}, u32[]{:S(2)}, u32[]{:S(2)}) collective-permute-start(bf16[3,96,384]{2,1,0:T(8,128)(2,1)S(1)} %broadcast_select_fusion.11), channel_id=1, source_target_pairs={{16,24},{24,8},{8,0},{0,16},{17,25},{25,9},{9,1},{1,17},{18,26},{2... | collective-permute-start | bytes 663560 | tf_op jit(solution)/shard_map/ppermute | solution.py:239
  120.0 9.4 %collective-permute-start.24 = (bf16[3,96,384]{2,1,0:T(8,128)(2,1)S(1)}, bf16[3,96,384]{2,1,0:T(8,128)(2,1)S(1)}, u32[]{:S(2)}, u32[]{:S(2)}) collective-permute-start(bf16[3,96,384]{2,1,0:T(8,128)(2,1)S(1)} %broadcast_select_fusion.6), channel_id=1, source_target_pairs={{0,8},{8,24},{24,16},{16,0},{1,9},{9,25},{25,17},{17,1},{2,10},{10... | collective-permute-start | bytes 663560 | tf_op jit(solution)/shard_map/ppermute | solution.py:239
  122.6 9.4 %collective-permute-start.30 = (bf16[3,96,384]{2,1,0:T(8,128)(2,1)S(1)}, bf16[3,96,384]{2,1,0:T(8,128)(2,1)S(1)}, u32[]{:S(2)}, u32[]{:S(2)}) collective-permute-start(bf16[3,96,384]{2,1,0:T(8,128)(2,1)S(1)} %broadcast_select_fusion.1), channel_id=1, source_target_pairs={{16,24},{24,8},{8,0},{0,16},{17,25},{25,9},{9,1},{1,17},{18,26},{2... | collective-permute-start | bytes 663560 | tf_op jit(solution)/shard_map/ppermute | solution.py:239
  124.8 9.4 %collective-permute-start.5 = (bf16[3,96,384]{2,1,0:T(8,128)(2,1)S(1)}, bf16[3,96,384]{2,1,0:T(8,128)(2,1)S(1)}, u32[]{:S(2)}, u32[]{:S(2)}) collective-permute-start(bf16[3,96,384]{2,1,0:T(8,128)(2,1)S(1)} %broadcast_select_fusion.15), channel_id=1, source_target_pairs={{0,8},{8,24},{24,16},{16,0},{1,9},{9,25},{25,17},{17,1},{2,10},{10... | collective-permute-start | bytes 663560 | tf_op jit(solution)/shard_map/ppermute | solution.py:239
  127.3 9.4 %collective-permute-start.11 = (bf16[3,96,384]{2,1,0:T(8,128)(2,1)S(1)}, bf16[3,96,384]{2,1,0:T(8,128)(2,1)S(1)}, u32[]{:S(2)}, u32[]{:S(2)}) collective-permute-start(bf16[3,96,384]{2,1,0:T(8,128)(2,1)S(1)} %broadcast_select_fusion.10), channel_id=1, source_target_pairs={{16,24},{24,8},{8,0},{0,16},{17,25},{25,9},{9,1},{1,17},{18,26},{2... | collective-permute-start | bytes 663560 | tf_op jit(solution)/shard_map/ppermute | solution.py:239
  129.5 31.5 %collective-permute-start.25 = (bf16[3,96,384]{2,1,0:T(8,128)(2,1)S(1)}, bf16[3,96,384]{2,1,0:T(8,128)(2,1)S(1)}, u32[]{:S(2)}, u32[]{:S(2)}) collective-permute-start(bf16[3,96,384]{2,1,0:T(8,128)(2,1)S(1)} %broadcast_select_fusion.5), channel_id=1, source_target_pairs={{0,8},{8,24},{24,16},{16,0},{1,9},{9,25},{25,17},{17,1},{2,10},{10... | collective-permute-start | bytes 663560 | tf_op jit(solution)/shard_map/ppermute | solution.py:239
  132.1 30.6 %collective-permute-start.31 = (bf16[3,96,384]{2,1,0:T(8,128)(2,1)S(1)}, bf16[3,96,384]{2,1,0:T(8,128)(2,1)S(1)}, u32[]{:S(2)}, u32[]{:S(2)}) collective-permute-start(bf16[3,96,384]{2,1,0:T(8,128)(2,1)S(1)} %broadcast_select_fusion), channel_id=1, source_target_pairs={{16,24},{24,8},{8,0},{0,16},{17,25},{25,9},{9,1},{1,17},{18,26},{2... | collective-permute-start | bytes 663560 | tf_op jit(solution)/shard_map/ppermute | solution.py:239
  161.0 27.7 %collective-permute-start.12 = (bf16[4,128,768]{2,1,0:T(8,128)(2,1)}, bf16[4,128,768]{2,1,0:T(8,128)(2,1)}, u32[]{:S(2)}, u32[]{:S(2)}) collective-permute-start(bf16[4,128,768]{2,1,0:T(8,128)(2,1)} %get-tuple-element.12), channel_id=1, source_target_pairs={{0,1},{1,0},{2,3},{3,2},{4,5},{5,4},{6,7},{7,6},{8,9},{9,8},{10,11... | collective-permute-start | bytes 2359304 | tf_op jit(solution)/shard_map/ppermute | solution.py:212
  188.2 23.7 %collective-permute-start.32 = (bf16[4,128,768]{2,1,0:T(8,128)(2,1)}, bf16[4,128,768]{2,1,0:T(8,128)(2,1)S(1)}, u32[]{:S(2)}, u32[]{:S(2)}) collective-permute-start(bf16[4,128,768]{2,1,0:T(8,128)(2,1)} %get-tuple-element.16), channel_id=1, source_target_pairs={{0,1},{1,0},{2,3},{3,2},{4,5},{5,4},{6,7},{7,6},{8,9},{9,8},{10,11... | collective-permute-start | bytes 2359304 | tf_op jit(solution)/shard_map/ppermute | solution.py:212
  190.1 10.2 %collective-permute-start.13 = (bf16[128,768]{1,0:T(8,128)(2,1)S(1)}, bf16[128,768]{1,0:T(8,128)(2,1)S(1)}, u32[]{:S(2)}, u32[]{:S(2)}) collective-permute-start(bf16[128,768]{1,0:T(8,128)(2,1)S(1)} %get-tuple-element.45), channel_id=1, source_target_pairs={{0,2},{1,3},{2,0},{3,1},{4,6},{5,7},{6,4},{7,5},{8,10},{9,11},{10,... | collective-permute-start | bytes 589832 | tf_op jit(solution)/shard_map/ppermute | solution.py:212
  191.8 17.1 %collective-permute-start.14 = (bf16[128,768]{1,0:T(8,128)(2,1)S(1)}, bf16[128,768]{1,0:T(8,128)(2,1)S(1)}, u32[]{:S(2)}, u32[]{:S(2)}) collective-permute-start(bf16[128,768]{1,0:T(8,128)(2,1)S(1)} %get-tuple-element.44), channel_id=1, source_target_pairs={{0,4},{1,5},{2,6},{3,7},{4,0},{5,1},{6,2},{7,3},{8,12},{9,13},{10,... | collective-permute-start | bytes 589832 | tf_op jit(solution)/shard_map/ppermute | solution.py:212
  194.1 14.9 %collective-permute-start.15 = (bf16[128,768]{1,0:T(8,128)(2,1)S(1)}, bf16[128,768]{1,0:T(8,128)(2,1)S(1)}, u32[]{:S(2)}, u32[]{:S(2)}) collective-permute-start(bf16[128,768]{1,0:T(8,128)(2,1)S(1)} %get-tuple-element.43), channel_id=1, source_target_pairs={{0,6},{1,7},{2,4},{3,5},{4,2},{5,3},{6,0},{7,1},{8,14},{9,15},{10,... | collective-permute-start | bytes 589832 | tf_op jit(solution)/shard_map/ppermute | solution.py:212
  212.8 12.9 %collective-permute-start.33 = (bf16[128,768]{1,0:T(8,128)(2,1)S(1)}, bf16[128,768]{1,0:T(8,128)(2,1)S(1)}, u32[]{:S(2)}, u32[]{:S(2)}) collective-permute-start(bf16[128,768]{1,0:T(8,128)(2,1)S(1)} %get-tuple-element.37), channel_id=1, source_target_pairs={{0,2},{1,3},{2,0},{3,1},{4,6},{5,7},{6,4},{7,5},{8,10},{9,11},{10,... | collective-permute-start | bytes 589832 | tf_op jit(solution)/shard_map/ppermute | solution.py:212
  216.4 17.1 %collective-permute-start.34 = (bf16[128,768]{1,0:T(8,128)(2,1)S(1)}, bf16[128,768]{1,0:T(8,128)(2,1)S(1)}, u32[]{:S(2)}, u32[]{:S(2)}) collective-permute-start(bf16[128,768]{1,0:T(8,128)(2,1)S(1)} %get-tuple-element.36), channel_id=1, source_target_pairs={{0,4},{1,5},{2,6},{3,7},{4,0},{5,1},{6,2},{7,3},{8,12},{9,13},{10,... | collective-permute-start | bytes 589832 | tf_op jit(solution)/shard_map/ppermute | solution.py:212
  216.9 16.6 %collective-permute-start.35 = (bf16[128,768]{1,0:T(8,128)(2,1)S(1)}, bf16[128,768]{1,0:T(8,128)(2,1)S(1)}, u32[]{:S(2)}, u32[]{:S(2)}) collective-permute-start(bf16[128,768]{1,0:T(8,128)(2,1)S(1)} %get-tuple-element.35), channel_id=1, source_target_pairs={{0,6},{1,7},{2,4},{3,5},{4,2},{5,3},{6,0},{7,1},{8,14},{9,15},{10,... | collective-permute-start | bytes 589832 | tf_op jit(solution)/shard_map/ppermute | solution.py:212
  219.6 14.9 %collective-permute-start.17 = (bf16[128,768]{1,0:T(8,128)(2,1)S(1)}, bf16[128,768]{1,0:T(8,128)(2,1)S(1)}, u32[]{:S(2)}, u32[]{:S(2)}) collective-permute-start(bf16[128,768]{1,0:T(8,128)(2,1)S(1)} %get-tuple-element.41), channel_id=1, source_target_pairs={{0,2},{1,3},{2,0},{3,1},{4,6},{5,7},{6,4},{7,5},{8,10},{9,11},{10,... | collective-permute-start | bytes 589832 | tf_op jit(solution)/shard_map/ppermute | solution.py:212
  220.8 29.6 %collective-permute-start.18 = (bf16[128,768]{1,0:T(8,128)(2,1)S(1)}, bf16[128,768]{1,0:T(8,128)(2,1)S(1)}, u32[]{:S(2)}, u32[]{:S(2)}) collective-permute-start(bf16[128,768]{1,0:T(8,128)(2,1)S(1)} %get-tuple-element.40), channel_id=1, source_target_pairs={{0,4},{1,5},{2,6},{3,7},{4,0},{5,1},{6,2},{7,3},{8,12},{9,13},{10,... | collective-permute-start | bytes 589832 | tf_op jit(solution)/shard_map/ppermute | solution.py:212
  225.7 24.7 %collective-permute-start.19 = (bf16[128,768]{1,0:T(8,128)(2,1)S(1)}, bf16[128,768]{1,0:T(8,128)(2,1)S(1)}, u32[]{:S(2)}, u32[]{:S(2)}) collective-permute-start(bf16[128,768]{1,0:T(8,128)(2,1)S(1)} %get-tuple-element.39), channel_id=1, source_target_pairs={{0,6},{1,7},{2,4},{3,5},{4,2},{5,3},{6,0},{7,1},{8,14},{9,15},{10,... | collective-permute-start | bytes 589832 | tf_op jit(solution)/shard_map/ppermute | solution.py:212
  (43 other events, 618.9 us)
where the time goes:
time: 267 us; the launch traced here: 266 us
  waiting for transfers between devices  64.7 us (24%)
  local copies, waits for them, and re-layouts  58.7 us (22%)
  Pallas kernels  53.5 us (20%)
  starting transfers between devices  47.5 us (18%)
  other arithmetic  15.2 us (6%)
  blocking collectives  14.8 us (6%)
  between operations  11 us (4%)
    pallas_call x2, Pallas kernels, front(): pl.pallas_call(front_kernel, grid_spec=spec, out_shape=[shape, shape], co...  48.4 us
    ppermute x16, waiting for transfers between devices, swap(): return lax.ppermute(array, axis, [(i, i ^ mask) for i in range(size)])  45.4 us
    ppermute x24, starting transfers between devices, round_ring(): got.append(lax.ppermute(sent, 'band', pairs))  26.5 us
    ppermute x16, starting transfers between devices, swap(): return lax.ppermute(array, axis, [(i, i ^ mask) for i in range(size)])  21 us
    ppermute x24, waiting for transfers between devices, round_ring(): got.append(lax.ppermute(sent, 'band', pairs))  19.3 us
    all_gather x1, blocking collectives, per_device(): points = jnp.take(lax.all_gather(gsphere, 'grid', axis=0), targets, axis=0)  14.8 us
    reshape x4, local copies, waits for them, and re-layouts, planes(): orbitals = orbitals.reshape(count, groups, XG, GRID_N, GRID_N)  14.1 us
    squeeze x8, local copies, waits for them, and re-layouts, chosen(): right = round_ring([mine[j] for j in range(half)], holder, n_band, False)  9.51 us
  transfers between devices with their start and end apart: 40, of which 26 were waited for; matrix products, arithmetic and copies ran while one was open for 22% of the time, Pallas kernels for 19%

commit v1 on v0

v1 whole, which is shorter than its diff:
```python
import functools
import math

import jax
import jax.numpy as jnp
import numpy as np
from jax import lax
from jax.experimental import pallas as pl
from jax.experimental.pallas import tpu as pltpu
from jax.sharding import PartitionSpec as P

GRID_N = 96
KF = 32
BLK = 8
XG = 4
LANES = XG * GRID_N
F32 = jnp.float32
BF16 = jnp.bfloat16


def fourier_parts(length, kept):
    phase = np.arange(length)[:, None] * (np.arange(kept) - kept // 2)[None, :] % length * (2.0 * math.pi / length)
    return (np.cos(phase) / math.sqrt(length)).astype(BF16), (np.sin(phase) / math.sqrt(length)).astype(BF16)


def y_table(cosine, sine):
    order = np.arange(GRID_N).reshape(-1, XG).T.reshape(-1)
    one = np.concatenate([cosine[order].T, -sine[order].T], axis=0)
    zero = np.zeros_like(one)
    return np.concatenate([np.concatenate([one, zero], axis=1), np.concatenate([zero, one], axis=1)], axis=0)


def z_table(cosine, sine):
    both = np.stack([np.stack([cosine, -sine], axis=1), np.stack([sine, cosine], axis=1)])
    table = np.zeros((2, XG, GRID_N, XG, 2, KF), BF16)
    for x in range(XG):
        table[:, x, :, x] = both
    return table.reshape(2 * LANES, XG * 2 * KF)


def x_phases(cosine, sine, n_grid):
    slab = GRID_N // n_grid
    fill = ((0, 0), (0, -slab % XG), (0, 0))
    parts = [np.pad(t.reshape(n_grid, slab, KF).astype(np.float32), fill) for t in (cosine, sine)]
    return np.concatenate(parts, axis=1).astype(BF16)


HOLDS = np.array([[0, 1, 3, 2], [0, 2, 3, 1], [1, 3, 0, 2], [1, 0, 3, 2]])
SOURCES = np.array([[0, 1, 1, 0], [2, 4, 2, 3], [3, 5, 2, 3], [4, 5, 2, 3]])


def slots_of():
    quarter = BLK // 4
    return np.argsort((quarter * HOLDS[:, :, None] + np.arange(quarter)).reshape(4, BLK), axis=1)


def planes_kernel(outs_of, blocks, src, *refs):
    outs, rows = refs[:-1], refs[-1]
    orbital = src[0]
    slab = orbital.shape[0]
    step = -(-slab // 8) * 8
    high = GRID_N // XG
    for y in range(high):
        for t in range(LANES // 128):
            cut = slice(y * LANES + 128 * t, y * LANES + 128 * t + 128)
            rows[t, y * step:y * step + slab, :] = orbital[:, cut].astype(F32)

    def write(out):
        for group in range(out.shape[1]):
            wide = []
            for x in range(XG * group, XG * group + XG):
                if x < slab:
                    wide.append(jnp.concatenate([rows[t, pl.ds(x, high, stride=step), :] for t in range(LANES // 128)], axis=1))
                else:
                    wide.append(jnp.zeros((high, LANES), F32))
            lines = [
                jnp.concatenate([w[:, GRID_N * low:GRID_N * low + GRID_N] for w in wide], axis=1) for low in range(XG)
            ]
            out[0, group] = jnp.concatenate(lines, axis=0).astype(BF16)

    if len(outs) == 1:
        write(outs[0])
        return
    for i, out in enumerate(outs):
        @pl.when(pl.program_id(0) // outs_of == i)
        def _(out=out):
            write(out)


def planes(orbitals, blocks, first, count, outs):
    slab, size = orbitals.shape[1:]
    groups = -(-slab // XG)
    each = count // outs
    spec = pltpu.PrefetchScalarGridSpec(
        num_scalar_prefetch=1,
        grid=(count,),
        in_specs=[pl.BlockSpec((1, slab, size), lambda f, b: (first(b) + f, 0, 0))],
        out_specs=[
            pl.BlockSpec((1, groups, GRID_N, LANES), lambda f, b, i=i: (jnp.clip(f - i * each, 0, each - 1), 0, 0, 0))
            for i in range(outs)
        ],
        scratch_shapes=[pltpu.VMEM((LANES // 128, GRID_N // XG * (-(-slab // 8) * 8), 128), F32)],
    )
    return pl.pallas_call(
        functools.partial(planes_kernel, each),
        grid_spec=spec,
        out_shape=[jax.ShapeDtypeStruct((each, groups, GRID_N, LANES), BF16)] * outs,
        compiler_params=pltpu.CompilerParams(vmem_limit_bytes=16 * 1024 * 1024),
        cost_estimate=pl.CostEstimate(flops=0, bytes_accessed=4 * count * slab * size, transcendentals=0),
        name="planes",
    )(blocks, orbitals)


def tables_kernel(*refs):
    *points, phases, pick, wave = refs
    cols = pick.shape[1]
    phase = phases[lax.axis_index("grid")]
    for r in range(pick.shape[0]):
        point = points[r // 2][r % 2:r % 2 + 1, :]
        shape = (cols, point.shape[1])
        found = lax.broadcasted_iota(jnp.int32, shape, 0) == jnp.broadcast_to(point & (cols - 1), shape)
        pick[r] = found.astype(F32).astype(BF16)
        shape = (KF, point.shape[1])
        turn = lax.broadcasted_iota(jnp.int32, shape, 0) == jnp.broadcast_to(point >> (cols.bit_length() - 1), shape)
        wave[r] = jnp.dot(phase, turn.astype(F32).astype(BF16), preferred_element_type=F32)


def tables(points, phases, cols):
    targets, own = 2 * len(points), points[0].shape[1]
    return pl.pallas_call(
        tables_kernel,
        out_shape=[
            jax.ShapeDtypeStruct((targets, cols, own), BF16),
            jax.ShapeDtypeStruct((targets, phases.shape[1], own), F32),
        ],
        compiler_params=pltpu.CompilerParams(vmem_limit_bytes=16 * 1024 * 1024),
        cost_estimate=pl.CostEstimate(flops=0, bytes_accessed=3 * targets * cols * own, transcendentals=0),
        name="tables",
    )(*points, phases)


def front_kernel(sources, find, blocks, source_of, *refs):
    parts_in, refs = refs[:sources], refs[sources:]
    cond, ytab, ztab, pick, wave, even, odd, vals, mixed, section, arrived = refs
    conds, groups = cond.shape[0], cond.shape[1]
    cols = pick.shape[1]
    own_y = cols // KF
    count = vals.shape[0]
    now = pl.program_id(0)

    @pl.when(now == 0)
    def _():
        for f in range(count):
            wanted, inside = find(blocks, source_of, f)
            for s in range(sources):
                @pl.when(wanted == s)
                def _(f=f, s=s):
                    pltpu.make_async_copy(parts_in[s].at[inside], vals.at[f], arrived.at[f]).start()

    pltpu.make_async_copy(parts_in[0].at[0], vals.at[now], arrived.at[now]).wait()
    for pair in range(conds // 2):
        for group in range(groups):
            orbital = vals[now, group]
            density = jnp.concatenate(
                [orbital * cond[2 * pair, group], orbital * cond[2 * pair + 1, group]], axis=0
            )
            out = jnp.dot(ytab[...], density, preferred_element_type=F32).astype(BF16)
            for half in range(2):
                row = (2 * pair + half) * KF
                base = half * 2 * KF
                mixed[group, row:row + KF, :LANES] = out[base:base + KF]
                mixed[group, row:row + KF, LANES:] = out[base + KF:base + 2 * KF]
    for group in range(groups):
        value = jnp.dot(mixed[group], ztab[...], preferred_element_type=F32)
        section[2 * group] = value[:, :128]
        section[2 * group + 1] = value[:, 128:]

    def one_target(step, parity, out_ref):
        order = 2 * step + parity
        target = lax.axis_index("grid").astype(jnp.int32) ^ order
        first = target * own_y
        parts = []
        for group in range(groups):
            for half in range(2):
                rows = [
                    section[2 * group + half, pl.ds(first + y, conds, stride=KF), :]
                    for y in range(own_y)
                ]
                for piece in range(4):
                    cut = slice(KF * piece, KF * piece + KF)
                    parts.append(jnp.concatenate([row[:, cut] for row in rows], axis=1))
        left = jnp.concatenate(parts, axis=0).astype(BF16)
        found = jnp.dot(left, pick[order], preferred_element_type=F32)
        real = imag = None
        count = XG * groups
        for x in range(count):
            cosine = wave[order, x:x + 1, :]
            sine = wave[order, count + x:count + x + 1, :]
            re = found[2 * x * conds:(2 * x + 1) * conds]
            im = found[(2 * x + 1) * conds:(2 * x + 2) * conds]
            add_real = re * cosine + im * sine
            add_imag = im * cosine - re * sine
            real = add_real if real is None else real + add_real
            imag = add_imag if imag is None else imag + add_imag
        out_ref[step] = jnp.concatenate([real, imag], axis=0).astype(BF16)

    def body(step, carry):
        one_target(step, 0, even)
        one_target(step, 1, odd)
        return carry

    lax.fori_loop(0, even.shape[0], body, 0)


def front(find, count, blocks, sources, cond, ytab, ztab, pick, wave):
    conds, groups = cond.shape[:2]
    targets, cols, own = pick.shape
    rows = 2 * conds
    shape = jax.ShapeDtypeStruct((targets // 2, count * rows, own), BF16)
    whole = lambda a: pl.BlockSpec(a.shape, lambda v, b, t: (0,) * a.ndim)
    spec = pltpu.PrefetchScalarGridSpec(
        num_scalar_prefetch=2,
        grid=(count,),
        in_specs=[pl.BlockSpec(memory_space=pl.ANY)] * len(sources) + [
            whole(cond), whole(ytab), whole(ztab), whole(pick), whole(wave),
        ],
        out_specs=[pl.BlockSpec((targets // 2, rows, own), lambda v, b, t: (0, v, 0))] * 2,
        scratch_shapes=[
            pltpu.VMEM((count,) + cond.shape[1:], BF16),
            pltpu.VMEM((groups, conds * KF, 2 * LANES), BF16),
            pltpu.VMEM((2 * groups, conds * KF, XG * KF), F32),
            pltpu.SemaphoreType.DMA((count,)),
        ],
    )
    return pl.pallas_call(
        functools.partial(front_kernel, len(sources), find),
        grid_spec=spec,
        out_shape=[shape, shape],
        compiler_params=pltpu.CompilerParams(vmem_limit_bytes=40 * 1024 * 1024),
        cost_estimate=pl.CostEstimate(flops=count * 900_000_000, bytes_accessed=count * 2_000_000, transcendentals=0),
        name="front",
    )(blocks, jnp.asarray(SOURCES.reshape(-1), jnp.int32), *sources, cond, ytab, ztab, pick, wave)


def screen_kernel(here, *refs):
    *pieces, w_even, w_odd, even, odd, side = refs

    @pl.when(pl.program_id(0) == 0)
    def _():
        total = pieces[0][...].astype(F32)
        for piece in pieces[1:]:
            total = total + piece[...].astype(F32)
        side[...] = total.astype(BF16)

    even[0] = jnp.dot(side[...], w_even[...], preferred_element_type=F32).astype(BF16)
    odd[0] = jnp.dot(side[...], w_odd[...], preferred_element_type=F32).astype(BF16)


def screen(here, pieces, screened, targets):
    rows, own = pieces[0].shape
    if own % 128:
        side = sum(p.astype(F32) for p in pieces).astype(BF16)
        part = jnp.dot(side, screened, preferred_element_type=F32).astype(BF16)
        part = jnp.transpose(part.reshape(rows, targets, own), (1, 0, 2))
        part = jnp.take(part, here[0] ^ jnp.arange(targets), axis=0)
        return part[0::2], part[1::2]
    shape = jax.ShapeDtypeStruct((targets // 2, rows, own), BF16)
    spec = pltpu.PrefetchScalarGridSpec(
        num_scalar_prefetch=1,
        grid=(targets // 2,),
        in_specs=[pl.BlockSpec((rows, own), lambda r, h: (0, 0))] * len(pieces) + [
            pl.BlockSpec((own, own), lambda r, h: (0, h[0] ^ (2 * r))),
            pl.BlockSpec((own, own), lambda r, h: (0, h[0] ^ (2 * r + 1))),
        ],
        out_specs=[pl.BlockSpec((1, rows, own), lambda r, h: (r, 0, 0))] * 2,
        scratch_shapes=[pltpu.VMEM((rows, own), BF16)],
    )
    return pl.pallas_call(
        screen_kernel,
        grid_spec=spec,
        out_shape=[shape, shape],
        compiler_params=pltpu.CompilerParams(vmem_limit_bytes=32 * 1024 * 1024),
        cost_estimate=pl.CostEstimate(flops=2 * rows * own * own * targets, bytes_accessed=2 * own * own * targets, transcendentals=0),
        name="screen",
    )(here, *pieces, screened, screened)


def close_kernel(split, place, blocks, slot_of, *refs):
    ins, outs, sums = refs[:sum(map(sum, split))], refs[sum(map(sum, split)):-2], refs[-2:]
    sides = []
    for side, pieces in enumerate(split):
        first = 0
        for count in pieces:
            group, ins = ins[:count], ins[count:]
            total = group[0][...].astype(F32)
            for piece in group[1:]:
                total = total + piece[...].astype(F32)
            rows, own = total.shape
            unit = sums[side].shape[1]
            sums[side][first:first + rows // unit] = total.reshape(rows // unit, unit, own)
            first += rows // unit
        units = [sums[side][place(blocks, slot_of, side, f)] for f in range(first)]
        half = unit // 2
        sides.append([
            jnp.concatenate([u[half * part:half * part + half] for u in units], axis=0).astype(BF16) for part in range(2)
        ])
    product = None
    for left, right in zip(*sides, strict=True):
        term = lax.dot_general(left, right, (((1,), (1,)), ((), ())), preferred_element_type=F32)
        product = term if product is None else product + term
    if len(outs) == 1:
        outs[0][...] = product
    else:
        rows = outs[0].shape[1]
        for r in range(product.shape[0] // rows):
            outs[r % 2][r // 2] = product[r * rows:(r + 1) * rows]


def close(place, blocks, u_pieces, b_pieces, conds, targets, by_target):
    split = [[len(p) for p in side] for side in (u_pieces, b_pieces)]
    flat = [x for side in (u_pieces, b_pieces) for p in side for x in p]
    functions = BLK
    rows = functions * conds
    own = flat[0].shape[1]
    if by_target:
        out = [jax.ShapeDtypeStruct((targets // 2, rows // targets, rows), F32)] * 2
    else:
        out = [jax.ShapeDtypeStruct((rows, rows), F32)]
    spec = pltpu.PrefetchScalarGridSpec(
        num_scalar_prefetch=2,
        grid=(1,),
        in_specs=[pl.BlockSpec(x.shape, lambda i, b, t: (0, 0)) for x in flat],
        out_specs=[pl.BlockSpec(o.shape, lambda i, b, t, o=o: (0,) * len(o.shape)) for o in out],
        scratch_shapes=[pltpu.VMEM((functions, 2 * conds, own), F32)] * 2,
    )
    return pl.pallas_call(
        functools.partial(close_kernel, split, place),
        grid_spec=spec,
        out_shape=out,
        cost_estimate=pl.CostEstimate(flops=4 * rows * rows * own, bytes_accessed=8 * rows * own, transcendentals=0),
        compiler_params=pltpu.CompilerParams(vmem_limit_bytes=32 * 1024 * 1024),
        name="close",
    )(blocks, jnp.asarray(slots_of().reshape(-1), jnp.int32), *flat)


def swap(array, axis, mask, size):
    return lax.ppermute(array, axis, [(i, i ^ mask) for i in range(size)])


def gather_sums(even, odd, targets):
    total = (even.astype(F32) + swap(odd, "grid", 1, targets).astype(F32)).astype(even.dtype)
    return [total[0]] + [swap(total[r], "grid", 2 * r, targets) for r in range(1, targets // 2)]


def round_ring(own, holder, size, reverse):
    order = list(range(size))
    if reverse:
        order = order[::-1]
    pairs = [(order[i], order[(i + 1) % size]) for i in range(size)]
    place = [0] * size
    for i, device in enumerate(order):
        place[device] = i
    place = jnp.array(place, jnp.int32)
    away = (place[lax.axis_index("band")] - place[holder]) % size
    chunks = len(own)
    got = []
    for step in range(chunks + size - 2):
        mine = own[min(step, chunks - 1)]
        sent = mine if step == 0 else jnp.where(away == 0, mine, got[-1])
        got.append(lax.ppermute(sent, "band", pairs))
    out = []
    for j in range(chunks):
        value = own[j]
        for hop in range(1, size):
            value = jnp.where(away == hop, got[j + hop - 1], value)
        out.append(value)
    return out


def by_ring(valence, blocks, side, held, size):
    half = BLK // 2
    own = planes(valence, blocks, lambda b: b[side] % held * BLK, BLK, BLK)
    right = round_ring(own[:half], blocks[side] // held, size, False)
    left = round_ring(own[half:], blocks[side] // held, size, True)
    return right, left


def by_swaps(early, valence, blocks, side, held):
    owner = lax.axis_index("band") == blocks[side] // held
    across = lambda a: swap(a, "band", 1, 4)
    along = lambda a: swap(a, "band", 2, 4)
    own0, own1 = early
    own2, own3 = planes(valence, blocks, lambda b: b[side] % held * BLK + BLK // 2, BLK // 2, 2)
    x1, y1 = across(own0), along(own1)
    x2 = across(jnp.where(owner, own2, y1))
    y2 = along(jnp.where(owner, own3, x1))
    x3 = across(jnp.where(owner, own3, y2))
    y3 = along(jnp.where(owner, own2, x2))
    return [own0, own1, x1, y1, x2, y2], [own2, own3, x3, y3]


def per_device(sizes, valence, conduction, screened, blocks, gsphere):
    n_band, n_grid = sizes
    held = valence.shape[0] // BLK
    conds, own = conduction.shape[0], gsphere.shape[0]
    cols = KF // n_grid * KF
    half, quarter = BLK // 2, BLK // 4
    swaps = n_band == 4
    at = lax.axis_index("grid").astype(jnp.int32)[None]
    cosine, sine = fourier_parts(GRID_N, KF)
    ytab, ztab = jnp.asarray(y_table(cosine, sine)), jnp.asarray(z_table(cosine, sine))

    def role(b, side):
        return lax.axis_index("band").astype(jnp.int32) ^ (b[side] // held)

    if swaps:
        early = [planes(valence, blocks, lambda b, s=s: b[s] % held * BLK, half, 2) for s in range(2)]
        chosen = [by_swaps(early[s], valence, blocks, s, held) for s in range(2)]
    else:
        chosen = [by_ring(valence, blocks, s, held, n_band) for s in range(2)]
    cond, = planes(conduction, blocks, lambda b: 0, conds, 1)

    pair = gsphere.reshape(1, own)
    pair = jnp.concatenate([pair, swap(pair, "grid", 1, n_grid)], axis=0)
    points = [pair] + [swap(pair, "grid", 2 * r, n_grid) for r in range(1, n_grid // 2)]
    pick, wave = tables(points, jnp.asarray(x_phases(cosine, sine, n_grid)), cols)

    def part(side, late):
        def find(b, source_of, f):
            if not swaps:
                return f, 0
            return source_of[role(b, side) * 4 + 2 * late + f // quarter], f % quarter
        return front(find, half, blocks, chosen[side][late], cond, ytab, ztab, pick, wave)

    part_a, part_b = [], []
    for late in range(2):
        part_a.append(part(0, late))
        part_b.append(part(1, late))
    side_a = [gather_sums(*p, n_grid) for p in part_a]
    side_u = [gather_sums(*screen(at, p, screened, n_grid), n_grid) for p in side_a]
    side_b = [gather_sums(*p, n_grid) for p in part_b]

    by_target = n_grid == BLK

    def place(b, slot_of, side, f):
        if side == 0 and by_target:
            f = f ^ lax.axis_index("grid").astype(jnp.int32)
        return slot_of[role(b, side) * BLK + f] if swaps else f

    shares = close(place, blocks, side_u, side_b, conds, n_grid, by_target)
    if not by_target:
        share = shares[0].reshape(n_grid, -1, shares[0].shape[1])
        share = jnp.take(share, at ^ jnp.arange(n_grid, dtype=jnp.int32), axis=0)
        shares = share[0::2], share[1::2]
    return sum(gather_sums(*shares, n_grid))[None]


def solution(mesh):
    sizes = (mesh.shape["band"], mesh.shape["grid"])
    in_specs = (P("band", "grid", None), P("band", "grid", None), P("grid", None), P(), P("grid"))
    out_specs = P("band", "grid", None)
    return jax.shard_map(
        functools.partial(per_device, sizes), mesh=mesh, in_specs=in_specs, out_specs=out_specs, check_vma=False
    )
```

time: 267 us -> 185 us (0.69)
  local copies, waits for them, and re-layouts: 58.7 us -> 10.6 us
  waiting for transfers between devices: 64.7 us -> 29.3 us
  Pallas kernels: 53.5 us -> 71.3 us
  starting transfers between devices: 47.5 us -> 63.6 us
  blocking collectives: 14.8 us -> 0 us
  other arithmetic: 15.2 us -> 3.76 us
  between operations: 11 us -> 5.89 us
    ppermute x16 -> x44, starting transfers between devices: 21 us -> 63.6 us  [swap(): return lax.ppermute(array, axis, [(i, i ^ mask) for i in range(size)])]
    ppermute x24 -> x0, starting transfers between devices: 26.5 us -> none  [round_ring(): got.append(lax.ppermute(sent, 'band', pairs))]
    ppermute x24 -> x0, waiting for transfers between devices: 19.3 us -> none  [round_ring(): got.append(lax.ppermute(sent, 'band', pairs))]
    squeeze x16 -> x0, local copies, waits for them, and re-layouts: 17.3 us -> none  [the longest x8 9.51 us: chosen(): right = round_ring([mine[j] for j in range(half)], holder, n_band, False)]
    reshape x5 -> x1, local copies, waits for them, and re-layouts: 16.8 us -> 0.01 us  [per_device(): pair = gsphere.reshape(1, own)]
    ppermute x16 -> x44, waiting for transfers between devices: 45.4 us -> 29.3 us  [swap(): return lax.ppermute(array, axis, [(i, i ^ mask) for i in range(size)])]
    all_gather x1 -> x0, blocking collectives: 14.8 us -> none  [per_device(): points = jnp.take(lax.all_gather(gsphere, 'grid', axis=0), targets, axis=0)]
    pallas_call x3 -> x11, Pallas kernels: 50.7 us -> 65.5 us  [the longest x4 52.1 us: front(): pl.pallas_call(functools.partial(front_kernel, len(sources), find), grid_...]
  transfers between devices with their start and end apart: 40 -> 44, of which waited for: 26 -> 11; matrix products, arithmetic and copies ran while one was open for 22% -> 3% of each run, Pallas kernels for 19% -> 36%
where the time goes in v1:
time: 185 us; the launch traced here: 184 us
  Pallas kernels  71.3 us (39%)
  starting transfers between devices  63.6 us (34%)
  waiting for transfers between devices  29.3 us (16%)
  local copies, waits for them, and re-layouts  10.6 us (6%)
  between operations  5.89 us (3%)
  other arithmetic  3.76 us (2%)
    ppermute x44, starting transfers between devices, swap(): return lax.ppermute(array, axis, [(i, i ^ mask) for i in range(size)])  63.6 us
    pallas_call x4, Pallas kernels, front(): pl.pallas_call(functools.partial(front_kernel, len(sources), find), grid_...  52.1 us
    ppermute x44, waiting for transfers between devices, swap(): return lax.ppermute(array, axis, [(i, i ^ mask) for i in range(size)])  29.3 us
    pallas_call x5, Pallas kernels, planes(): pl.pallas_call(functools.partial(planes_kernel, each), grid_spec=spec, ou...  10.9 us
    unnamed x36, local copies, waits for them, and re-layouts  9.8 us
    pallas_call x2, Pallas kernels, screen(): pl.pallas_call(screen_kernel, grid_spec=spec, out_shape=[shape, shape], c...  5.83 us
  transfers between devices with their start and end apart: 44, of which 11 were waited for; matrix products, arithmetic and copies ran while one was open for 3% of the time, Pallas kernels for 36%

profile of v1, /device:TPU:0, one launch (start us, length us, event | category | flops | bytes accessed | tf_op | source)
XLA Modules:
  0.0 184.4 jit_solution(1400920766774752125)
XLA Ops:
  0.0 4.0 %copy.14.src = bf16[16,12,9216]{2,1,0:T(8,128)(2,1)S(1)} copy(bf16[16,12,9216]{2,0,1:T(8,128)(2,1)} %param.13) | data formatting | bytes 7077888 | tf_op args[0]
  4.1 3.4 %planes.5 = (bf16[2,3,96,384]{3,2,1,0:T(8,128)(2,1)}, bf16[2,3,96,384]{3,2,1,0:T(8,128)(2,1)}) custom-call(s32[2]{0:T(128)S(1)} %copy-done.3, bf16[16,12,9216]{2,1,0:T(8,128)(2,1)S(1)} %copy.14.src), custom_call_target="tpu_custom_call" | custom-call | bytes 1769472 | tf_op jit(solution)/shard_map/planes/pallas_call | solution.py:104
  7.4 3.0 %collective-permute-start.1 = (bf16[2,3,96,384]{3,2,1,0:T(8,128)(2,1)}, bf16[2,3,96,384]{3,2,1,0:T(8,128)(2,1)}, u32[]{:S(2)}, u32[]{:S(2)}) collective-permute-start(bf16[2,3,96,384]{3,2,1,0:T(8,128)(2,1)} %get-tuple-element.30.refs_1_), channel_id=1, source_target_pairs={{0,16},{8,24},{16,0},{24,8},{1,17},{9,25},{17,1},{25,9},{2,18},{10... | collective-permute-start | bytes 1327112 | tf_op jit(solution)/shard_map/ppermute | solution.py:347
  12.0 1.6 collective-permute-start.5
  13.6 2.6 %collective-permute-start.6 = (s32[2,768]{1,0:T(2,128)S(1)}, s32[2,768]{1,0:T(2,128)}, u32[]{:S(2)}, u32[]{:S(2)}) collective-permute-start(s32[2,768]{1,0:T(2,128)S(1)} %pad_add_fusion.refs_0_), channel_id=1, source_target_pairs={{0,4},{1,5},{2,6},{3,7},{4,0},{5,1},{6,2},{7,3},{8,12},{9,13},{10,... | collective-permute-start | bytes 18440 | tf_op jit(solution)/shard_map/ppermute | solution.py:347
  17.0 1.6 planes.6
  21.4 2.3 %copy-done.1 = bf16[16,12,9216]{2,1,0:T(8,128)(2,1)S(1)} copy-done((bf16[16,12,9216]{2,1,0:T(8,128)(2,1)S(1)}, bf16[16,12,9216]{2,1,0:T(8,128)(2,1)}, u32[]{:S(2)}) %copy-start.1) | copy-done | bytes 3538968
  23.7 1.6 planes.8
  26.9 1.6 planes.9
  32.2 2.6 %planes.7.refs_6_.refs_4_ = bf16[8,3,96,384]{3,2,1,0:T(8,128)(2,1)S(1)} custom-call(s32[2]{0:T(128)S(1)} %copy-done.3, bf16[8,12,9216]{2,1,0:T(8,128)(2,1)S(1)} %copy.16.src), custom_call_target="tpu_custom_call" | custom-call | bytes 3538944 | tf_op jit(solution)/shard_map/planes/pallas_call | solution.py:104
  37.4 1.6 tables.1
  42.8 6.5 %collective-permute-done.27.refs_3_ = bf16[2,3,96,384]{3,2,1,0:T(8,128)(2,1)S(1)} collective-permute-done((bf16[2,3,96,384]{3,2,1,0:T(8,128)(2,1)}, bf16[2,3,96,384]{3,2,1,0:T(8,128)(2,1)S(1)}, u32[]{:S(2)}, u32[]{:S(2)}) %collective-permute-start.27) | collective-permute-done | bytes 442400 | tf_op jit(solution)/shard_map/ppermute | solution.py:347
  51.1 6.7 %collective-permute-done.2.refs_4_ = bf16[2,3,96,384]{3,2,1,0:T(8,128)(2,1)S(1)} collective-permute-done((bf16[2,3,96,384]{3,2,1,0:T(8,128)(2,1)S(1)}, bf16[2,3,96,384]{3,2,1,0:T(8,128)(2,1)S(1)}, u32[]{:S(2)}, u32[]{:S(2)}) %collective-permute-start.2) | collective-permute-done | bytes 442400 | tf_op jit(solution)/shard_map/ppermute | solution.py:347
  58.8 12.7 %front.4 = (bf16[4,64,768]{2,1,0:T(8,128)(2,1)S(1)}, bf16[4,64,768]{2,1,0:T(8,128)(2,1)S(1)}) custom-call(s32[2]{0:T(128)S(1)} %copy-done.3, s32[16]{0:T(128)S(1)} %copy-done.11, bf16[2,3,96,384]{3,2,1,0:T(8,128)(2,1)} %get-tuple-element.29.refs_0_, bf16[2,3,96,384]{3,2,1,0:T(8,128)(2,1)} %get-tuple-element.30.refs_1_, ...), custom_call_target="tpu_custom_call" | custom-call | flops 3600000000 | bytes 8000000 | tf_op jit(solution)/shard_map/front/pallas_call | solution.py:235
  73.4 13.1 %front.6 = (bf16[4,64,768]{2,1,0:T(8,128)(2,1)S(1)}, bf16[4,64,768]{2,1,0:T(8,128)(2,1)S(1)}) custom-call(s32[2]{0:T(128)S(1)} %copy-done.3, s32[16]{0:T(128)S(1)} %copy-done.11, bf16[2,3,96,384]{3,2,1,0:T(8,128)(2,1)S(1)} %copy-done.6, bf16[2,3,96,384]{3,2,1,0:T(8,128)(2,1)S(1)} %copy-done.8, bf16[2,3,96,384]{3,2,1,0:T(8,128)(2,1)S(1)} %collective-permute-done.26.refs_2_, ...), custom_call_target="tpu_custom_call" | custom-call | flops 3600000000 | bytes 8000000 | tf_op jit(solution)/shard_map/front/pallas_call | solution.py:235
  87.9 1.6 collective-permute-start.35
  90.4 3.6 %collective-permute-start.10 = (bf16[64,768]{1,0:T(8,128)(2,1)S(1)}, bf16[64,768]{1,0:T(8,128)(2,1)S(1)}, u32[]{:S(2)}, u32[]{:S(2)}) collective-permute-start(bf16[64,768]{1,0:T(8,128)(2,1)S(1)} %get-tuple-element.74), channel_id=1, source_target_pairs={{0,4},{1,5},{2,6},{3,7},{4,0},{5,1},{6,2},{7,3},{8,12},{9,13},{10,... | collective-permute-start | bytes 294920 | tf_op jit(solution)/shard_map/ppermute | solution.py:347
  94.3 13.0 %front.5 = (bf16[4,64,768]{2,1,0:T(8,128)(2,1)S(1)}, bf16[4,64,768]{2,1,0:T(8,128)(2,1)S(1)}) custom-call(s32[2]{0:T(128)S(1)} %copy-done.3, s32[16]{0:T(128)S(1)} %copy-done.11, bf16[2,3,96,384]{3,2,1,0:T(8,128)(2,1)S(1)} %get-tuple-element.31.refs_0_, bf16[2,3,96,384]{3,2,1,0:T(8,128)(2,1)S(1)} %get-tuple-element.32.refs_1_, ...), custom_call_target="tpu_custom_call" | custom-call | flops 3600000000 | bytes 8000000 | tf_op jit(solution)/shard_map/front/pallas_call | solution.py:235
  107.8 13.2 %front.7 = (bf16[4,64,768]{2,1,0:T(8,128)(2,1)S(1)}, bf16[4,64,768]{2,1,0:T(8,128)(2,1)S(1)}) custom-call(s32[2]{0:T(128)S(1)} %copy-done.3, s32[16]{0:T(128)S(1)} %copy-done.11, bf16[2,3,96,384]{3,2,1,0:T(8,128)(2,1)S(1)} %get-tuple-element.45.refs_0_, bf16[2,3,96,384]{3,2,1,0:T(8,128)(2,1)S(1)} %get-tuple-element.46.refs_1_, ...), custom_call_target="tpu_custom_call" | custom-call | flops 3600000000 | bytes 8000000 | tf_op jit(solution)/shard_map/front/pallas_call | solution.py:235
  121.7 2.9 %screen.2 = (bf16[4,64,768]{2,1,0:T(8,128)(2,1)S(1)}, bf16[4,64,768]{2,1,0:T(8,128)(2,1)S(1)}) custom-call(s32[1]{0:T(128)} %bitcast.here, bf16[64,768]{1,0:T(8,128)(2,1)S(1)} %get-tuple-element.76.refs_0_, bf16[64,768]{1,0:T(8,128)(2,1)S(1)} %collective-permute-done.9.refs_1_, bf16[64,768]{1,0:T(8,128)(2,1)S(1)} %collective-permute-done.10.refs_2_, ...), custom_call_target="tpu_custom_call" | custom-call | flops 603979776 | bytes 9437184 | tf_op jit(solution)/shard_map/screen/pallas_call | solution.py:278
  124.9 1.7 collective-permute-start.19
  126.5 2.2 %collective-permute-start.20 = (bf16[64,768]{1,0:T(8,128)(2,1)S(1)}, bf16[64,768]{1,0:T(8,128)(2,1)S(1)}, u32[]{:S(2)}, u32[]{:S(2)}) collective-permute-start(bf16[64,768]{1,0:T(8,128)(2,1)S(1)} %get-tuple-element.66), channel_id=1, source_target_pairs={{0,4},{1,5},{2,6},{3,7},{4,0},{5,1},{6,2},{7,3},{8,12},{9,13},{10,... | collective-permute-start | bytes 294920 | tf_op jit(solution)/shard_map/ppermute | solution.py:347
  130.3 4.0 %collective-permute-start.32 = (bf16[64,768]{1,0:T(8,128)(2,1)S(1)}, bf16[64,768]{1,0:T(8,128)(2,1)S(1)}, u32[]{:S(2)}, u32[]{:S(2)}) collective-permute-start(bf16[64,768]{1,0:T(8,128)(2,1)S(1)} %get-tuple-element.58), channel_id=1, source_target_pairs={{0,4},{1,5},{2,6},{3,7},{4,0},{5,1},{6,2},{7,3},{8,12},{9,13},{10,... | collective-permute-start | bytes 294920 | tf_op jit(solution)/shard_map/ppermute | solution.py:347
  134.3 7.8 %collective-permute-start.33 = (bf16[64,768]{1,0:T(8,128)(2,1)S(1)}, bf16[64,768]{1,0:T(8,128)(2,1)S(1)}, u32[]{:S(2)}, u32[]{:S(2)}) collective-permute-start(bf16[64,768]{1,0:T(8,128)(2,1)S(1)} %get-tuple-element.57), channel_id=1, source_target_pairs={{0,6},{1,7},{2,4},{3,5},{4,2},{5,3},{6,0},{7,1},{8,14},{9,15},{10,... | collective-permute-start | bytes 294920 | tf_op jit(solution)/shard_map/ppermute | solution.py:347
  142.3 2.9 %screen.3 = (bf16[4,64,768]{2,1,0:T(8,128)(2,1)S(1)}, bf16[4,64,768]{2,1,0:T(8,128)(2,1)S(1)}) custom-call(s32[1]{0:T(128)} %bitcast.here, bf16[64,768]{1,0:T(8,128)(2,1)S(1)} %get-tuple-element.68.refs_0_, bf16[64,768]{1,0:T(8,128)(2,1)S(1)} %collective-permute-done.19.refs_1_, bf16[64,768]{1,0:T(8,128)(2,1)S(1)} %collective-permute-done.20.refs_2_, ...), custom_call_target="tpu_custom_call" | custom-call | flops 603979776 | bytes 9437184 | tf_op jit(solution)/shard_map/screen/pallas_call | solution.py:278
  148.2 3.2 %collective-permute-start.39 = (bf16[64,768]{1,0:T(8,128)(2,1)S(1)}, bf16[64,768]{1,0:T(8,128)(2,1)S(1)}, u32[]{:S(2)}, u32[]{:S(2)}) collective-permute-start(bf16[64,768]{1,0:T(8,128)(2,1)S(1)} %get-tuple-element.53), channel_id=1, source_target_pairs={{0,6},{1,7},{2,4},{3,5},{4,2},{5,3},{6,0},{7,1},{8,14},{9,15},{10,... | collective-permute-start | bytes 294920 | tf_op jit(solution)/shard_map/ppermute | solution.py:347
  152.7 3.2 %collective-permute-start.15 = (bf16[64,768]{1,0:T(8,128)(2,1)S(1)}, bf16[64,768]{1,0:T(8,128)(2,1)S(1)}, u32[]{:S(2)}, u32[]{:S(2)}) collective-permute-start(bf16[64,768]{1,0:T(8,128)(2,1)S(1)} %get-tuple-element.69), channel_id=1, source_target_pairs={{0,6},{1,7},{2,4},{3,5},{4,2},{5,3},{6,0},{7,1},{8,14},{9,15},{10,... | collective-permute-start | bytes 294920 | tf_op jit(solution)/shard_map/ppermute | solution.py:347
  155.9 2.0 %collective-permute-done.38.refs_14_ = bf16[64,768]{1,0:T(8,128)(2,1)S(1)} collective-permute-done((bf16[64,768]{1,0:T(8,128)(2,1)S(1)}, bf16[64,768]{1,0:T(8,128)(2,1)S(1)}, u32[]{:S(2)}, u32[]{:S(2)}) %collective-permute-start.38) | collective-permute-done | bytes 98336 | tf_op jit(solution)/shard_map/ppermute | solution.py:347
  157.9 6.5 %collective-permute-start.24 = (bf16[64,768]{1,0:T(8,128)(2,1)S(1)}, bf16[64,768]{1,0:T(8,128)(2,1)S(1)}, u32[]{:S(2)}, u32[]{:S(2)}) collective-permute-start(bf16[64,768]{1,0:T(8,128)(2,1)S(1)} %get-tuple-element.62), channel_id=1, source_target_pairs={{0,4},{1,5},{2,6},{3,7},{4,0},{5,1},{6,2},{7,3},{8,12},{9,13},{10,... | collective-permute-start | bytes 294920 | tf_op jit(solution)/shard_map/ppermute | solution.py:347
  164.4 2.5 %collective-permute-start.25 = (bf16[64,768]{1,0:T(8,128)(2,1)S(1)}, bf16[64,768]{1,0:T(8,128)(2,1)S(1)}, u32[]{:S(2)}, u32[]{:S(2)}) collective-permute-start(bf16[64,768]{1,0:T(8,128)(2,1)S(1)} %get-tuple-element.61), channel_id=1, source_target_pairs={{0,6},{1,7},{2,4},{3,5},{4,2},{5,3},{6,0},{7,1},{8,14},{9,15},{10,... | collective-permute-start | bytes 294920 | tf_op jit(solution)/shard_map/ppermute | solution.py:347
  167.2 7.4 %collective-permute-done.24.refs_6_ = bf16[64,768]{1,0:T(8,128)(2,1)S(1)} collective-permute-done((bf16[64,768]{1,0:T(8,128)(2,1)S(1)}, bf16[64,768]{1,0:T(8,128)(2,1)S(1)}, u32[]{:S(2)}, u32[]{:S(2)}) %collective-permute-start.24) | collective-permute-done | bytes 98336 | tf_op jit(solution)/shard_map/ppermute | solution.py:347
  178.2 2.1 %collective-permute-start.42 = (f32[8,64]{1,0:T(8,128)S(1)}, f32[8,64]{1,0:T(8,128)S(1)}, u32[]{:S(2)}, u32[]{:S(2)}) collective-permute-start(f32[8,64]{1,0:T(8,128)S(1)} %get-tuple-element.79), channel_id=1, source_target_pairs={{0,4},{1,5},{2,6},{3,7},{4,0},{5,1},{6,2},{7,3},{8,12},{9,13},{10,... | collective-permute-start | bytes 6152 | tf_op jit(solution)/shard_map/ppermute | solution.py:347
  (132 shorter events, 33.6 us)
Async XLA Ops:
  7.4 31.5 %collective-permute-start.1 = (bf16[2,3,96,384]{3,2,1,0:T(8,128)(2,1)}, bf16[2,3,96,384]{3,2,1,0:T(8,128)(2,1)}, u32[]{:S(2)}, u32[]{:S(2)}) collective-permute-start(bf16[2,3,96,384]{3,2,1,0:T(8,128)(2,1)} %get-tuple-element.30.refs_1_), channel_id=1, source_target_pairs={{0,16},{8,24},{16,0},{24,8},{1,17},{9,25},{17,1},{25,9},{2,18},{10... | collective-permute-start | bytes 1327112 | tf_op jit(solution)/shard_map/ppermute | solution.py:347
  10.4 30.7 %collective-permute-start = (bf16[2,3,96,384]{3,2,1,0:T(8,128)(2,1)}, bf16[2,3,96,384]{3,2,1,0:T(8,128)(2,1)}, u32[]{:S(2)}, u32[]{:S(2)}) collective-permute-start(bf16[2,3,96,384]{3,2,1,0:T(8,128)(2,1)} %get-tuple-element.29.refs_0_), channel_id=1, source_target_pairs={{0,8},{8,0},{16,24},{24,16},{1,9},{9,1},{17,25},{25,17},{2,10},{10... | collective-permute-start | bytes 1327112 | tf_op jit(solution)/shard_map/ppermute | solution.py:347
  12.0 22.9 %collective-permute-start.5 = (s32[2,768]{1,0:T(2,128)S(1)}, s32[2,768]{1,0:T(2,128)}, u32[]{:S(2)}, u32[]{:S(2)}) collective-permute-start(s32[2,768]{1,0:T(2,128)S(1)} %pad_add_fusion.refs_0_), channel_id=1, source_target_pairs={{0,2},{1,3},{2,0},{3,1},{4,6},{5,7},{6,4},{7,5},{8,10},{9,11},{10,... | collective-permute-start | bytes 18440 | tf_op jit(solution)/shard_map/ppermute | solution.py:347
  13.6 22.4 %collective-permute-start.6 = (s32[2,768]{1,0:T(2,128)S(1)}, s32[2,768]{1,0:T(2,128)}, u32[]{:S(2)}, u32[]{:S(2)}) collective-permute-start(s32[2,768]{1,0:T(2,128)S(1)} %pad_add_fusion.refs_0_), channel_id=1, source_target_pairs={{0,4},{1,5},{2,6},{3,7},{4,0},{5,1},{6,2},{7,3},{8,12},{9,13},{10,... | collective-permute-start | bytes 18440 | tf_op jit(solution)/shard_map/ppermute | solution.py:347
  16.2 20.3 %collective-permute-start.7 = (s32[2,768]{1,0:T(2,128)S(1)}, s32[2,768]{1,0:T(2,128)}, u32[]{:S(2)}, u32[]{:S(2)}) collective-permute-start(s32[2,768]{1,0:T(2,128)S(1)} %pad_add_fusion.refs_0_), channel_id=1, source_target_pairs={{0,6},{1,7},{2,4},{3,5},{4,2},{5,3},{6,0},{7,1},{8,14},{9,15},{10,... | collective-permute-start | bytes 18440 | tf_op jit(solution)/shard_map/ppermute | solution.py:347
  34.9 15.5 %collective-permute-start.26 = (bf16[2,3,96,384]{3,2,1,0:T(8,128)(2,1)}, bf16[2,3,96,384]{3,2,1,0:T(8,128)(2,1)S(1)}, u32[]{:S(2)}, u32[]{:S(2)}) collective-permute-start(bf16[2,3,96,384]{3,2,1,0:T(8,128)(2,1)} %copy-done.5), channel_id=1, source_target_pairs={{0,8},{8,0},{16,24},{24,16},{1,9},{9,1},{17,25},{25,17},{2,10},{10... | collective-permute-start | bytes 1327112 | tf_op jit(solution)/shard_map/ppermute | solution.py:347
  36.0 13.3 %collective-permute-start.27 = (bf16[2,3,96,384]{3,2,1,0:T(8,128)(2,1)}, bf16[2,3,96,384]{3,2,1,0:T(8,128)(2,1)S(1)}, u32[]{:S(2)}, u32[]{:S(2)}) collective-permute-start(bf16[2,3,96,384]{3,2,1,0:T(8,128)(2,1)} %copy-done.7), channel_id=1, source_target_pairs={{0,16},{8,24},{16,0},{24,8},{1,17},{9,25},{17,1},{25,9},{2,18},{10... | collective-permute-start | bytes 1327112 | tf_op jit(solution)/shard_map/ppermute | solution.py:347
  40.1 17.6 %collective-permute-start.2 = (bf16[2,3,96,384]{3,2,1,0:T(8,128)(2,1)S(1)}, bf16[2,3,96,384]{3,2,1,0:T(8,128)(2,1)S(1)}, u32[]{:S(2)}, u32[]{:S(2)}) collective-permute-start(bf16[2,3,96,384]{3,2,1,0:T(8,128)(2,1)S(1)} %broadcast_select_fusion.7), channel_id=1, source_target_pairs={{0,8},{8,0},{16,24},{24,16},{1,9},{9,1},{17,25},{25,17},{2,10},{10... | collective-permute-start | bytes 1327112 | tf_op jit(solution)/shard_map/ppermute | solution.py:347
  42.2 16.6 %collective-permute-start.3 = (bf16[2,3,96,384]{3,2,1,0:T(8,128)(2,1)S(1)}, bf16[2,3,96,384]{3,2,1,0:T(8,128)(2,1)S(1)}, u32[]{:S(2)}, u32[]{:S(2)}) collective-permute-start(bf16[2,3,96,384]{3,2,1,0:T(8,128)(2,1)S(1)} %broadcast_select_fusion.6), channel_id=1, source_target_pairs={{0,16},{8,24},{16,0},{24,8},{1,17},{9,25},{17,1},{25,9},{2,18},{10... | collective-permute-start | bytes 1327112 | tf_op jit(solution)/shard_map/ppermute | solution.py:347
  49.4 24.0 %collective-permute-start.28 = (bf16[2,3,96,384]{3,2,1,0:T(8,128)(2,1)S(1)}, bf16[2,3,96,384]{3,2,1,0:T(8,128)(2,1)S(1)}, u32[]{:S(2)}, u32[]{:S(2)}) collective-permute-start(bf16[2,3,96,384]{3,2,1,0:T(8,128)(2,1)S(1)} %broadcast_select_fusion.3), channel_id=1, source_target_pairs={{0,8},{8,0},{16,24},{24,16},{1,9},{9,1},{17,25},{25,17},{2,10},{10... | collective-permute-start | bytes 1327112 | tf_op jit(solution)/shard_map/ppermute | solution.py:347
  50.5 22.9 %collective-permute-start.29 = (bf16[2,3,96,384]{3,2,1,0:T(8,128)(2,1)S(1)}, bf16[2,3,96,384]{3,2,1,0:T(8,128)(2,1)S(1)}, u32[]{:S(2)}, u32[]{:S(2)}) collective-permute-start(bf16[2,3,96,384]{3,2,1,0:T(8,128)(2,1)S(1)} %broadcast_select_fusion.2), channel_id=1, source_target_pairs={{0,16},{8,24},{16,0},{24,8},{1,17},{9,25},{17,1},{25,9},{2,18},{10... | collective-permute-start | bytes 1327112 | tf_op jit(solution)/shard_map/ppermute | solution.py:347
  71.6 16.2 %collective-permute-start.8 = (bf16[4,64,768]{2,1,0:T(8,128)(2,1)S(1)}, bf16[4,64,768]{2,1,0:T(8,128)(2,1)S(1)}, u32[]{:S(2)}, u32[]{:S(2)}) collective-permute-start(bf16[4,64,768]{2,1,0:T(8,128)(2,1)S(1)} %get-tuple-element.36), channel_id=1, source_target_pairs={{0,1},{1,0},{2,3},{3,2},{4,5},{5,4},{6,7},{7,6},{8,9},{9,8},{10,11... | collective-permute-start | bytes 1179656 | tf_op jit(solution)/shard_map/ppermute | solution.py:347
  71.8 18.7 %collective-permute-start.16 = (bf16[2,3,96,384]{3,2,1,0:T(8,128)(2,1)S(1)}, bf16[2,3,96,384]{3,2,1,0:T(8,128)(2,1)S(1)}, u32[]{:S(2)}, u32[]{:S(2)}) collective-permute-start(bf16[2,3,96,384]{3,2,1,0:T(8,128)(2,1)S(1)} %broadcast_select_fusion.5), channel_id=1, source_target_pairs={{0,8},{8,0},{16,24},{24,16},{1,9},{9,1},{17,25},{25,17},{2,10},{10... | collective-permute-start | bytes 1327112 | tf_op jit(solution)/shard_map/ppermute | solution.py:347
  73.1 21.0 %collective-permute-start.17 = (bf16[2,3,96,384]{3,2,1,0:T(8,128)(2,1)S(1)}, bf16[2,3,96,384]{3,2,1,0:T(8,128)(2,1)S(1)}, u32[]{:S(2)}, u32[]{:S(2)}) collective-permute-start(bf16[2,3,96,384]{3,2,1,0:T(8,128)(2,1)S(1)} %broadcast_select_fusion.4), channel_id=1, source_target_pairs={{0,16},{8,24},{16,0},{24,8},{1,17},{9,25},{17,1},{25,9},{2,18},{10... | collective-permute-start | bytes 1327112 | tf_op jit(solution)/shard_map/ppermute | solution.py:347
  86.7 20.7 %collective-permute-start.34 = (bf16[2,3,96,384]{3,2,1,0:T(8,128)(2,1)S(1)}, bf16[2,3,96,384]{3,2,1,0:T(8,128)(2,1)S(1)}, u32[]{:S(2)}, u32[]{:S(2)}) collective-permute-start(bf16[2,3,96,384]{3,2,1,0:T(8,128)(2,1)S(1)} %broadcast_select_fusion.1), channel_id=1, source_target_pairs={{0,8},{8,0},{16,24},{24,16},{1,9},{9,1},{17,25},{25,17},{2,10},{10... | collective-permute-start | bytes 1327112 | tf_op jit(solution)/shard_map/ppermute | solution.py:347
  87.9 20.0 %collective-permute-start.35 = (bf16[2,3,96,384]{3,2,1,0:T(8,128)(2,1)S(1)}, bf16[2,3,96,384]{3,2,1,0:T(8,128)(2,1)S(1)}, u32[]{:S(2)}, u32[]{:S(2)}) collective-permute-start(bf16[2,3,96,384]{3,2,1,0:T(8,128)(2,1)S(1)} %broadcast_select_fusion), channel_id=1, source_target_pairs={{0,16},{8,24},{16,0},{24,8},{1,17},{9,25},{17,1},{25,9},{2,18},{10... | collective-permute-start | bytes 1327112 | tf_op jit(solution)/shard_map/ppermute | solution.py:347
  89.6 31.5 %collective-permute-start.9 = (bf16[64,768]{1,0:T(8,128)(2,1)S(1)}, bf16[64,768]{1,0:T(8,128)(2,1)S(1)}, u32[]{:S(2)}, u32[]{:S(2)}) collective-permute-start(bf16[64,768]{1,0:T(8,128)(2,1)S(1)} %get-tuple-element.75), channel_id=1, source_target_pairs={{0,2},{1,3},{2,0},{3,1},{4,6},{5,7},{6,4},{7,5},{8,10},{9,11},{10,... | collective-permute-start | bytes 294920 | tf_op jit(solution)/shard_map/ppermute | solution.py:347
  90.4 31.2 %collective-permute-start.10 = (bf16[64,768]{1,0:T(8,128)(2,1)S(1)}, bf16[64,768]{1,0:T(8,128)(2,1)S(1)}, u32[]{:S(2)}, u32[]{:S(2)}) collective-permute-start(bf16[64,768]{1,0:T(8,128)(2,1)S(1)} %get-tuple-element.74), channel_id=1, source_target_pairs={{0,4},{1,5},{2,6},{3,7},{4,0},{5,1},{6,2},{7,3},{8,12},{9,13},{10,... | collective-permute-start | bytes 294920 | tf_op jit(solution)/shard_map/ppermute | solution.py:347
  94.1 27.6 %collective-permute-start.11 = (bf16[64,768]{1,0:T(8,128)(2,1)S(1)}, bf16[64,768]{1,0:T(8,128)(2,1)S(1)}, u32[]{:S(2)}, u32[]{:S(2)}) collective-permute-start(bf16[64,768]{1,0:T(8,128)(2,1)S(1)} %get-tuple-element.73), channel_id=1, source_target_pairs={{0,6},{1,7},{2,4},{3,5},{4,2},{5,3},{6,0},{7,1},{8,14},{9,15},{10,... | collective-permute-start | bytes 294920 | tf_op jit(solution)/shard_map/ppermute | solution.py:347
  107.3 40.8 %collective-permute-start.31 = (bf16[64,768]{1,0:T(8,128)(2,1)S(1)}, bf16[64,768]{1,0:T(8,128)(2,1)S(1)}, u32[]{:S(2)}, u32[]{:S(2)}) collective-permute-start(bf16[64,768]{1,0:T(8,128)(2,1)S(1)} %get-tuple-element.59), channel_id=1, source_target_pairs={{0,2},{1,3},{2,0},{3,1},{4,6},{5,7},{6,4},{7,5},{8,10},{9,11},{10,... | collective-permute-start | bytes 294920 | tf_op jit(solution)/shard_map/ppermute | solution.py:347
  107.8 16.9 %collective-permute-start.18 = (bf16[4,64,768]{2,1,0:T(8,128)(2,1)S(1)}, bf16[4,64,768]{2,1,0:T(8,128)(2,1)S(1)}, u32[]{:S(2)}, u32[]{:S(2)}) collective-permute-start(bf16[4,64,768]{2,1,0:T(8,128)(2,1)S(1)} %get-tuple-element.40), channel_id=1, source_target_pairs={{0,1},{1,0},{2,3},{3,2},{4,5},{5,4},{6,7},{7,6},{8,9},{9,8},{10,11... | collective-permute-start | bytes 1179656 | tf_op jit(solution)/shard_map/ppermute | solution.py:347
  124.6 20.6 %collective-permute-start.12 = (bf16[4,64,768]{2,1,0:T(8,128)(2,1)S(1)}, bf16[4,64,768]{2,1,0:T(8,128)(2,1)S(1)}, u32[]{:S(2)}, u32[]{:S(2)}) collective-permute-start(bf16[4,64,768]{2,1,0:T(8,128)(2,1)S(1)} %get-tuple-element.38), channel_id=1, source_target_pairs={{0,1},{1,0},{2,3},{3,2},{4,5},{5,4},{6,7},{7,6},{8,9},{9,8},{10,11... | collective-permute-start | bytes 1179656 | tf_op jit(solution)/shard_map/ppermute | solution.py:347
  128.8 13.3 %collective-permute-start.21 = (bf16[64,768]{1,0:T(8,128)(2,1)S(1)}, bf16[64,768]{1,0:T(8,128)(2,1)S(1)}, u32[]{:S(2)}, u32[]{:S(2)}) collective-permute-start(bf16[64,768]{1,0:T(8,128)(2,1)S(1)} %get-tuple-element.65), channel_id=1, source_target_pairs={{0,6},{1,7},{2,4},{3,5},{4,2},{5,3},{6,0},{7,1},{8,14},{9,15},{10,... | collective-permute-start | bytes 294920 | tf_op jit(solution)/shard_map/ppermute | solution.py:347
  130.3 21.1 %collective-permute-start.32 = (bf16[64,768]{1,0:T(8,128)(2,1)S(1)}, bf16[64,768]{1,0:T(8,128)(2,1)S(1)}, u32[]{:S(2)}, u32[]{:S(2)}) collective-permute-start(bf16[64,768]{1,0:T(8,128)(2,1)S(1)} %get-tuple-element.58), channel_id=1, source_target_pairs={{0,4},{1,5},{2,6},{3,7},{4,0},{5,1},{6,2},{7,3},{8,12},{9,13},{10,... | collective-permute-start | bytes 294920 | tf_op jit(solution)/shard_map/ppermute | solution.py:347
  134.3 17.2 %collective-permute-start.33 = (bf16[64,768]{1,0:T(8,128)(2,1)S(1)}, bf16[64,768]{1,0:T(8,128)(2,1)S(1)}, u32[]{:S(2)}, u32[]{:S(2)}) collective-permute-start(bf16[64,768]{1,0:T(8,128)(2,1)S(1)} %get-tuple-element.57), channel_id=1, source_target_pairs={{0,6},{1,7},{2,4},{3,5},{4,2},{5,3},{6,0},{7,1},{8,14},{9,15},{10,... | collective-permute-start | bytes 294920 | tf_op jit(solution)/shard_map/ppermute | solution.py:347
  142.1 10.6 %collective-permute-start.37 = (bf16[64,768]{1,0:T(8,128)(2,1)S(1)}, bf16[64,768]{1,0:T(8,128)(2,1)S(1)}, u32[]{:S(2)}, u32[]{:S(2)}) collective-permute-start(bf16[64,768]{1,0:T(8,128)(2,1)S(1)} %get-tuple-element.55), channel_id=1, source_target_pairs={{0,2},{1,3},{2,0},{3,1},{4,6},{5,7},{6,4},{7,5},{8,10},{9,11},{10,... | collective-permute-start | bytes 294920 | tf_op jit(solution)/shard_map/ppermute | solution.py:347
  147.0 10.9 %collective-permute-start.38 = (bf16[64,768]{1,0:T(8,128)(2,1)S(1)}, bf16[64,768]{1,0:T(8,128)(2,1)S(1)}, u32[]{:S(2)}, u32[]{:S(2)}) collective-permute-start(bf16[64,768]{1,0:T(8,128)(2,1)S(1)} %get-tuple-element.54), channel_id=1, source_target_pairs={{0,4},{1,5},{2,6},{3,7},{4,0},{5,1},{6,2},{7,3},{8,12},{9,13},{10,... | collective-permute-start | bytes 294920 | tf_op jit(solution)/shard_map/ppermute | solution.py:347
  151.4 13.0 %collective-permute-start.13 = (bf16[64,768]{1,0:T(8,128)(2,1)S(1)}, bf16[64,768]{1,0:T(8,128)(2,1)S(1)}, u32[]{:S(2)}, u32[]{:S(2)}) collective-permute-start(bf16[64,768]{1,0:T(8,128)(2,1)S(1)} %get-tuple-element.71), channel_id=1, source_target_pairs={{0,2},{1,3},{2,0},{3,1},{4,6},{5,7},{6,4},{7,5},{8,10},{9,11},{10,... | collective-permute-start | bytes 294920 | tf_op jit(solution)/shard_map/ppermute | solution.py:347
  151.5 15.7 %collective-permute-start.14 = (bf16[64,768]{1,0:T(8,128)(2,1)S(1)}, bf16[64,768]{1,0:T(8,128)(2,1)S(1)}, u32[]{:S(2)}, u32[]{:S(2)}) collective-permute-start(bf16[64,768]{1,0:T(8,128)(2,1)S(1)} %get-tuple-element.70), channel_id=1, source_target_pairs={{0,4},{1,5},{2,6},{3,7},{4,0},{5,1},{6,2},{7,3},{8,12},{9,13},{10,... | collective-permute-start | bytes 294920 | tf_op jit(solution)/shard_map/ppermute | solution.py:347
  152.7 14.4 %collective-permute-start.15 = (bf16[64,768]{1,0:T(8,128)(2,1)S(1)}, bf16[64,768]{1,0:T(8,128)(2,1)S(1)}, u32[]{:S(2)}, u32[]{:S(2)}) collective-permute-start(bf16[64,768]{1,0:T(8,128)(2,1)S(1)} %get-tuple-element.69), channel_id=1, source_target_pairs={{0,6},{1,7},{2,4},{3,5},{4,2},{5,3},{6,0},{7,1},{8,14},{9,15},{10,... | collective-permute-start | bytes 294920 | tf_op jit(solution)/shard_map/ppermute | solution.py:347
  157.9 16.7 %collective-permute-start.24 = (bf16[64,768]{1,0:T(8,128)(2,1)S(1)}, bf16[64,768]{1,0:T(8,128)(2,1)S(1)}, u32[]{:S(2)}, u32[]{:S(2)}) collective-permute-start(bf16[64,768]{1,0:T(8,128)(2,1)S(1)} %get-tuple-element.62), channel_id=1, source_target_pairs={{0,4},{1,5},{2,6},{3,7},{4,0},{5,1},{6,2},{7,3},{8,12},{9,13},{10,... | collective-permute-start | bytes 294920 | tf_op jit(solution)/shard_map/ppermute | solution.py:347
  164.4 10.1 %collective-permute-start.25 = (bf16[64,768]{1,0:T(8,128)(2,1)S(1)}, bf16[64,768]{1,0:T(8,128)(2,1)S(1)}, u32[]{:S(2)}, u32[]{:S(2)}) collective-permute-start(bf16[64,768]{1,0:T(8,128)(2,1)S(1)} %get-tuple-element.61), channel_id=1, source_target_pairs={{0,6},{1,7},{2,4},{3,5},{4,2},{5,3},{6,0},{7,1},{8,14},{9,15},{10,... | collective-permute-start | bytes 294920 | tf_op jit(solution)/shard_map/ppermute | solution.py:347
  (29 other events, 254.7 us)

commit v2 on v1

v2 whole, which is shorter than its diff:
```python
import functools
import math

import jax
import jax.numpy as jnp
import numpy as np
from jax import lax
from jax.experimental import pallas as pl
from jax.experimental.pallas import tpu as pltpu
from jax.sharding import PartitionSpec as P

GRID_N = 96
KF = 32
BLK = 8
XG = 4
LANES = XG * GRID_N
F32 = jnp.float32
BF16 = jnp.bfloat16
WHOLE_VMEM = 56 * 1024 * 1024
PART_VMEM = 20 * 1024 * 1024
FRONT_VMEM = 24 * 1024 * 1024


def fourier_parts(length, kept):
    phase = np.arange(length)[:, None] * (np.arange(kept) - kept // 2)[None, :] % length * (2.0 * math.pi / length)
    return (np.cos(phase) / math.sqrt(length)).astype(BF16), (np.sin(phase) / math.sqrt(length)).astype(BF16)


def classes_of(own_y):
    return XG if own_y == XG else 1


def y_table(cosine, sine, classes):
    order = np.arange(GRID_N).reshape(-1, XG).T.reshape(-1)
    one = np.stack([cosine[order].T, -sine[order].T]).reshape(2, KF // classes, classes, GRID_N)
    table = np.zeros((2, classes, 2, KF // classes, 2, GRID_N), BF16)
    for pair in range(2):
        table[:, :, pair, :, pair] = one.transpose(0, 2, 1, 3)
    return table.reshape(4 * KF, 2 * GRID_N)


def z_table(cosine, sine, classes):
    both = np.stack([np.stack([cosine, -sine], axis=1), np.stack([sine, cosine], axis=1)])
    table = np.zeros((2, XG, GRID_N, XG, 2, KF), BF16)
    for x in range(XG):
        table[:, x, :, x] = both
    table = table.reshape(2 * LANES, 2, 4, KF)
    return np.stack([np.roll(table, i, axis=2).reshape(2 * LANES, XG * 2 * KF) for i in range(classes)])


def x_phases(n_grid):
    slab = GRID_N // n_grid
    lines = -(-slab // XG) * XG // 2
    freqs = 2.0 * math.pi / GRID_N * (np.arange(KF) - KF // 2)
    away = (lines - 0.5 - np.arange(lines))[:, None] * freqs
    middle = (slab * np.arange(n_grid) + lines - 0.5)[:, None, None] * freqs
    scale = 1.0 / math.sqrt(GRID_N)
    fixed = np.broadcast_to(np.concatenate([np.cos(away), np.sin(away)]), (n_grid, 2 * lines, KF))
    rows = np.concatenate([fixed, np.cos(middle) * scale, np.sin(middle) * scale], axis=1)
    rows = np.pad(rows, ((0, 0), (0, -rows.shape[1] % 8), (0, 0)))
    high = rows.astype(BF16)
    return np.stack([high, (rows - high.astype(np.float64)).astype(BF16)], axis=1)


HOLDS = np.array([[0, 1, 3, 2], [0, 2, 3, 1], [1, 3, 0, 2], [1, 0, 3, 2]])
SOURCES = np.array([[0, 1, 1, 0], [2, 4, 2, 3], [3, 5, 2, 3], [4, 5, 2, 3]])


def slots_of():
    quarter = BLK // 4
    return np.argsort((quarter * HOLDS[:, :, None] + np.arange(quarter)).reshape(4, BLK), axis=1)


def planes_kernel(firsts, blocks, src, *refs):
    outs, (rows, held, arrived) = refs[:-3], refs[-3:]
    groups, together = outs[0].shape[1], held.shape[0] // outs[0].shape[1]
    functions = src.shape[1]
    tiles, high = LANES // 128, GRID_N // XG

    def fetch(group):
        part = pl.ds(together * group, together)
        return pltpu.make_async_copy(src.at[part], held.at[part], arrived.at[group])

    for group in range(groups):
        fetch(group).start()
    for group in range(groups):
        fetch(group).wait()
        for x in range(together):
            for y in range(high):
                for t in range(tiles):
                    cut = slice(y * LANES + 128 * t, y * LANES + 128 * t + 128)
                    rows[x * tiles + t, y * functions:(y + 1) * functions, :] = held[together * group + x, :, cut].astype(F32)
        for first, out in zip(firsts, outs, strict=True):
            for f in range(out.shape[0]):
                at = pl.ds(first(blocks) + f, high, stride=functions)
                wide = [jnp.concatenate([rows[x * tiles + t, at, :] for t in range(tiles)], axis=1) for x in range(together)]
                wide += [jnp.zeros((high, LANES), F32)] * (XG - together)
                lines = [
                    jnp.concatenate([w[:, GRID_N * low:GRID_N * low + GRID_N] for w in wide], axis=1) for low in range(XG)
                ]
                out[f, group] = jnp.concatenate(lines, axis=0).astype(BF16)


def planes(orbitals, blocks, firsts, count, stay=False):
    orbitals = jnp.transpose(orbitals, (1, 0, 2))
    slab, functions, size = orbitals.shape
    together = min(XG, slab)
    groups = slab // together
    shape = (count, groups, GRID_N, LANES)
    spec = pltpu.PrefetchScalarGridSpec(
        num_scalar_prefetch=1,
        grid=(1,),
        in_specs=[pl.BlockSpec(memory_space=pl.ANY)],
        out_specs=[pl.BlockSpec(shape, lambda g, b: (0, 0, 0, 0))] * len(firsts),
        scratch_shapes=[
            pltpu.VMEM((LANES // 128 * together, GRID_N // XG * functions, 128), F32),
            pltpu.VMEM((slab, functions, size), BF16),
            pltpu.SemaphoreType.DMA((groups,)),
        ],
    )
    return pl.pallas_call(
        functools.partial(planes_kernel, firsts),
        grid_spec=spec,
        out_shape=[jax.ShapeDtypeStruct(shape, BF16)] * len(firsts),
        compiler_params=pltpu.CompilerParams(vmem_limit_bytes=WHOLE_VMEM if stay else PART_VMEM),
        cost_estimate=pl.CostEstimate(flops=0, bytes_accessed=4 * slab * functions * size, transcendentals=0),
        name="planes",
    )(blocks, orbitals)


def tables_kernel(*refs):
    *points, phases, pick, wave = refs
    cols = pick.shape[1]
    phase = phases[lax.axis_index("grid")]
    for r in range(pick.shape[0]):
        half = points[0].shape[0]
        point = points[r // half][r % half:r % half + 1, :]
        shape = (cols, point.shape[1])
        found = lax.broadcasted_iota(jnp.int32, shape, 0) == jnp.broadcast_to(point & (cols - 1), shape)
        pick[r] = found.astype(F32).astype(BF16)
        shape = (KF, point.shape[1])
        turn = lax.broadcasted_iota(jnp.int32, shape, 0) == jnp.broadcast_to(point >> (cols.bit_length() - 1), shape)
        turn = turn.astype(F32).astype(BF16)
        wave[r] = sum(jnp.dot(phase[i], turn, preferred_element_type=F32) for i in range(2))


def tables(points, phases, cols):
    targets, own = 2 * points[0].shape[0], points[0].shape[1]
    return pl.pallas_call(
        tables_kernel,
        out_shape=[
            jax.ShapeDtypeStruct((targets, cols, own), BF16),
            jax.ShapeDtypeStruct((targets, phases.shape[2], own), F32),
        ],
        compiler_params=pltpu.CompilerParams(vmem_limit_bytes=16 * 1024 * 1024),
        cost_estimate=pl.CostEstimate(flops=0, bytes_accessed=3 * targets * cols * own, transcendentals=0),
        name="tables",
    )(*points, phases)


def front_kernel(sources, find, blocks, source_of, *refs):
    parts_in, refs = refs[:sources], refs[sources:]
    cond, ytab, ztab, pick, wave, even, odd, vals, mixed, section, arrived = refs
    conds, groups = cond.shape[0], cond.shape[1]
    cols = pick.shape[1]
    own_y = cols // KF
    classes = ztab.shape[0]
    each = KF // classes
    count = vals.shape[0]
    for f in range(count):
        wanted, inside = find(blocks, source_of, f)
        for s in range(sources):
            @pl.when(wanted == s)
            def _(f=f, s=s):
                pltpu.make_async_copy(parts_in[s].at[inside], vals.at[f], arrived.at[f]).start()

    units = [(pair, group) for pair in range(conds // 2) for group in range(groups)]
    rows = 2 * each

    def sections(now, carry):
        pltpu.make_async_copy(parts_in[0].at[0], vals.at[now], arrived.at[now]).wait()
        for first in range(0, len(units), 2):
            two = units[first:first + 2]
            density = [
                jnp.concatenate([vals[now, group] * cond[2 * pair + i, group] for pair, group in two], axis=1) for i in range(2)
            ]
            out = jnp.dot(ytab[...], jnp.concatenate(density, axis=0), preferred_element_type=F32).astype(BF16)
            for i, (pair, group) in enumerate(two):
                at = (group * conds + 2 * pair) * each
                for kind in range(classes):
                    for half in range(2):
                        base = (half * classes + kind) * rows
                        mixed[kind, at:at + rows, half * LANES:half * LANES + LANES] = out[base:base + rows, i * LANES:i * LANES + LANES]
        for kind in range(classes):
            value = jnp.dot(mixed[kind], ztab[kind], preferred_element_type=F32)
            section[now, 2 * kind] = value[:, :128]
            section[now, 2 * kind + 1] = value[:, 128:]
        return carry

    lax.fori_loop(0, count, sections, 0)
    place = lax.broadcasted_iota(jnp.int32, (conds, 128), 1) // KF
    planes_in = [(group, half) for group in range(groups) for half in range(2)]

    def rows_of(f, kind, half, group, k):
        return section[f, 2 * kind + half, pl.ds(group * conds * each + k, conds, stride=each), :]

    def pieces_of(f, target):
        if classes == 1:
            parts = []
            for group, half in planes_in:
                rows = [rows_of(f, 0, half, group, target * own_y + y) for y in range(own_y)]
                for piece in range(4):
                    cut = slice(KF * piece, KF * piece + KF)
                    parts.append(jnp.concatenate([row[:, cut] for row in rows], axis=1))
            return parts
        found = {}
        loaded = [[rows_of(f, kind, half, group, target) for kind in range(classes)] for group, half in planes_in]
        for piece in range(4):
            merged = []
            for rows in loaded:
                value = rows[-piece % 4]
                for slot in range(1, 4):
                    value = jnp.where(place == slot, rows[(slot - piece) % 4], value)
                merged.append(value)
            turned = jnp.concatenate(merged, axis=0)
            if piece:
                turned = pltpu.roll(turned, 128 - KF * piece, 1)
            for i in range(len(planes_in)):
                found[4 * i + piece] = turned[i * conds:(i + 1) * conds]
        return [found[i] for i in range(4 * len(planes_in))]

    def folded(f, target):
        parts = pieces_of(f, target)
        planes_count = len(parts) // 2
        out = []
        for x in range(planes_count // 2):
            high = planes_count - 1 - x
            out += [parts[2 * high + i] + parts[2 * x + i] for i in range(2)]
            out += [parts[2 * high + i] - parts[2 * x + i] for i in range(2)]
        return out

    def one_target(step, parity, out_ref):
        order = target_of(step, pick.shape[0]) + parity
        target = lax.axis_index("grid").astype(jnp.int32) ^ order
        parts = [folded(f, target) for f in range(count)]
        lines = XG * groups // 2
        left = jnp.concatenate([p for part in parts for p in part], axis=0).astype(BF16)
        found = jnp.dot(left, pick[order], preferred_element_type=F32)
        turn = [wave[order, i:i + 1, :] for i in range(2 * lines + 2)]
        for f in range(count):
            real = imag = None
            for x in range(lines):
                cosine, sine = turn[x], turn[lines + x]
                base = 4 * (f * lines + x) * conds
                sum_re, sum_im, diff_re, diff_im = (found[base + i * conds:base + (i + 1) * conds] for i in range(4))
                add_real = sum_re * cosine + diff_im * sine
                add_imag = sum_im * cosine - diff_re * sine
                real = add_real if real is None else real + add_real
                imag = add_imag if imag is None else imag + add_imag
            cosine, sine = turn[2 * lines], turn[2 * lines + 1]
            both = [real * cosine + imag * sine, imag * cosine - real * sine]
            out_ref[step, 2 * conds * f:2 * conds * f + 2 * conds, :] = jnp.concatenate(both, axis=0).astype(BF16)

    def body(step, carry):
        one_target(step, 0, even)
        one_target(step, 1, odd)
        return carry

    lax.fori_loop(0, even.shape[0], body, 0)


def front(find, count, blocks, sources, cond, ytab, ztab, pick, wave):
    conds, groups = cond.shape[:2]
    targets, cols, own = pick.shape
    classes = ztab.shape[0]
    rows = 2 * conds
    shape = jax.ShapeDtypeStruct((targets // 2, count * rows, own), BF16)
    inside, scalars = pl.BlockSpec(memory_space=pltpu.VMEM), pl.BlockSpec(memory_space=pltpu.SMEM)
    return pl.pallas_call(
        functools.partial(front_kernel, len(sources), find),
        in_specs=[scalars] * 2 + [pl.BlockSpec(memory_space=pl.ANY)] * len(sources) + [inside] * 5,
        out_specs=[inside] * 2,
        scratch_shapes=[
            pltpu.VMEM((count,) + cond.shape[1:], BF16),
            pltpu.VMEM((classes, groups * conds * KF // classes, 2 * LANES), BF16),
            pltpu.VMEM((count, 2 * classes, groups * conds * KF // classes, XG * KF), F32),
            pltpu.SemaphoreType.DMA((count,)),
        ],
        out_shape=[shape, shape],
        compiler_params=pltpu.CompilerParams(vmem_limit_bytes=FRONT_VMEM),
        cost_estimate=pl.CostEstimate(flops=count * 900_000_000, bytes_accessed=count * 2_000_000, transcendentals=0),
        name="front",
    )(blocks, jnp.asarray(SOURCES.reshape(-1), jnp.int32), *sources, cond, ytab, ztab, pick, wave)


def screen_kernel(split, here, *refs):
    *pieces, w_even, w_odd, even, odd, side = refs

    @pl.when(pl.program_id(0) == 0)
    def _():
        first = 0
        for i, count in enumerate(split):
            group = pieces[sum(split[:i]):sum(split[:i]) + count]
            total = group[0][...].astype(F32)
            for piece in group[1:]:
                total = total + piece[...].astype(F32)
            side[first:first + total.shape[0], :] = total.astype(BF16)
            first += total.shape[0]

    even[0] = jnp.dot(side[...], w_even[...], preferred_element_type=F32).astype(BF16)
    odd[0] = jnp.dot(side[...], w_odd[...], preferred_element_type=F32).astype(BF16)


def screen(here, parts, screened, targets):
    own = parts[0][0].shape[1]
    rows = sum(p[0].shape[0] for p in parts)
    flat = [piece for part in parts for piece in part]
    if own % 128:
        side = jnp.concatenate([sum(p.astype(F32) for p in part) for part in parts], axis=0).astype(BF16)
        part = jnp.dot(side, screened, preferred_element_type=F32).astype(BF16)
        part = jnp.transpose(part.reshape(rows, targets, own), (1, 0, 2))
        even = here[0] ^ target_of(jnp.arange(targets // 2, dtype=jnp.int32), targets)
        return jnp.take(part, even, axis=0), jnp.take(part, even ^ 1, axis=0)
    shape = jax.ShapeDtypeStruct((targets // 2, rows, own), BF16)
    spec = pltpu.PrefetchScalarGridSpec(
        num_scalar_prefetch=1,
        grid=(targets // 2,),
        in_specs=[pl.BlockSpec(x.shape, lambda r, h: (0, 0)) for x in flat] + [
            pl.BlockSpec((own, own), lambda r, h: (0, h[0] ^ target_of(r, targets))),
            pl.BlockSpec((own, own), lambda r, h: (0, h[0] ^ target_of(r, targets) ^ 1)),
        ],
        out_specs=[pl.BlockSpec((1, rows, own), lambda r, h: (r, 0, 0))] * 2,
        scratch_shapes=[pltpu.VMEM((rows, own), BF16)],
    )
    return pl.pallas_call(
        functools.partial(screen_kernel, [len(p) for p in parts]),
        grid_spec=spec,
        out_shape=[shape, shape],
        compiler_params=pltpu.CompilerParams(vmem_limit_bytes=WHOLE_VMEM),
        cost_estimate=pl.CostEstimate(flops=2 * rows * own * own * targets, bytes_accessed=2 * own * own * targets, transcendentals=0),
        name="screen",
    )(here, *flat, screened, screened)


def close_kernel(split, place, blocks, slot_of, *refs):
    ins, outs, sums = refs[:sum(map(sum, split))], refs[sum(map(sum, split)):-2], refs[-2:]
    chunks, functions, unit, _ = sums[0].shape
    half = unit // 2
    for side, pieces in enumerate(split):
        first = 0
        for count in pieces:
            group, ins = ins[:count], ins[count:]
            here = group[0].shape[1] // unit
            for chunk in range(chunks):
                total = group[0][chunk].astype(F32)
                for piece in group[1:]:
                    total = total + piece[chunk].astype(F32)
                sums[side][chunk, first:first + here] = total.reshape(here, unit, total.shape[1])
            first += here
    slots = [[place(blocks, slot_of, side, f) for f in range(functions)] for side in range(2)]
    product = None
    for chunk in range(chunks):
        for part in range(2):
            rows = slice(half * part, half * part + half)
            left, right = (
                jnp.concatenate([sums[side][chunk, slot][rows] for slot in slots[side]], axis=0).astype(BF16) for side in range(2)
            )
            term = lax.dot_general(left, right, (((1,), (1,)), ((), ())), preferred_element_type=F32)
            product = term if product is None else product + term
    if len(outs) == 1:
        outs[0][...] = product
    else:
        steps, rows = outs[0].shape[:2]
        for step in range(steps):
            for parity in range(2):
                first = (target_of(step, 2 * steps) + parity) * rows
                outs[parity][step] = product[first:first + rows]


def close(place, blocks, u_parts, b_parts, conds, targets, by_target):
    split = [[len(p) for p in side] for side in (u_parts, b_parts)]
    flat = [x for side in (u_parts, b_parts) for p in side for x in p]
    functions = BLK
    rows = functions * conds
    chunks, _, own = flat[0].shape
    if by_target:
        out = [jax.ShapeDtypeStruct((targets // 2, rows // targets, rows), F32)] * 2
    else:
        out = [jax.ShapeDtypeStruct((rows, rows), F32)]
    spec = pltpu.PrefetchScalarGridSpec(
        num_scalar_prefetch=2,
        grid=(1,),
        in_specs=[pl.BlockSpec(x.shape, lambda i, b, t: (0, 0, 0)) for x in flat],
        out_specs=[pl.BlockSpec(o.shape, lambda i, b, t, o=o: (0,) * len(o.shape)) for o in out],
        scratch_shapes=[pltpu.VMEM((chunks, functions, 2 * conds, own), F32)] * 2,
    )
    return pl.pallas_call(
        functools.partial(close_kernel, split, place),
        grid_spec=spec,
        out_shape=out,
        cost_estimate=pl.CostEstimate(flops=4 * rows * rows * own, bytes_accessed=8 * rows * own, transcendentals=0),
        compiler_params=pltpu.CompilerParams(vmem_limit_bytes=24 * 1024 * 1024),
        name="close",
    )(blocks, jnp.asarray(slots_of().reshape(-1), jnp.int32), *flat)


def swap(array, axis, mask, size):
    return lax.ppermute(array, axis, [(i, i ^ mask) for i in range(size)])


def target_of(step, targets):
    bits = (targets // 2).bit_length() - 1
    return 2 * sum(((step >> i) & 1) << (bits - 1 - i) for i in range(bits))


def after(value, *others):
    return lax.optimization_barrier((value, *others))[0]


def add(left, right):
    return (left.astype(F32) + right.astype(F32)).astype(left.dtype)


def halve(kept, got, mask, targets):
    half = kept.shape[0] // 2
    sent = add(kept[half:], got[half:])
    return add(kept[:half], got[:half]), swap(sent, "grid", mask, targets), sent


def halving(even, odd, targets):
    got = swap(odd, "grid", 1, targets)
    mask = 2
    while even.shape[0] > 1:
        even, got, _ = halve(even, got, mask, targets)
        mask *= 2
    return [even[0], got[0]]


def both_blocks(kept, got, targets):
    total = add(kept, got)
    come = swap(total, "grid", targets // 2, targets)
    return [total, come[::-1]]


def round_ring(own, holder, size, reverse):
    order = list(range(size))
    if reverse:
        order = order[::-1]
    pairs = [(order[i], order[(i + 1) % size]) for i in range(size)]
    place = [0] * size
    for i, device in enumerate(order):
        place[device] = i
    place = jnp.array(place, jnp.int32)
    away = (place[lax.axis_index("band")] - place[holder]) % size
    chunks = len(own)
    got = []
    for step in range(chunks + size - 2):
        mine = own[min(step, chunks - 1)]
        sent = mine if step == 0 else jnp.where(away == 0, mine, got[-1])
        got.append(lax.ppermute(sent, "band", pairs))
    out = []
    for j in range(chunks):
        value = own[j]
        for hop in range(1, size):
            value = jnp.where(away == hop, got[j + hop - 1], value)
        out.append(value)
    return out


def by_ring(valence, blocks, side, held, size):
    half = BLK // 2
    own = planes(valence, blocks, [lambda b, j=j: b[side] % held * BLK + j for j in range(BLK)], 1)
    right = round_ring(own[:half], blocks[side] // held, size, False)
    left = round_ring(own[half:], blocks[side] // held, size, True)
    return right, left


class Swaps:
    def __init__(self, own, owner):
        self.own, self.owner = own, owner
        self.got = [(own[0], own[1])]
        self.sent = [(own[0], own[1])]

    def send(self):
        across, along = self.sent[-1]
        self.got.append((swap(across, "band", 1, 4), swap(along, "band", 2, 4)))

    def choose(self):
        x, y = self.got[-1]
        ahead = (2, 3) if len(self.got) == 2 else (3, 2)
        self.sent.append(tuple(jnp.where(self.owner, self.own[q], a) for q, a in zip(ahead, (y, x), strict=True)))

    def sources(self, late):
        if late:
            return [*self.own[2:], *self.got[3]]
        return [*self.own[:2], *self.got[1], *self.got[2]]


def per_device(sizes, valence, conduction, screened, blocks, gsphere):
    n_band, n_grid = sizes
    held = valence.shape[0] // BLK
    conds, own = conduction.shape[0], gsphere.shape[0]
    cols = KF // n_grid * KF
    half, quarter = BLK // 2, BLK // 4
    swaps = n_band == 4
    at = lax.axis_index("grid").astype(jnp.int32)[None]
    cosine, sine = fourier_parts(GRID_N, KF)
    classes = classes_of(cols // KF)
    ytab, ztab = (jnp.asarray(t(cosine, sine, classes)) for t in (y_table, z_table))

    def role(b, side):
        return lax.axis_index("band").astype(jnp.int32) ^ (b[side] // held)

    def quarters(wanted, stay=False):
        firsts = [lambda b, s=s, q=q: b[s] % held * BLK + quarter * q for s, q in wanted]
        return planes(valence, blocks, firsts, quarter, stay)

    def more(points, i):
        return jnp.concatenate([points, swap(points, "grid", 1 << i, n_grid)], axis=0)

    points = gsphere.reshape(1, own)
    levels = n_grid.bit_length() - 1
    if swaps:
        own_a = quarters([(0, 0), (0, 1)], True)
        own_b = quarters([(1, 0), (1, 1), (0, 2), (0, 3), (1, 2), (1, 3)])
        a, b = (
            Swaps(o, lax.axis_index("band") == blocks[s] // held)
            for s, o in enumerate(([*own_a, *own_b[2:4]], [*own_b[:2], *own_b[4:]]))
        )
        a.send()
        a.choose()
        a.send()
        b.send()
        a.choose()
        a.send()
        points = after(points, *a.sent[1])
        conduction = after(conduction, *a.sent[1])
        for i in range(levels - 1):
            points = more(points, i)
        last = swap(points, "grid", n_grid // 2, n_grid)
        sources = lambda side, late: (a, b)[side].sources(late)
    else:
        rings = [by_ring(valence, blocks, s, held, n_band) for s in range(2)]
        sources = lambda side, late: rings[side][late]
        for i in range(levels - 1):
            points = more(points, i)
        last = swap(points, "grid", n_grid // 2, n_grid)
    cond, = planes(conduction, blocks, [lambda b: 0], conds)
    pick, wave = tables([points, last], jnp.asarray(x_phases(n_grid)), cols)

    def part(side, late, *others):
        def find(b, source_of, f):
            if not swaps:
                return f, 0
            return source_of[role(b, side) * 4 + 2 * late + f // quarter], f % quarter
        return front(find, half, after(blocks, *others), sources(side, late), cond, ytab, ztab, pick, wave)

    def core(pair):
        return pair[0], swap(pair[1], "grid", 1, n_grid)

    early_a = core(part(0, 0, *(a.sent[2] if swaps else ())))
    if swaps:
        b.got[1] = lax.optimization_barrier((*b.got[1], early_a[0]))[:2]
        b.choose()
        b.send()
    early_a = halve(*early_a, 2, n_grid)
    late_a = core(part(0, 1, early_a[2]))
    late_a = halve(*late_a, 2, n_grid)
    if swaps:
        b.choose()
        b.send()
    early_b = core(part(1, 0, late_a[2], *(b.sent[2] if swaps else ())))
    side_a = [after(early_a[0], early_b[0]), early_a[1]], [late_a[0], late_a[1]]
    side_a = [jnp.concatenate([e, l], axis=1) for e, l in zip(*side_a, strict=True)]
    side_a = halve(*side_a, 4, n_grid)
    late_b = core(part(1, 1, side_a[2]))
    early_b = halve(*early_b, 2, n_grid)

    def finish(pair, mask):
        pair = pair[:2]
        while pair[0].shape[0] > 1:
            pair = halve(*pair, mask, n_grid)[:2]
            mask *= 2
        return [p[0] for p in pair]

    def until_two(pair, mask):
        pair = pair[:2]
        while pair[0].shape[0] > 2:
            pair = halve(*pair, mask, n_grid)[:2]
            mask *= 2
        return pair

    side_a = [finish(side_a, 8)]
    part_u = screen(after(at, late_b[0]), side_a, screened, n_grid)
    late_b = until_two((after(late_b[0], part_u[0]), late_b[1]), 2)
    part_u = until_two(core(part_u), 2)
    side_b = [both_blocks(*until_two(early_b, 4), n_grid), both_blocks(*late_b, n_grid)]

    by_target = n_grid == BLK

    def place(b, slot_of, side, f):
        if side == 0 and by_target:
            f = f ^ lax.axis_index("grid").astype(jnp.int32)
        return slot_of[role(b, side) * BLK + f] if swaps else f

    shares = close(place, blocks, [part_u], side_b, conds, n_grid, by_target)
    if not by_target:
        share = shares[0].reshape(n_grid, -1, shares[0].shape[1])
        even = at ^ target_of(jnp.arange(n_grid // 2, dtype=jnp.int32), n_grid)
        shares = jnp.take(share, even, axis=0), jnp.take(share, even ^ 1, axis=0)
    return sum(halving(*shares, n_grid))[None]


def solution(mesh):
    sizes = (mesh.shape["band"], mesh.shape["grid"])
    in_specs = (P("band", "grid", None), P("band", "grid", None), P("grid", None), P(), P("grid"))
    out_specs = P("band", "grid", None)
    return jax.shard_map(
        functools.partial(per_device, sizes), mesh=mesh, in_specs=in_specs, out_specs=out_specs, check_vma=False
    )
```

time: 185 us -> 143 us (0.77)
  starting transfers between devices: 63.6 us -> 29.5 us
  Pallas kernels: 71.3 us -> 56.8 us
  local copies, waits for them, and re-layouts: 10.6 us -> 1.41 us
  other arithmetic: 3.76 us -> 11.7 us
  waiting for transfers between devices: 29.3 us -> 37.1 us
    ppermute x44 -> x31, starting transfers between devices: 63.6 us -> 29.5 us  [swap(): return lax.ppermute(array, axis, [(i, i ^ mask) for i in range(size)])]
    pallas_call x11 -> x8, Pallas kernels: 68.8 us -> 54.1 us  [the longest x4 35.3 us: front(): pl.pallas_call(functools.partial(front_kernel, len(sources), find), in_sp...]
    unnamed x36 -> x29, local copies, waits for them, and re-layouts: 9.8 us -> 0.76 us
    ppermute x44 -> x31, waiting for transfers between devices: 29.3 us -> 37.1 us  [swap(): return lax.ppermute(array, axis, [(i, i ^ mask) for i in range(size)])]
    select_n x8, other arithmetic: 2.57 us -> 8.27 us  [choose(): jnp.where(self.owner, self.own[q], a)]
  transfers between devices with their start and end apart: 44 -> 31, of which waited for: 11 -> 14; matrix products, arithmetic and copies ran while one was open for 3% -> 8% of each run, Pallas kernels for 36% -> 36%
where the time goes in v2:
time: 143 us; the launch traced here: 142 us
  Pallas kernels  56.8 us (40%)
  waiting for transfers between devices  37.1 us (26%)
  starting transfers between devices  29.5 us (21%)
  other arithmetic  11.7 us (8%)
  between operations  5.58 us (4%)
    ppermute x31, waiting for transfers between devices, swap(): return lax.ppermute(array, axis, [(i, i ^ mask) for i in range(size)])  37.1 us
    pallas_call x4, Pallas kernels, front(): pl.pallas_call(functools.partial(front_kernel, len(sources), find), in_sp...  35.3 us
    ppermute x31, starting transfers between devices, swap(): return lax.ppermute(array, axis, [(i, i ^ mask) for i in range(size)])  29.5 us
    pallas_call x3, Pallas kernels, planes(): pl.pallas_call(functools.partial(planes_kernel, firsts), grid_spec=spec,...  12.7 us
    select_n x8, other arithmetic, choose(): jnp.where(self.owner, self.own[q], a)  8.27 us
    pallas_call x1, Pallas kernels, screen(): pl.pallas_call(functools.partial(screen_kernel, [len(p) for p in parts]),...  6.09 us
  transfers between devices with their start and end apart: 31, of which 14 were waited for; matrix products, arithmetic and copies ran while one was open for 8% of the time, Pallas kernels for 36%

profile of v2, /device:TPU:0, one launch (start us, length us, event | category | flops | bytes accessed | tf_op | source)
XLA Modules:
  0.0 142.2 jit_solution(14955597387469115706)
XLA Ops:
  0.0 5.0 %planes.4 = (bf16[2,3,96,384]{3,2,1,0:T(8,128)(2,1)}, bf16[2,3,96,384]{3,2,1,0:T(8,128)(2,1)}) custom-call(s32[2]{0:T(128)} %blocks.11, bf16[12,16,9216]{2,1,0:T(8,128)(2,1)} %bitcast.8), custom_call_target="tpu_custom_call" | custom-call | bytes 7077888 | tf_op jit(solution)/shard_map/planes/pallas_call | solution.py:121
  5.0 3.0 %collective-permute-start = (bf16[2,3,96,384]{3,2,1,0:T(8,128)(2,1)}, bf16[2,3,96,384]{3,2,1,0:T(8,128)(2,1)}, u32[]{:S(2)}, u32[]{:S(2)}) collective-permute-start(bf16[2,3,96,384]{3,2,1,0:T(8,128)(2,1)} %get-tuple-element.39.refs_0_), channel_id=1, source_target_pairs={{0,8},{8,0},{16,24},{24,16},{1,9},{9,1},{17,25},{25,17},{2,10},{10... | collective-permute-start | bytes 1327112 | tf_op jit(solution)/shard_map/ppermute | solution.py:408
  8.0 1.5 %collective-permute-start.2 = (bf16[2,3,96,384]{3,2,1,0:T(8,128)(2,1)}, bf16[2,3,96,384]{3,2,1,0:T(8,128)(2,1)}, u32[]{:S(2)}, u32[]{:S(2)}) collective-permute-start(bf16[2,3,96,384]{3,2,1,0:T(8,128)(2,1)} %get-tuple-element.41.refs_1_), channel_id=1, source_target_pairs={{0,16},{8,24},{16,0},{24,8},{1,17},{9,25},{17,1},{25,9},{2,18},{10... | collective-permute-start | bytes 1327112 | tf_op jit(solution)/shard_map/ppermute | solution.py:408
  9.5 5.5 %planes.3 = (bf16[2,3,96,384]{3,2,1,0:T(8,128)(2,1)}, bf16[2,3,96,384]{3,2,1,0:T(8,128)(2,1)}, bf16[2,3,96,384]{3,2,1,0:T(8,128)(2,1)S(1)}, bf16[2,3,96,384]{3,2...) custom-call(s32[2]{0:T(128)S(1)} %copy-done.3, ...), custom_call_target="tpu_custom_call" | custom-call | bytes 7077888 | tf_op jit(solution)/shard_map/planes/pallas_call | solution.py:121
  18.5 1.9 %broadcast_select_fusion.7 = bf16[2,3,96,384]{3,2,1,0:T(8,128)(2,1)} fusion(bf16[2,3,96,384]{3,2,1,0:T(8,128)(2,1)S(1)} %get-tuple-element.38.refs_1_, bf16[2,3,96,384]{3,2,1,0:T(8,128)(2,1)} %collective-permute-done.refs_2_, pred[]{:T(512)S(6)} %eq.6), kind=kLoop, calls=%fused_computation.9 | loop fusion | flops 221184 | bytes 1327105 | tf_op jit(solution)/shard_map/jit(_where)/select_n | solution.py:491
  20.4 1.8 %collective-permute-start.1 = (bf16[2,3,96,384]{3,2,1,0:T(8,128)(2,1)}, bf16[2,3,96,384]{3,2,1,0:T(8,128)(2,1)}, u32[]{:S(2)}, u32[]{:S(2)}) collective-permute-start(bf16[2,3,96,384]{3,2,1,0:T(8,128)(2,1)} %broadcast_select_fusion.7), channel_id=1, source_target_pairs={{0,16},{8,24},{16,0},{24,8},{1,17},{9,25},{17,1},{25,9},{2,18},{10... | collective-permute-start | bytes 1327112 | tf_op jit(solution)/shard_map/ppermute | solution.py:408
  22.1 1.9 %broadcast_select_fusion.5 = bf16[2,3,96,384]{3,2,1,0:T(8,128)(2,1)} fusion(bf16[2,3,96,384]{3,2,1,0:T(8,128)(2,1)S(1)} %get-tuple-element.40.refs_0_, bf16[2,3,96,384]{3,2,1,0:T(8,128)(2,1)} %collective-permute-done.2.refs_3_, pred[]{:T(512)S(6)} %eq.6), kind=kLoop, calls=%fused_computation.7 | loop fusion | flops 221184 | bytes 1327105 | tf_op jit(solution)/shard_map/jit(_where)/select_n | solution.py:491
  25.2 1.6 %collective-permute-start.5 = (s32[2,768]{1,0:T(2,128)S(1)}, s32[2,768]{1,0:T(2,128)S(1)}, u32[]{:S(2)}, u32[]{:S(2)}) collective-permute-start(s32[2,768]{1,0:T(2,128)S(1)} %pad_add_fusion.1), channel_id=1, source_target_pairs={{0,2},{1,3},{2,0},{3,1},{4,6},{5,7},{6,4},{7,5},{8,10},{9,11},{10,... | collective-permute-start | bytes 18440 | tf_op jit(solution)/shard_map/ppermute | solution.py:408
  26.8 2.0 %collective-permute-done.5 = s32[2,768]{1,0:T(2,128)S(1)} collective-permute-done((s32[2,768]{1,0:T(2,128)S(1)}, s32[2,768]{1,0:T(2,128)S(1)}, u32[]{:S(2)}, u32[]{:S(2)}) %collective-permute-start.5) | collective-permute-done | bytes 6176 | tf_op jit(solution)/shard_map/ppermute | solution.py:408
  29.6 2.7 %collective-permute-start.6 = (s32[4,768]{1,0:T(4,128)S(1)}, s32[4,768]{1,0:T(4,128)}, u32[]{:S(2)}, u32[]{:S(2)}) collective-permute-start(s32[4,768]{1,0:T(4,128)S(1)} %pad_add_fusion.refs_0_), channel_id=1, source_target_pairs={{0,4},{1,5},{2,6},{3,7},{4,0},{5,1},{6,2},{7,3},{8,12},{9,13},{10,... | collective-permute-start | bytes 36872 | tf_op jit(solution)/shard_map/ppermute | solution.py:408
  36.2 2.2 %planes.5.refs_6_.refs_4_ = bf16[8,3,96,384]{3,2,1,0:T(8,128)(2,1)S(1)} custom-call(s32[2]{0:T(128)S(1)} %copy-done.3, bf16[12,8,9216]{2,1,0:T(8,128)(2,1)S(1)} %bitcast.10), custom_call_target="tpu_custom_call" | custom-call | bytes 3538944 | tf_op jit(solution)/shard_map/planes/pallas_call | solution.py:121
  38.5 1.7 %tables.1 = (bf16[8,128,768]{2,1,0:T(8,128)(2,1)S(1)}, f32[8,16,768]{2,1,0:T(8,128)S(1)}) custom-call(s32[4,768]{1,0:T(4,128)S(1)} %pad_add_fusion.refs_0_, s32[4,768]{1,0:T(4,128)} %collective-permute-done.6.refs_1_, bf16[8,2,16,32]{3,2,1,0:T(8,128)(2,1)S(1)} %copy-done.2), custom_call_target="tpu_custom_call" | custom-call | bytes 2359296 | tf_op jit(solution)/shard_map/tables/pallas_call | solution.py:149
  41.3 1.2 collective-permute-start.8
  44.2 8.6 %front.4 = (bf16[4,64,768]{2,1,0:T(8,128)(2,1)S(1)}, bf16[4,64,768]{2,1,0:T(8,128)(2,1)S(1)}) custom-call(s32[2]{0:T(128)S(1)} %copy-done.3, s32[16]{0:T(128)S(1)} %copy-done.9, bf16[2,3,96,384]{3,2,1,0:T(8,128)(2,1)S(1)} %copy-done.5, bf16[2,3,96,384]{3,2,1,0:T(8,128)(2,1)S(1)} %copy-done.6, bf16[2,3,96,384]{3,2,1,0:T(8,128)(2,1)} %collective-permute-done.refs_2_, ...), custom_call_target="tpu_custom_call" | custom-call | flops 3600000000 | bytes 8000000 | tf_op jit(solution)/shard_map/front/pallas_call | solution.py:279
  55.7 2.2 %collective-permute-start.14 = (bf16[2,3,96,384]{3,2,1,0:T(8,128)(2,1)S(1)}, bf16[2,3,96,384]{3,2,1,0:T(8,128)(2,1)S(1)}, u32[]{:S(2)}, u32[]{:S(2)}) collective-permute-start(bf16[2,3,96,384]{3,2,1,0:T(8,128)(2,1)S(1)} %broadcast_select_fusion.1), channel_id=1, source_target_pairs={{0,8},{8,0},{16,24},{24,16},{1,9},{9,1},{17,25},{25,17},{2,10},{10... | collective-permute-start | bytes 1327112 | tf_op jit(solution)/shard_map/ppermute | solution.py:408
  58.1 1.6 %collective-permute-start.15 = (bf16[2,64,768]{2,1,0:T(8,128)(2,1)S(1)}, bf16[2,64,768]{2,1,0:T(8,128)(2,1)S(1)}, u32[]{:S(2)}, u32[]{:S(2)}) collective-permute-start(bf16[2,64,768]{2,1,0:T(8,128)(2,1)S(1)} %get-tuple-element.77), channel_id=1, source_target_pairs={{0,2},{1,3},{2,0},{3,1},{4,6},{5,7},{6,4},{7,5},{8,10},{9,11},{10,... | collective-permute-start | bytes 589832 | tf_op jit(solution)/shard_map/ppermute | solution.py:408
  59.7 9.1 %front.5 = (bf16[4,64,768]{2,1,0:T(8,128)(2,1)S(1)}, bf16[4,64,768]{2,1,0:T(8,128)(2,1)S(1)}) custom-call(s32[2]{0:T(128)S(1)} %copy-done.3, s32[16]{0:T(128)S(1)} %copy-done.9, bf16[2,3,96,384]{3,2,1,0:T(8,128)(2,1)S(1)} %get-tuple-element.40.refs_0_, bf16[2,3,96,384]{3,2,1,0:T(8,128)(2,1)S(1)} %get-tuple-element.38.refs_1_, ...), custom_call_target="tpu_custom_call" | custom-call | flops 3600000000 | bytes 8000000 | tf_op jit(solution)/shard_map/front/pallas_call | solution.py:279
  71.4 8.6 %front.6 = (bf16[4,64,768]{2,1,0:T(8,128)(2,1)S(1)}, bf16[4,64,768]{2,1,0:T(8,128)(2,1)S(1)}) custom-call(s32[2]{0:T(128)S(1)} %copy-done.3, s32[16]{0:T(128)S(1)} %copy-done.9, bf16[2,3,96,384]{3,2,1,0:T(8,128)(2,1)} %get-tuple-element.53.refs_0_, bf16[2,3,96,384]{3,2,1,0:T(8,128)(2,1)} %get-tuple-element.54.refs_1_, ...), custom_call_target="tpu_custom_call" | custom-call | flops 3600000000 | bytes 8000000 | tf_op jit(solution)/shard_map/front/pallas_call | solution.py:279
  81.8 8.9 %front.7 = (bf16[4,64,768]{2,1,0:T(8,128)(2,1)S(1)}, bf16[4,64,768]{2,1,0:T(8,128)(2,1)S(1)}) custom-call(s32[2]{0:T(128)S(1)} %copy-done.3, s32[16]{0:T(128)S(1)} %copy-done.9, bf16[2,3,96,384]{3,2,1,0:T(8,128)(2,1)S(1)} %get-tuple-element.56.refs_0_, bf16[2,3,96,384]{3,2,1,0:T(8,128)(2,1)S(1)} %get-tuple-element.52.refs_1_, ...), custom_call_target="tpu_custom_call" | custom-call | flops 3600000000 | bytes 8000000 | tf_op jit(solution)/shard_map/front/pallas_call | solution.py:279
  90.7 2.6 %collective-permute-done.19 = bf16[1,128,768]{2,1,0:T(8,128)(2,1)S(1)} collective-permute-done((bf16[1,128,768]{2,1,0:T(8,128)(2,1)S(1)}, bf16[1,128,768]{2,1,0:T(8,128)(2,1)S(1)}, u32[]{:S(2)}, u32[]{:S(2)}) %collective-permute-start.19) | collective-permute-done | bytes 196640 | tf_op jit(solution)/shard_map/ppermute | solution.py:408
  94.0 6.1 %screen.1 = (bf16[4,128,768]{2,1,0:T(8,128)(2,1)}, bf16[4,128,768]{2,1,0:T(8,128)(2,1)}) custom-call(s32[1]{0:T(128)} %bitcast.here, bf16[128,768]{1,0:T(8,128)(2,1)} %get-tuple-element.73.refs_0_, bf16[128,768]{1,0:T(8,128)(2,1)} %bitcast.11, bf16[768,6144]{1,0:T(8,128)(2,1)} %refs_3_.1, bf16[768,6144]{1,0:T(8,128)(2,1)} %refs_3_.1), custom_call_target="tpu_custom_call" | custom-call | flops 1207959552 | bytes 9437184 | tf_op jit(solution)/shard_map/screen/pallas_call | solution.py:335
  100.8 6.7 %collective-permute-done.23 = bf16[2,64,768]{2,1,0:T(8,128)(2,1)S(1)} collective-permute-done((bf16[2,64,768]{2,1,0:T(8,128)(2,1)S(1)}, bf16[2,64,768]{2,1,0:T(8,128)(2,1)S(1)}, u32[]{:S(2)}, u32[]{:S(2)}) %collective-permute-start.23) | collective-permute-done | bytes 196640 | tf_op jit(solution)/shard_map/ppermute | solution.py:408
  107.7 1.8 %collective-permute-start.26 = (bf16[2,64,768]{2,1,0:T(8,128)(2,1)S(1)}, bf16[2,64,768]{2,1,0:T(8,128)(2,1)S(1)}, u32[]{:S(2)}, u32[]{:S(2)}) collective-permute-start(bf16[2,64,768]{2,1,0:T(8,128)(2,1)S(1)} %add_convert_fusion.3), channel_id=1, source_target_pairs={{0,2},{1,3},{2,0},{3,1},{4,6},{5,7},{6,4},{7,5},{8,10},{9,11},{10,... | collective-permute-start | bytes 589832 | tf_op jit(solution)/shard_map/ppermute | solution.py:408
  110.8 9.0 %collective-permute-done.26 = bf16[2,64,768]{2,1,0:T(8,128)(2,1)S(1)} collective-permute-done((bf16[2,64,768]{2,1,0:T(8,128)(2,1)S(1)}, bf16[2,64,768]{2,1,0:T(8,128)(2,1)S(1)}, u32[]{:S(2)}, u32[]{:S(2)}) %collective-permute-start.26) | collective-permute-done | bytes 196640 | tf_op jit(solution)/shard_map/ppermute | solution.py:408
  119.9 2.7 %collective-permute-start.27 = (bf16[2,64,768]{2,1,0:T(8,128)(2,1)S(1)}, bf16[2,64,768]{2,1,0:T(8,128)(2,1)S(1)}, u32[]{:S(2)}, u32[]{:S(2)}) collective-permute-start(bf16[2,64,768]{2,1,0:T(8,128)(2,1)S(1)} %add_convert_fusion.2.refs_4_), channel_id=1, source_target_pairs={{0,4},{1,5},{2,6},{3,7},{4,0},{5,1},{6,2},{7,3},{8,12},{9,13},{10,... | collective-permute-start | bytes 589832 | tf_op jit(solution)/shard_map/ppermute | solution.py:408
  122.6 6.3 %collective-permute-done.27 = bf16[2,64,768]{2,1,0:T(8,128)(2,1)S(1)} collective-permute-done((bf16[2,64,768]{2,1,0:T(8,128)(2,1)S(1)}, bf16[2,64,768]{2,1,0:T(8,128)(2,1)S(1)}, u32[]{:S(2)}, u32[]{:S(2)}) %collective-permute-start.27) | collective-permute-done | bytes 196640 | tf_op jit(solution)/shard_map/ppermute | solution.py:408
  128.9 2.2 %collective-permute-done.21.refs_1_ = bf16[2,128,768]{2,1,0:T(8,128)(2,1)S(1)} collective-permute-done((bf16[2,128,768]{2,1,0:T(8,128)(2,1)}, bf16[2,128,768]{2,1,0:T(8,128)(2,1)S(1)}, u32[]{:S(2)}, u32[]{:S(2)}) %collective-permute-start.21) | collective-permute-done | bytes 393248 | tf_op jit(solution)/shard_map/ppermute | solution.py:408
  132.2 1.2 collective-permute-done.28
  133.4 1.3 collective-permute-start.29
  134.7 2.3 %collective-permute-done.29 = f32[2,8,64]{2,1,0:T(8,128)S(1)} collective-permute-done((f32[2,8,64]{2,1,0:T(8,128)S(1)}, f32[2,8,64]{2,1,0:T(8,128)S(1)}, u32[]{:S(2)}, u32[]{:S(2)}) %collective-permute-start.29) | collective-permute-done | bytes 4128 | tf_op jit(solution)/shard_map/ppermute | solution.py:408
  137.1 2.2 %collective-permute-start.30 = (f32[1,8,64]{2,1,0:T(8,128)S(1)}, f32[1,8,64]{2,1,0:T(8,128)S(1)}, u32[]{:S(2)}, u32[]{:S(2)}) collective-permute-start(f32[1,8,64]{2,1,0:T(8,128)S(1)} %slice_add_fusion.2), channel_id=1, source_target_pairs={{0,4},{1,5},{2,6},{3,7},{4,0},{5,1},{6,2},{7,3},{8,12},{9,13},{10,... | collective-permute-start | bytes 6152 | tf_op jit(solution)/shard_map/ppermute | solution.py:408
  139.3 2.3 %collective-permute-done.30 = f32[1,8,64]{2,1,0:T(8,128)S(1)} collective-permute-done((f32[1,8,64]{2,1,0:T(8,128)S(1)}, f32[1,8,64]{2,1,0:T(8,128)S(1)}, u32[]{:S(2)}, u32[]{:S(2)}) %collective-permute-start.30) | collective-permute-done | bytes 2080 | tf_op jit(solution)/shard_map/ppermute | solution.py:408
  (95 shorter events, 18.6 us)
Async XLA Ops:
  5.0 13.5 %collective-permute-start = (bf16[2,3,96,384]{3,2,1,0:T(8,128)(2,1)}, bf16[2,3,96,384]{3,2,1,0:T(8,128)(2,1)}, u32[]{:S(2)}, u32[]{:S(2)}) collective-permute-start(bf16[2,3,96,384]{3,2,1,0:T(8,128)(2,1)} %get-tuple-element.39.refs_0_), channel_id=1, source_target_pairs={{0,8},{8,0},{16,24},{24,16},{1,9},{9,1},{17,25},{25,17},{2,10},{10... | collective-permute-start | bytes 1327112 | tf_op jit(solution)/shard_map/ppermute | solution.py:408
  8.0 14.1 %collective-permute-start.2 = (bf16[2,3,96,384]{3,2,1,0:T(8,128)(2,1)}, bf16[2,3,96,384]{3,2,1,0:T(8,128)(2,1)}, u32[]{:S(2)}, u32[]{:S(2)}) collective-permute-start(bf16[2,3,96,384]{3,2,1,0:T(8,128)(2,1)} %get-tuple-element.41.refs_1_), channel_id=1, source_target_pairs={{0,16},{8,24},{16,0},{24,8},{1,17},{9,25},{17,1},{25,9},{2,18},{10... | collective-permute-start | bytes 1327112 | tf_op jit(solution)/shard_map/ppermute | solution.py:408
  20.4 19.8 %collective-permute-start.1 = (bf16[2,3,96,384]{3,2,1,0:T(8,128)(2,1)}, bf16[2,3,96,384]{3,2,1,0:T(8,128)(2,1)}, u32[]{:S(2)}, u32[]{:S(2)}) collective-permute-start(bf16[2,3,96,384]{3,2,1,0:T(8,128)(2,1)} %broadcast_select_fusion.7), channel_id=1, source_target_pairs={{0,16},{8,24},{16,0},{24,8},{1,17},{9,25},{17,1},{25,9},{2,18},{10... | collective-permute-start | bytes 1327112 | tf_op jit(solution)/shard_map/ppermute | solution.py:408
  24.0 1.2 collective-permute-start.4
  24.0 18.5 %collective-permute-start.3 = (bf16[2,3,96,384]{3,2,1,0:T(8,128)(2,1)}, bf16[2,3,96,384]{3,2,1,0:T(8,128)(2,1)}, u32[]{:S(2)}, u32[]{:S(2)}) collective-permute-start(bf16[2,3,96,384]{3,2,1,0:T(8,128)(2,1)} %broadcast_select_fusion.5), channel_id=1, source_target_pairs={{0,8},{8,0},{16,24},{24,16},{1,9},{9,1},{17,25},{25,17},{2,10},{10... | collective-permute-start | bytes 1327112 | tf_op jit(solution)/shard_map/ppermute | solution.py:408
  25.2 3.7 %collective-permute-start.5 = (s32[2,768]{1,0:T(2,128)S(1)}, s32[2,768]{1,0:T(2,128)S(1)}, u32[]{:S(2)}, u32[]{:S(2)}) collective-permute-start(s32[2,768]{1,0:T(2,128)S(1)} %pad_add_fusion.1), channel_id=1, source_target_pairs={{0,2},{1,3},{2,0},{3,1},{4,6},{5,7},{6,4},{7,5},{8,10},{9,11},{10,... | collective-permute-start | bytes 18440 | tf_op jit(solution)/shard_map/ppermute | solution.py:408
  29.6 8.9 %collective-permute-start.6 = (s32[4,768]{1,0:T(4,128)S(1)}, s32[4,768]{1,0:T(4,128)}, u32[]{:S(2)}, u32[]{:S(2)}) collective-permute-start(s32[4,768]{1,0:T(4,128)S(1)} %pad_add_fusion.refs_0_), channel_id=1, source_target_pairs={{0,4},{1,5},{2,6},{3,7},{4,0},{5,1},{6,2},{7,3},{8,12},{9,13},{10,... | collective-permute-start | bytes 36872 | tf_op jit(solution)/shard_map/ppermute | solution.py:408
  32.2 20.7 %collective-permute-start.11 = (bf16[2,3,96,384]{3,2,1,0:T(8,128)(2,1)}, bf16[2,3,96,384]{3,2,1,0:T(8,128)(2,1)}, u32[]{:S(2)}, u32[]{:S(2)}) collective-permute-start(bf16[2,3,96,384]{3,2,1,0:T(8,128)(2,1)} %get-tuple-element.53.refs_0_), channel_id=1, source_target_pairs={{0,8},{8,0},{16,24},{24,16},{1,9},{9,1},{17,25},{25,17},{2,10},{10... | collective-permute-start | bytes 1327112 | tf_op jit(solution)/shard_map/ppermute | solution.py:408
  33.1 19.8 %collective-permute-start.12 = (bf16[2,3,96,384]{3,2,1,0:T(8,128)(2,1)}, bf16[2,3,96,384]{3,2,1,0:T(8,128)(2,1)}, u32[]{:S(2)}, u32[]{:S(2)}) collective-permute-start(bf16[2,3,96,384]{3,2,1,0:T(8,128)(2,1)} %get-tuple-element.54.refs_1_), channel_id=1, source_target_pairs={{0,16},{8,24},{16,0},{24,8},{1,17},{9,25},{17,1},{25,9},{2,18},{10... | collective-permute-start | bytes 1327112 | tf_op jit(solution)/shard_map/ppermute | solution.py:408
  41.3 18.4 %collective-permute-start.8 = (bf16[2,3,96,384]{3,2,1,0:T(8,128)(2,1)S(1)}, bf16[2,3,96,384]{3,2,1,0:T(8,128)(2,1)S(1)}, u32[]{:S(2)}, u32[]{:S(2)}) collective-permute-start(bf16[2,3,96,384]{3,2,1,0:T(8,128)(2,1)S(1)} %broadcast_select_fusion.6), channel_id=1, source_target_pairs={{0,8},{8,0},{16,24},{24,16},{1,9},{9,1},{17,25},{25,17},{2,10},{10... | collective-permute-start | bytes 1327112 | tf_op jit(solution)/shard_map/ppermute | solution.py:408
  43.6 16.1 %collective-permute-start.9 = (bf16[2,3,96,384]{3,2,1,0:T(8,128)(2,1)S(1)}, bf16[2,3,96,384]{3,2,1,0:T(8,128)(2,1)S(1)}, u32[]{:S(2)}, u32[]{:S(2)}) collective-permute-start(bf16[2,3,96,384]{3,2,1,0:T(8,128)(2,1)S(1)} %broadcast_select_fusion.4), channel_id=1, source_target_pairs={{0,16},{8,24},{16,0},{24,8},{1,17},{9,25},{17,1},{25,9},{2,18},{10... | collective-permute-start | bytes 1327112 | tf_op jit(solution)/shard_map/ppermute | solution.py:408
  52.8 5.1 %collective-permute-start.7 = (bf16[4,64,768]{2,1,0:T(8,128)(2,1)S(1)}, bf16[4,64,768]{2,1,0:T(8,128)(2,1)S(1)}, u32[]{:S(2)}, u32[]{:S(2)}) collective-permute-start(bf16[4,64,768]{2,1,0:T(8,128)(2,1)S(1)} %get-tuple-element.48), channel_id=1, source_target_pairs={{0,1},{1,0},{2,3},{3,2},{4,5},{5,4},{6,7},{7,6},{8,9},{9,8},{10,11... | collective-permute-start | bytes 1179656 | tf_op jit(solution)/shard_map/ppermute | solution.py:408
  54.1 14.9 %collective-permute-start.13 = (bf16[2,3,96,384]{3,2,1,0:T(8,128)(2,1)S(1)}, bf16[2,3,96,384]{3,2,1,0:T(8,128)(2,1)S(1)}, u32[]{:S(2)}, u32[]{:S(2)}) collective-permute-start(bf16[2,3,96,384]{3,2,1,0:T(8,128)(2,1)S(1)} %broadcast_select_fusion.3), channel_id=1, source_target_pairs={{0,16},{8,24},{16,0},{24,8},{1,17},{9,25},{17,1},{25,9},{2,18},{10... | collective-permute-start | bytes 1327112 | tf_op jit(solution)/shard_map/ppermute | solution.py:408
  55.7 13.4 %collective-permute-start.14 = (bf16[2,3,96,384]{3,2,1,0:T(8,128)(2,1)S(1)}, bf16[2,3,96,384]{3,2,1,0:T(8,128)(2,1)S(1)}, u32[]{:S(2)}, u32[]{:S(2)}) collective-permute-start(bf16[2,3,96,384]{3,2,1,0:T(8,128)(2,1)S(1)} %broadcast_select_fusion.1), channel_id=1, source_target_pairs={{0,8},{8,0},{16,24},{24,16},{1,9},{9,1},{17,25},{25,17},{2,10},{10... | collective-permute-start | bytes 1327112 | tf_op jit(solution)/shard_map/ppermute | solution.py:408
  58.1 11.5 %collective-permute-start.15 = (bf16[2,64,768]{2,1,0:T(8,128)(2,1)S(1)}, bf16[2,64,768]{2,1,0:T(8,128)(2,1)S(1)}, u32[]{:S(2)}, u32[]{:S(2)}) collective-permute-start(bf16[2,64,768]{2,1,0:T(8,128)(2,1)S(1)} %get-tuple-element.77), channel_id=1, source_target_pairs={{0,2},{1,3},{2,0},{3,1},{4,6},{5,7},{6,4},{7,5},{8,10},{9,11},{10,... | collective-permute-start | bytes 589832 | tf_op jit(solution)/shard_map/ppermute | solution.py:408
  68.8 1.8 %collective-permute-start.10 = (bf16[4,64,768]{2,1,0:T(8,128)(2,1)S(1)}, bf16[4,64,768]{2,1,0:T(8,128)(2,1)S(1)}, u32[]{:S(2)}, u32[]{:S(2)}) collective-permute-start(bf16[4,64,768]{2,1,0:T(8,128)(2,1)S(1)} %get-tuple-element.51), channel_id=1, source_target_pairs={{0,1},{1,0},{2,3},{3,2},{4,5},{5,4},{6,7},{7,6},{8,9},{9,8},{10,11... | collective-permute-start | bytes 1179656 | tf_op jit(solution)/shard_map/ppermute | solution.py:408
  69.0 12.6 %collective-permute-start.17 = (bf16[2,3,96,384]{3,2,1,0:T(8,128)(2,1)S(1)}, bf16[2,3,96,384]{3,2,1,0:T(8,128)(2,1)S(1)}, u32[]{:S(2)}, u32[]{:S(2)}) collective-permute-start(bf16[2,3,96,384]{3,2,1,0:T(8,128)(2,1)S(1)} %broadcast_select_fusion.2), channel_id=1, source_target_pairs={{0,8},{8,0},{16,24},{24,16},{1,9},{9,1},{17,25},{25,17},{2,10},{10... | collective-permute-start | bytes 1327112 | tf_op jit(solution)/shard_map/ppermute | solution.py:408
  69.2 12.6 %collective-permute-start.18 = (bf16[2,3,96,384]{3,2,1,0:T(8,128)(2,1)S(1)}, bf16[2,3,96,384]{3,2,1,0:T(8,128)(2,1)S(1)}, u32[]{:S(2)}, u32[]{:S(2)}) collective-permute-start(bf16[2,3,96,384]{3,2,1,0:T(8,128)(2,1)S(1)} %broadcast_select_fusion), channel_id=1, source_target_pairs={{0,16},{8,24},{16,0},{24,8},{1,17},{9,25},{17,1},{25,9},{2,18},{10... | collective-permute-start | bytes 1327112 | tf_op jit(solution)/shard_map/ppermute | solution.py:408
  70.7 9.3 %collective-permute-start.16 = (bf16[2,64,768]{2,1,0:T(8,128)(2,1)S(1)}, bf16[2,64,768]{2,1,0:T(8,128)(2,1)S(1)}, u32[]{:S(2)}, u32[]{:S(2)}) collective-permute-start(bf16[2,64,768]{2,1,0:T(8,128)(2,1)S(1)} %get-tuple-element.76), channel_id=1, source_target_pairs={{0,2},{1,3},{2,0},{3,1},{4,6},{5,7},{6,4},{7,5},{8,10},{9,11},{10,... | collective-permute-start | bytes 589832 | tf_op jit(solution)/shard_map/ppermute | solution.py:408
  80.0 20.1 %collective-permute-start.22 = (bf16[4,64,768]{2,1,0:T(8,128)(2,1)S(1)}, bf16[4,64,768]{2,1,0:T(8,128)(2,1)S(1)}, u32[]{:S(2)}, u32[]{:S(2)}) collective-permute-start(bf16[4,64,768]{2,1,0:T(8,128)(2,1)S(1)} %get-tuple-element.66), channel_id=1, source_target_pairs={{0,1},{1,0},{2,3},{3,2},{4,5},{5,4},{6,7},{7,6},{8,9},{9,8},{10,11... | collective-permute-start | bytes 1179656 | tf_op jit(solution)/shard_map/ppermute | solution.py:408
  80.9 12.4 %collective-permute-start.19 = (bf16[1,128,768]{2,1,0:T(8,128)(2,1)S(1)}, bf16[1,128,768]{2,1,0:T(8,128)(2,1)S(1)}, u32[]{:S(2)}, u32[]{:S(2)}) collective-permute-start(bf16[1,128,768]{2,1,0:T(8,128)(2,1)S(1)} %get-tuple-element.74), channel_id=1, source_target_pairs={{0,4},{1,5},{2,6},{3,7},{4,0},{5,1},{6,2},{7,3},{8,12},{9,13},{10,... | collective-permute-start | bytes 589832 | tf_op jit(solution)/shard_map/ppermute | solution.py:408
  100.0 9.5 %collective-permute-start.20 = (bf16[4,128,768]{2,1,0:T(8,128)(2,1)}, bf16[4,128,768]{2,1,0:T(8,128)(2,1)S(1)}, u32[]{:S(2)}, u32[]{:S(2)}) collective-permute-start(bf16[4,128,768]{2,1,0:T(8,128)(2,1)} %get-tuple-element.65), channel_id=1, source_target_pairs={{0,1},{1,0},{2,3},{3,2},{4,5},{5,4},{6,7},{7,6},{8,9},{9,8},{10,11... | collective-permute-start | bytes 2359304 | tf_op jit(solution)/shard_map/ppermute | solution.py:408
  100.1 7.4 %collective-permute-start.23 = (bf16[2,64,768]{2,1,0:T(8,128)(2,1)S(1)}, bf16[2,64,768]{2,1,0:T(8,128)(2,1)S(1)}, u32[]{:S(2)}, u32[]{:S(2)}) collective-permute-start(bf16[2,64,768]{2,1,0:T(8,128)(2,1)S(1)} %add_convert_fusion.6), channel_id=1, source_target_pairs={{0,2},{1,3},{2,0},{3,1},{4,6},{5,7},{6,4},{7,5},{8,10},{9,11},{10,... | collective-permute-start | bytes 589832 | tf_op jit(solution)/shard_map/ppermute | solution.py:408
  100.2 7.5 %collective-permute-start.25 = (bf16[4,64,768]{2,1,0:T(8,128)(2,1)S(1)}, bf16[4,64,768]{2,1,0:T(8,128)(2,1)S(1)}, u32[]{:S(2)}, u32[]{:S(2)}) collective-permute-start(bf16[4,64,768]{2,1,0:T(8,128)(2,1)S(1)} %get-tuple-element.68), channel_id=1, source_target_pairs={{0,1},{1,0},{2,3},{3,2},{4,5},{5,4},{6,7},{7,6},{8,9},{9,8},{10,11... | collective-permute-start | bytes 1179656 | tf_op jit(solution)/shard_map/ppermute | solution.py:408
  107.6 15.0 %collective-permute-start.24 = (bf16[2,64,768]{2,1,0:T(8,128)(2,1)S(1)}, bf16[2,64,768]{2,1,0:T(8,128)(2,1)S(1)}, u32[]{:S(2)}, u32[]{:S(2)}) collective-permute-start(bf16[2,64,768]{2,1,0:T(8,128)(2,1)S(1)} %add_convert_fusion.5.refs_2_), channel_id=1, source_target_pairs={{0,4},{1,5},{2,6},{3,7},{4,0},{5,1},{6,2},{7,3},{8,12},{9,13},{10,... | collective-permute-start | bytes 589832 | tf_op jit(solution)/shard_map/ppermute | solution.py:408
  107.7 23.4 %copy-start.4 = (s32[32]{0:T(128)S(1)}, s32[32]{0:T(128)}, u32[]{:S(2)}) copy-start(s32[32]{0:T(128)} %constant.43.clone.slot_of) | copy-start | bytes 388
  107.7 12.0 %collective-permute-start.26 = (bf16[2,64,768]{2,1,0:T(8,128)(2,1)S(1)}, bf16[2,64,768]{2,1,0:T(8,128)(2,1)S(1)}, u32[]{:S(2)}, u32[]{:S(2)}) collective-permute-start(bf16[2,64,768]{2,1,0:T(8,128)(2,1)S(1)} %add_convert_fusion.3), channel_id=1, source_target_pairs={{0,2},{1,3},{2,0},{3,1},{4,6},{5,7},{6,4},{7,5},{8,10},{9,11},{10,... | collective-permute-start | bytes 589832 | tf_op jit(solution)/shard_map/ppermute | solution.py:408
  110.5 20.7 %collective-permute-start.21 = (bf16[2,128,768]{2,1,0:T(8,128)(2,1)}, bf16[2,128,768]{2,1,0:T(8,128)(2,1)S(1)}, u32[]{:S(2)}, u32[]{:S(2)}) collective-permute-start(bf16[2,128,768]{2,1,0:T(8,128)(2,1)} %get-tuple-element.71), channel_id=1, source_target_pairs={{0,2},{1,3},{2,0},{3,1},{4,6},{5,7},{6,4},{7,5},{8,10},{9,11},{10,... | collective-permute-start | bytes 1179656 | tf_op jit(solution)/shard_map/ppermute | solution.py:408
  119.9 9.0 %collective-permute-start.27 = (bf16[2,64,768]{2,1,0:T(8,128)(2,1)S(1)}, bf16[2,64,768]{2,1,0:T(8,128)(2,1)S(1)}, u32[]{:S(2)}, u32[]{:S(2)}) collective-permute-start(bf16[2,64,768]{2,1,0:T(8,128)(2,1)S(1)} %add_convert_fusion.2.refs_4_), channel_id=1, source_target_pairs={{0,4},{1,5},{2,6},{3,7},{4,0},{5,1},{6,2},{7,3},{8,12},{9,13},{10,... | collective-permute-start | bytes 589832 | tf_op jit(solution)/shard_map/ppermute | solution.py:408
  132.2 1.2 collective-permute-start.28
  133.4 3.7 %collective-permute-start.29 = (f32[2,8,64]{2,1,0:T(8,128)S(1)}, f32[2,8,64]{2,1,0:T(8,128)S(1)}, u32[]{:S(2)}, u32[]{:S(2)}) collective-permute-start(f32[2,8,64]{2,1,0:T(8,128)S(1)} %get-tuple-element.80), channel_id=1, source_target_pairs={{0,2},{1,3},{2,0},{3,1},{4,6},{5,7},{6,4},{7,5},{8,10},{9,11},{10,... | collective-permute-start | bytes 12296 | tf_op jit(solution)/shard_map/ppermute | solution.py:408
  137.1 4.5 %collective-permute-start.30 = (f32[1,8,64]{2,1,0:T(8,128)S(1)}, f32[1,8,64]{2,1,0:T(8,128)S(1)}, u32[]{:S(2)}, u32[]{:S(2)}) collective-permute-start(f32[1,8,64]{2,1,0:T(8,128)S(1)} %slice_add_fusion.2), channel_id=1, source_target_pairs={{0,4},{1,5},{2,6},{3,7},{4,0},{5,1},{6,2},{7,3},{8,12},{9,13},{10,... | collective-permute-start | bytes 6152 | tf_op jit(solution)/shard_map/ppermute | solution.py:408
  (13 other events, 98.8 us)

commit v3 on v2

--- a/solution.py
+++ b/solution.py
@@ -293,53 +293,49 @@
     )(blocks, jnp.asarray(SOURCES.reshape(-1), jnp.int32), *sources, cond, ytab, ztab, pick, wave)
 
 
-def screen_kernel(split, here, *refs):
-    *pieces, w_even, w_odd, even, odd, side = refs
-
-    @pl.when(pl.program_id(0) == 0)
-    def _():
-        first = 0
-        for i, count in enumerate(split):
-            group = pieces[sum(split[:i]):sum(split[:i]) + count]
-            total = group[0][...].astype(F32)
-            for piece in group[1:]:
-                total = total + piece[...].astype(F32)
-            side[first:first + total.shape[0], :] = total.astype(BF16)
-            first += total.shape[0]
-
-    even[0] = jnp.dot(side[...], w_even[...], preferred_element_type=F32).astype(BF16)
-    odd[0] = jnp.dot(side[...], w_odd[...], preferred_element_type=F32).astype(BF16)
-
-
-def screen(here, parts, screened, targets):
+def screen_kernel(split, parity, *refs):
+    *pieces, screened, out = refs
+    sums = []
+    for i, count in enumerate(split):
+        group = pieces[sum(split[:i]):sum(split[:i]) + count]
+        total = group[0][...].astype(F32)
+        for piece in group[1:]:
+            total = total + piece[...].astype(F32)
+        sums.append(total.astype(BF16))
+    side = jnp.concatenate(sums, axis=0)
+    steps, _, own = out.shape
+    here = lax.axis_index("grid").astype(jnp.int32)
+
+    def step(r, carry):
+        target = here ^ target_of(r, 2 * steps) ^ parity
+        columns = screened[:, pl.ds(pl.multiple_of(target * own, own), own)]
+        out[r] = jnp.dot(side, columns, preferred_element_type=F32).astype(BF16)
+        return carry
+
+    lax.fori_loop(0, steps, step, 0)
+
+
+def screen(parts, screened, targets, parity):
     own = parts[0][0].shape[1]
     rows = sum(p[0].shape[0] for p in parts)
     flat = [piece for part in parts for piece in part]
     if own % 128:
+        here = lax.axis_index("grid").astype(jnp.int32)
         side = jnp.concatenate([sum(p.astype(F32) for p in part) for part in parts], axis=0).astype(BF16)
         part = jnp.dot(side, screened, preferred_element_type=F32).astype(BF16)
         part = jnp.transpose(part.reshape(rows, targets, own), (1, 0, 2))
-        even = here[0] ^ target_of(jnp.arange(targets // 2, dtype=jnp.int32), targets)
-        return jnp.take(part, even, axis=0), jnp.take(part, even ^ 1, axis=0)
-    shape = jax.ShapeDtypeStruct((targets // 2, rows, own), BF16)
-    spec = pltpu.PrefetchScalarGridSpec(
-        num_scalar_prefetch=1,
-        grid=(targets // 2,),
-        in_specs=[pl.BlockSpec(x.shape, lambda r, h: (0, 0)) for x in flat] + [
-            pl.BlockSpec((own, own), lambda r, h: (0, h[0] ^ target_of(r, targets))),
-            pl.BlockSpec((own, own), lambda r, h: (0, h[0] ^ target_of(r, targets) ^ 1)),
-        ],
-        out_specs=[pl.BlockSpec((1, rows, own), lambda r, h: (r, 0, 0))] * 2,
-        scratch_shapes=[pltpu.VMEM((rows, own), BF16)],
-    )
+        wanted = here ^ target_of(jnp.arange(targets // 2, dtype=jnp.int32), targets) ^ parity
+        return jnp.take(part, wanted, axis=0)
+    inside = pl.BlockSpec(memory_space=pltpu.VMEM)
     return pl.pallas_call(
-        functools.partial(screen_kernel, [len(p) for p in parts]),
-        grid_spec=spec,
-        out_shape=[shape, shape],
-        compiler_params=pltpu.CompilerParams(vmem_limit_bytes=WHOLE_VMEM),
-        cost_estimate=pl.CostEstimate(flops=2 * rows * own * own * targets, bytes_accessed=2 * own * own * targets, transcendentals=0),
+        functools.partial(screen_kernel, [len(p) for p in parts], parity),
+        in_specs=[inside] * (len(flat) + 1),
+        out_specs=inside,
+        out_shape=jax.ShapeDtypeStruct((targets // 2, rows, own), BF16),
+        compiler_params=pltpu.CompilerParams(vmem_limit_bytes=PART_VMEM),
+        cost_estimate=pl.CostEstimate(flops=rows * own * own * targets, bytes_accessed=own * own * targets, transcendentals=0),
         name="screen",
-    )(here, *flat, screened, screened)
+    )(*flat, screened)
 
 
 def close_kernel(split, place, blocks, slot_of, *refs):
@@ -573,8 +569,8 @@
     side_a = [after(early_a[0], early_b[0]), early_a[1]], [late_a[0], late_a[1]]
     side_a = [jnp.concatenate([e, l], axis=1) for e, l in zip(*side_a, strict=True)]
     side_a = halve(*side_a, 4, n_grid)
-    late_b = core(part(1, 1, side_a[2]))
     early_b = halve(*early_b, 2, n_grid)
+    late_b = core(part(1, 1, side_a[2], early_b[2]))
 
     def finish(pair, mask):
         pair = pair[:2]
@@ -591,10 +587,12 @@
         return pair
 
     side_a = [finish(side_a, 8)]
-    part_u = screen(after(at, late_b[0]), side_a, screened, n_grid)
-    late_b = until_two((after(late_b[0], part_u[0]), late_b[1]), 2)
-    part_u = until_two(core(part_u), 2)
-    side_b = [both_blocks(*until_two(early_b, 4), n_grid), both_blocks(*late_b, n_grid)]
+    early_b = both_blocks(*until_two(early_b, 4), n_grid)
+    odd_u = screen([[after(side_a[0][0], late_b[0], early_b[0]), *side_a[0][1:]]], screened, n_grid, 1)
+    late_b = halve(*late_b, 2, n_grid)
+    even_u = screen([[after(side_a[0][0], odd_u, late_b[2]), *side_a[0][1:]]], screened, n_grid, 0)
+    part_u = until_two(core((even_u, odd_u)), 2)
+    side_b = [early_b, both_blocks(*until_two(late_b, 4), n_grid)]
 
     by_target = n_grid == BLK
 
@@ -608,7 +606,9 @@
         share = shares[0].reshape(n_grid, -1, shares[0].shape[1])
         even = at ^ target_of(jnp.arange(n_grid // 2, dtype=jnp.int32), n_grid)
         shares = jnp.take(share, even, axis=0), jnp.take(share, even ^ 1, axis=0)
-    return sum(halving(*shares, n_grid))[None]
+    share = add(shares[0], swap(shares[1], "grid", 1, n_grid))
+    far = [swap(share[i], "grid", target_of(i, n_grid), n_grid) for i in range(1, n_grid // 2)]
+    return sum(far, share[0])[None]
 
 
 def solution(mesh):

time: 143 us -> 132 us (0.923)
  waiting for transfers between devices: 37.1 us -> 28.8 us
  Pallas kernels: 56.8 us -> 53.8 us
  starting transfers between devices: 29.5 us -> 31.6 us
    ppermute x31 -> x32, waiting for transfers between devices: 37.1 us -> 28.8 us  [swap(): return lax.ppermute(array, axis, [(i, i ^ mask) for i in range(size)])]
    pallas_call x1 -> x2, Pallas kernels: 6.09 us -> 2.79 us  [screen(): pl.pallas_call(functools.partial(screen_kernel, [len(p) for p in parts],...]
    ppermute x31 -> x32, starting transfers between devices: 29.5 us -> 31.6 us  [swap(): return lax.ppermute(array, axis, [(i, i ^ mask) for i in range(size)])]
  transfers between devices with their start and end apart: 31 -> 32, of which waited for: 14 -> 13; matrix products, arithmetic and copies ran while one was open for 8% -> 8% of each run, Pallas kernels for 36% -> 35%
where the time goes in v3:
time: 132 us; the launch traced here: 131 us
  Pallas kernels  53.8 us (41%)
  starting transfers between devices  31.6 us (24%)
  waiting for transfers between devices  28.8 us (22%)
  other arithmetic  10.3 us (8%)
  between operations  5.86 us (4%)
    pallas_call x4, Pallas kernels, front(): pl.pallas_call(functools.partial(front_kernel, len(sources), find), in_sp...  35.6 us
    ppermute x32, starting transfers between devices, swap(): return lax.ppermute(array, axis, [(i, i ^ mask) for i in range(size)])  31.6 us
    ppermute x32, waiting for transfers between devices, swap(): return lax.ppermute(array, axis, [(i, i ^ mask) for i in range(size)])  28.8 us
    pallas_call x3, Pallas kernels, planes(): pl.pallas_call(functools.partial(planes_kernel, firsts), grid_spec=spec,...  12.7 us
    select_n x8, other arithmetic, choose(): jnp.where(self.owner, self.own[q], a)  8.31 us
    pallas_call x2, Pallas kernels, screen(): pl.pallas_call(functools.partial(screen_kernel, [len(p) for p in parts],...  2.79 us
  transfers between devices with their start and end apart: 32, of which 13 were waited for; matrix products, arithmetic and copies ran while one was open for 8% of the time, Pallas kernels for 35%

profile of v3, /device:TPU:0, one launch (start us, length us, event | category | flops | bytes accessed | tf_op | source)
XLA Modules:
  0.0 131.2 jit_solution(6253613517316342163)
XLA Ops:
  0.0 5.0 %planes.4 = (bf16[2,3,96,384]{3,2,1,0:T(8,128)(2,1)}, bf16[2,3,96,384]{3,2,1,0:T(8,128)(2,1)}) custom-call(s32[2]{0:T(128)} %blocks.11, bf16[12,16,9216]{2,1,0:T(8,128)(2,1)} %bitcast.27), custom_call_target="tpu_custom_call" | custom-call | bytes 7077888 | tf_op jit(solution)/shard_map/planes/pallas_call | solution.py:121
  5.0 3.0 %collective-permute-start = (bf16[2,3,96,384]{3,2,1,0:T(8,128)(2,1)}, bf16[2,3,96,384]{3,2,1,0:T(8,128)(2,1)}, u32[]{:S(2)}, u32[]{:S(2)}) collective-permute-start(bf16[2,3,96,384]{3,2,1,0:T(8,128)(2,1)} %get-tuple-element.37.refs_0_), channel_id=1, source_target_pairs={{0,8},{8,0},{16,24},{24,16},{1,9},{9,1},{17,25},{25,17},{2,10},{10... | collective-permute-start | bytes 1327112 | tf_op jit(solution)/shard_map/ppermute | solution.py:404
  8.0 1.5 %collective-permute-start.2 = (bf16[2,3,96,384]{3,2,1,0:T(8,128)(2,1)}, bf16[2,3,96,384]{3,2,1,0:T(8,128)(2,1)}, u32[]{:S(2)}, u32[]{:S(2)}) collective-permute-start(bf16[2,3,96,384]{3,2,1,0:T(8,128)(2,1)} %get-tuple-element.39.refs_1_), channel_id=1, source_target_pairs={{0,16},{8,24},{16,0},{24,8},{1,17},{9,25},{17,1},{25,9},{2,18},{10... | collective-permute-start | bytes 1327112 | tf_op jit(solution)/shard_map/ppermute | solution.py:404
  9.5 5.5 %planes.3 = (bf16[2,3,96,384]{3,2,1,0:T(8,128)(2,1)}, bf16[2,3,96,384]{3,2,1,0:T(8,128)(2,1)}, bf16[2,3,96,384]{3,2,1,0:T(8,128)(2,1)S(1)}, bf16[2,3,96,384]{3,2...) custom-call(s32[2]{0:T(128)S(1)} %copy-done.3, ...), custom_call_target="tpu_custom_call" | custom-call | bytes 7077888 | tf_op jit(solution)/shard_map/planes/pallas_call | solution.py:121
  18.5 1.9 %broadcast_select_fusion.7 = bf16[2,3,96,384]{3,2,1,0:T(8,128)(2,1)} fusion(bf16[2,3,96,384]{3,2,1,0:T(8,128)(2,1)S(1)} %get-tuple-element.36.refs_1_, bf16[2,3,96,384]{3,2,1,0:T(8,128)(2,1)} %collective-permute-done.refs_2_, pred[]{:T(512)S(6)} %eq.6), kind=kLoop, calls=%fused_computation.9 | loop fusion | flops 221184 | bytes 1327105 | tf_op jit(solution)/shard_map/jit(_where)/select_n | solution.py:487
  20.4 1.8 %collective-permute-start.1 = (bf16[2,3,96,384]{3,2,1,0:T(8,128)(2,1)}, bf16[2,3,96,384]{3,2,1,0:T(8,128)(2,1)}, u32[]{:S(2)}, u32[]{:S(2)}) collective-permute-start(bf16[2,3,96,384]{3,2,1,0:T(8,128)(2,1)} %broadcast_select_fusion.7), channel_id=1, source_target_pairs={{0,16},{8,24},{16,0},{24,8},{1,17},{9,25},{17,1},{25,9},{2,18},{10... | collective-permute-start | bytes 1327112 | tf_op jit(solution)/shard_map/ppermute | solution.py:404
  22.1 1.9 %broadcast_select_fusion.5 = bf16[2,3,96,384]{3,2,1,0:T(8,128)(2,1)} fusion(bf16[2,3,96,384]{3,2,1,0:T(8,128)(2,1)S(1)} %get-tuple-element.38.refs_0_, bf16[2,3,96,384]{3,2,1,0:T(8,128)(2,1)} %collective-permute-done.2.refs_3_, pred[]{:T(512)S(6)} %eq.6), kind=kLoop, calls=%fused_computation.7 | loop fusion | flops 221184 | bytes 1327105 | tf_op jit(solution)/shard_map/jit(_where)/select_n | solution.py:487
  25.2 1.6 %collective-permute-start.5 = (s32[2,768]{1,0:T(2,128)S(1)}, s32[2,768]{1,0:T(2,128)S(1)}, u32[]{:S(2)}, u32[]{:S(2)}) collective-permute-start(s32[2,768]{1,0:T(2,128)S(1)} %pad_add_fusion.1), channel_id=1, source_target_pairs={{0,2},{1,3},{2,0},{3,1},{4,6},{5,7},{6,4},{7,5},{8,10},{9,11},{10,... | collective-permute-start | bytes 18440 | tf_op jit(solution)/shard_map/ppermute | solution.py:404
  26.8 2.0 %collective-permute-done.5 = s32[2,768]{1,0:T(2,128)S(1)} collective-permute-done((s32[2,768]{1,0:T(2,128)S(1)}, s32[2,768]{1,0:T(2,128)S(1)}, u32[]{:S(2)}, u32[]{:S(2)}) %collective-permute-start.5) | collective-permute-done | bytes 6176 | tf_op jit(solution)/shard_map/ppermute | solution.py:404
  29.6 2.7 %collective-permute-start.6 = (s32[4,768]{1,0:T(4,128)S(1)}, s32[4,768]{1,0:T(4,128)}, u32[]{:S(2)}, u32[]{:S(2)}) collective-permute-start(s32[4,768]{1,0:T(4,128)S(1)} %pad_add_fusion.refs_0_), channel_id=1, source_target_pairs={{0,4},{1,5},{2,6},{3,7},{4,0},{5,1},{6,2},{7,3},{8,12},{9,13},{10,... | collective-permute-start | bytes 36872 | tf_op jit(solution)/shard_map/ppermute | solution.py:404
  36.5 2.2 %planes.5.refs_6_.refs_4_ = bf16[8,3,96,384]{3,2,1,0:T(8,128)(2,1)S(1)} custom-call(s32[2]{0:T(128)S(1)} %copy-done.3, bf16[12,8,9216]{2,1,0:T(8,128)(2,1)S(1)} %bitcast.29), custom_call_target="tpu_custom_call" | custom-call | bytes 3538944 | tf_op jit(solution)/shard_map/planes/pallas_call | solution.py:121
  38.8 1.7 %tables.1 = (bf16[8,128,768]{2,1,0:T(8,128)(2,1)S(1)}, f32[8,16,768]{2,1,0:T(8,128)S(1)}) custom-call(s32[4,768]{1,0:T(4,128)S(1)} %pad_add_fusion.refs_0_, s32[4,768]{1,0:T(4,128)} %collective-permute-done.6.refs_1_, bf16[8,2,16,32]{3,2,1,0:T(8,128)(2,1)S(1)} %copy-done.2), custom_call_target="tpu_custom_call" | custom-call | bytes 2359296 | tf_op jit(solution)/shard_map/tables/pallas_call | solution.py:149
  42.8 2.6 %collective-permute-start.9 = (bf16[2,3,96,384]{3,2,1,0:T(8,128)(2,1)S(1)}, bf16[2,3,96,384]{3,2,1,0:T(8,128)(2,1)S(1)}, u32[]{:S(2)}, u32[]{:S(2)}) collective-permute-start(bf16[2,3,96,384]{3,2,1,0:T(8,128)(2,1)S(1)} %broadcast_select_fusion.4), channel_id=1, source_target_pairs={{0,16},{8,24},{16,0},{24,8},{1,17},{9,25},{17,1},{25,9},{2,18},{10... | collective-permute-start | bytes 1327112 | tf_op jit(solution)/shard_map/ppermute | solution.py:404
  45.4 8.6 %front.4 = (bf16[4,64,768]{2,1,0:T(8,128)(2,1)S(1)}, bf16[4,64,768]{2,1,0:T(8,128)(2,1)S(1)}) custom-call(s32[2]{0:T(128)S(1)} %copy-done.3, s32[16]{0:T(128)S(1)} %copy-done.9, bf16[2,3,96,384]{3,2,1,0:T(8,128)(2,1)S(1)} %copy-done.5, bf16[2,3,96,384]{3,2,1,0:T(8,128)(2,1)S(1)} %copy-done.6, bf16[2,3,96,384]{3,2,1,0:T(8,128)(2,1)} %collective-permute-done.refs_2_, ...), custom_call_target="tpu_custom_call" | custom-call | flops 3600000000 | bytes 8000000 | tf_op jit(solution)/shard_map/front/pallas_call | solution.py:279
  56.5 1.2 collective-permute-start.14
  57.8 1.7 %collective-permute-start.15 = (bf16[2,64,768]{2,1,0:T(8,128)(2,1)S(1)}, bf16[2,64,768]{2,1,0:T(8,128)(2,1)S(1)}, u32[]{:S(2)}, u32[]{:S(2)}) collective-permute-start(bf16[2,64,768]{2,1,0:T(8,128)(2,1)S(1)} %get-tuple-element.73), channel_id=1, source_target_pairs={{0,2},{1,3},{2,0},{3,1},{4,6},{5,7},{6,4},{7,5},{8,10},{9,11},{10,... | collective-permute-start | bytes 589832 | tf_op jit(solution)/shard_map/ppermute | solution.py:404
  59.4 9.1 %front.5 = (bf16[4,64,768]{2,1,0:T(8,128)(2,1)S(1)}, bf16[4,64,768]{2,1,0:T(8,128)(2,1)S(1)}) custom-call(s32[2]{0:T(128)S(1)} %copy-done.3, s32[16]{0:T(128)S(1)} %copy-done.9, bf16[2,3,96,384]{3,2,1,0:T(8,128)(2,1)S(1)} %get-tuple-element.38.refs_0_, bf16[2,3,96,384]{3,2,1,0:T(8,128)(2,1)S(1)} %get-tuple-element.36.refs_1_, ...), custom_call_target="tpu_custom_call" | custom-call | flops 3600000000 | bytes 8000000 | tf_op jit(solution)/shard_map/front/pallas_call | solution.py:279
  69.8 1.2 collective-permute-start.19
  72.1 8.9 %front.6 = (bf16[4,64,768]{2,1,0:T(8,128)(2,1)S(1)}, bf16[4,64,768]{2,1,0:T(8,128)(2,1)S(1)}) custom-call(s32[2]{0:T(128)S(1)} %copy-done.3, s32[16]{0:T(128)S(1)} %copy-done.9, bf16[2,3,96,384]{3,2,1,0:T(8,128)(2,1)} %get-tuple-element.51.refs_0_, bf16[2,3,96,384]{3,2,1,0:T(8,128)(2,1)} %get-tuple-element.52.refs_1_, ...), custom_call_target="tpu_custom_call" | custom-call | flops 3600000000 | bytes 8000000 | tf_op jit(solution)/shard_map/front/pallas_call | solution.py:279
  81.7 1.1 collective-permute-done.17
  82.9 1.1 collective-permute-start.20
  84.0 8.9 %front.7 = (bf16[4,64,768]{2,1,0:T(8,128)(2,1)S(1)}, bf16[4,64,768]{2,1,0:T(8,128)(2,1)S(1)}) custom-call(s32[2]{0:T(128)S(1)} %copy-done.3, s32[16]{0:T(128)S(1)} %copy-done.9, bf16[2,3,96,384]{3,2,1,0:T(8,128)(2,1)S(1)} %get-tuple-element.54.refs_0_, bf16[2,3,96,384]{3,2,1,0:T(8,128)(2,1)S(1)} %get-tuple-element.50.refs_1_, ...), custom_call_target="tpu_custom_call" | custom-call | flops 3600000000 | bytes 8000000 | tf_op jit(solution)/shard_map/front/pallas_call | solution.py:279
  93.8 1.4 %screen.2 = bf16[4,128,768]{2,1,0:T(8,128)(2,1)S(1)} custom-call(bf16[128,768]{1,0:T(8,128)(2,1)S(1)} %get-tuple-element.64.refs_0_, bf16[128,768]{1,0:T(8,128)(2,1)S(1)} %bitcast.30, bf16[768,6144]{1,0:T(8,128)(2,1)S(1)} %bitcast.26), custom_call_target="tpu_custom_call" | custom-call | flops 603979776 | bytes 4718592 | tf_op jit(solution)/shard_map/screen/pallas_call | solution.py:330
  95.7 1.2 collective-permute-start.25
  97.0 1.1 collective-permute-done.22
  98.5 1.4 %screen.3 = bf16[4,128,768]{2,1,0:T(8,128)(2,1)S(1)} custom-call(bf16[128,768]{1,0:T(8,128)(2,1)S(1)} %get-tuple-element.64.refs_0_, bf16[128,768]{1,0:T(8,128)(2,1)S(1)} %bitcast.31, bf16[768,6144]{1,0:T(8,128)(2,1)S(1)} %bitcast.26), custom_call_target="tpu_custom_call" | custom-call | flops 603979776 | bytes 4718592 | tf_op jit(solution)/shard_map/screen/pallas_call | solution.py:330
  100.1 1.8 %collective-permute-start.24 = (bf16[2,128,768]{2,1,0:T(8,128)(2,1)S(1)}, bf16[2,128,768]{2,1,0:T(8,128)(2,1)S(1)}, u32[]{:S(2)}, u32[]{:S(2)}) collective-permute-start(bf16[2,128,768]{2,1,0:T(8,128)(2,1)S(1)} %get-tuple-element.67), channel_id=1, source_target_pairs={{0,2},{1,3},{2,0},{3,1},{4,6},{5,7},{6,4},{7,5},{8,10},{9,11},{10,... | collective-permute-start | bytes 1179656 | tf_op jit(solution)/shard_map/ppermute | solution.py:404
  101.9 8.1 %collective-permute-done.26 = bf16[2,64,768]{2,1,0:T(8,128)(2,1)S(1)} collective-permute-done((bf16[2,64,768]{2,1,0:T(8,128)(2,1)S(1)}, bf16[2,64,768]{2,1,0:T(8,128)(2,1)S(1)}, u32[]{:S(2)}, u32[]{:S(2)}) %collective-permute-start.26) | collective-permute-done | bytes 196640 | tf_op jit(solution)/shard_map/ppermute | solution.py:404
  110.2 10.8 %collective-permute-done.27 = bf16[2,64,768]{2,1,0:T(8,128)(2,1)S(1)} collective-permute-done((bf16[2,64,768]{2,1,0:T(8,128)(2,1)S(1)}, bf16[2,64,768]{2,1,0:T(8,128)(2,1)S(1)}, u32[]{:S(2)}, u32[]{:S(2)}) %collective-permute-start.27) | collective-permute-done | bytes 196640 | tf_op jit(solution)/shard_map/ppermute | solution.py:404
  123.0 1.2 collective-permute-done.28
  124.1 1.9 %collective-permute-start.31 = (f32[8,64]{1,0:T(8,128)S(1)}, f32[8,64]{1,0:T(8,128)S(1)}, u32[]{:S(2)}, u32[]{:S(2)}) collective-permute-start(f32[8,64]{1,0:T(8,128)S(1)} %get-tuple-element.76), channel_id=1, source_target_pairs={{0,6},{1,7},{2,4},{3,5},{4,2},{5,3},{6,0},{7,1},{8,14},{9,15},{10,... | collective-permute-start | bytes 6152 | tf_op jit(solution)/shard_map/ppermute | solution.py:404
  126.1 2.5 %collective-permute-start.29 = (f32[8,64]{1,0:T(8,128)S(1)}, f32[8,64]{1,0:T(8,128)S(1)}, u32[]{:S(2)}, u32[]{:S(2)}) collective-permute-start(f32[8,64]{1,0:T(8,128)S(1)} %get-tuple-element.75), channel_id=1, source_target_pairs={{0,4},{1,5},{2,6},{3,7},{4,0},{5,1},{6,2},{7,3},{8,12},{9,13},{10,... | collective-permute-start | bytes 6152 | tf_op jit(solution)/shard_map/ppermute | solution.py:404
  (101 shorter events, 18.5 us)
Async XLA Ops:
  5.0 13.5 %collective-permute-start = (bf16[2,3,96,384]{3,2,1,0:T(8,128)(2,1)}, bf16[2,3,96,384]{3,2,1,0:T(8,128)(2,1)}, u32[]{:S(2)}, u32[]{:S(2)}) collective-permute-start(bf16[2,3,96,384]{3,2,1,0:T(8,128)(2,1)} %get-tuple-element.37.refs_0_), channel_id=1, source_target_pairs={{0,8},{8,0},{16,24},{24,16},{1,9},{9,1},{17,25},{25,17},{2,10},{10... | collective-permute-start | bytes 1327112 | tf_op jit(solution)/shard_map/ppermute | solution.py:404
  8.0 14.2 %collective-permute-start.2 = (bf16[2,3,96,384]{3,2,1,0:T(8,128)(2,1)}, bf16[2,3,96,384]{3,2,1,0:T(8,128)(2,1)}, u32[]{:S(2)}, u32[]{:S(2)}) collective-permute-start(bf16[2,3,96,384]{3,2,1,0:T(8,128)(2,1)} %get-tuple-element.39.refs_1_), channel_id=1, source_target_pairs={{0,16},{8,24},{16,0},{24,8},{1,17},{9,25},{17,1},{25,9},{2,18},{10... | collective-permute-start | bytes 1327112 | tf_op jit(solution)/shard_map/ppermute | solution.py:404
  20.4 20.1 %collective-permute-start.1 = (bf16[2,3,96,384]{3,2,1,0:T(8,128)(2,1)}, bf16[2,3,96,384]{3,2,1,0:T(8,128)(2,1)}, u32[]{:S(2)}, u32[]{:S(2)}) collective-permute-start(bf16[2,3,96,384]{3,2,1,0:T(8,128)(2,1)} %broadcast_select_fusion.7), channel_id=1, source_target_pairs={{0,16},{8,24},{16,0},{24,8},{1,17},{9,25},{17,1},{25,9},{2,18},{10... | collective-permute-start | bytes 1327112 | tf_op jit(solution)/shard_map/ppermute | solution.py:404
  24.0 1.2 collective-permute-start.4
  24.0 17.7 %collective-permute-start.3 = (bf16[2,3,96,384]{3,2,1,0:T(8,128)(2,1)}, bf16[2,3,96,384]{3,2,1,0:T(8,128)(2,1)}, u32[]{:S(2)}, u32[]{:S(2)}) collective-permute-start(bf16[2,3,96,384]{3,2,1,0:T(8,128)(2,1)} %broadcast_select_fusion.5), channel_id=1, source_target_pairs={{0,8},{8,0},{16,24},{24,16},{1,9},{9,1},{17,25},{25,17},{2,10},{10... | collective-permute-start | bytes 1327112 | tf_op jit(solution)/shard_map/ppermute | solution.py:404
  25.2 3.7 %collective-permute-start.5 = (s32[2,768]{1,0:T(2,128)S(1)}, s32[2,768]{1,0:T(2,128)S(1)}, u32[]{:S(2)}, u32[]{:S(2)}) collective-permute-start(s32[2,768]{1,0:T(2,128)S(1)} %pad_add_fusion.1), channel_id=1, source_target_pairs={{0,2},{1,3},{2,0},{3,1},{4,6},{5,7},{6,4},{7,5},{8,10},{9,11},{10,... | collective-permute-start | bytes 18440 | tf_op jit(solution)/shard_map/ppermute | solution.py:404
  29.6 9.2 %collective-permute-start.6 = (s32[4,768]{1,0:T(4,128)S(1)}, s32[4,768]{1,0:T(4,128)}, u32[]{:S(2)}, u32[]{:S(2)}) collective-permute-start(s32[4,768]{1,0:T(4,128)S(1)} %pad_add_fusion.refs_0_), channel_id=1, source_target_pairs={{0,4},{1,5},{2,6},{3,7},{4,0},{5,1},{6,2},{7,3},{8,12},{9,13},{10,... | collective-permute-start | bytes 36872 | tf_op jit(solution)/shard_map/ppermute | solution.py:404
  32.2 21.9 %collective-permute-start.11 = (bf16[2,3,96,384]{3,2,1,0:T(8,128)(2,1)}, bf16[2,3,96,384]{3,2,1,0:T(8,128)(2,1)}, u32[]{:S(2)}, u32[]{:S(2)}) collective-permute-start(bf16[2,3,96,384]{3,2,1,0:T(8,128)(2,1)} %get-tuple-element.51.refs_0_), channel_id=1, source_target_pairs={{0,8},{8,0},{16,24},{24,16},{1,9},{9,1},{17,25},{25,17},{2,10},{10... | collective-permute-start | bytes 1327112 | tf_op jit(solution)/shard_map/ppermute | solution.py:404
  33.1 21.1 %collective-permute-start.12 = (bf16[2,3,96,384]{3,2,1,0:T(8,128)(2,1)}, bf16[2,3,96,384]{3,2,1,0:T(8,128)(2,1)}, u32[]{:S(2)}, u32[]{:S(2)}) collective-permute-start(bf16[2,3,96,384]{3,2,1,0:T(8,128)(2,1)} %get-tuple-element.52.refs_1_), channel_id=1, source_target_pairs={{0,16},{8,24},{16,0},{24,8},{1,17},{9,25},{17,1},{25,9},{2,18},{10... | collective-permute-start | bytes 1327112 | tf_op jit(solution)/shard_map/ppermute | solution.py:404
  41.6 17.8 %collective-permute-start.8 = (bf16[2,3,96,384]{3,2,1,0:T(8,128)(2,1)S(1)}, bf16[2,3,96,384]{3,2,1,0:T(8,128)(2,1)S(1)}, u32[]{:S(2)}, u32[]{:S(2)}) collective-permute-start(bf16[2,3,96,384]{3,2,1,0:T(8,128)(2,1)S(1)} %broadcast_select_fusion.6), channel_id=1, source_target_pairs={{0,8},{8,0},{16,24},{24,16},{1,9},{9,1},{17,25},{25,17},{2,10},{10... | collective-permute-start | bytes 1327112 | tf_op jit(solution)/shard_map/ppermute | solution.py:404
  42.8 16.6 %collective-permute-start.9 = (bf16[2,3,96,384]{3,2,1,0:T(8,128)(2,1)S(1)}, bf16[2,3,96,384]{3,2,1,0:T(8,128)(2,1)S(1)}, u32[]{:S(2)}, u32[]{:S(2)}) collective-permute-start(bf16[2,3,96,384]{3,2,1,0:T(8,128)(2,1)S(1)} %broadcast_select_fusion.4), channel_id=1, source_target_pairs={{0,16},{8,24},{16,0},{24,8},{1,17},{9,25},{17,1},{25,9},{2,18},{10... | collective-permute-start | bytes 1327112 | tf_op jit(solution)/shard_map/ppermute | solution.py:404
  54.1 3.6 %collective-permute-start.7 = (bf16[4,64,768]{2,1,0:T(8,128)(2,1)S(1)}, bf16[4,64,768]{2,1,0:T(8,128)(2,1)S(1)}, u32[]{:S(2)}, u32[]{:S(2)}) collective-permute-start(bf16[4,64,768]{2,1,0:T(8,128)(2,1)S(1)} %get-tuple-element.46), channel_id=1, source_target_pairs={{0,1},{1,0},{2,3},{3,2},{4,5},{5,4},{6,7},{7,6},{8,9},{9,8},{10,11... | collective-permute-start | bytes 1179656 | tf_op jit(solution)/shard_map/ppermute | solution.py:404
  55.3 13.4 %collective-permute-start.13 = (bf16[2,3,96,384]{3,2,1,0:T(8,128)(2,1)S(1)}, bf16[2,3,96,384]{3,2,1,0:T(8,128)(2,1)S(1)}, u32[]{:S(2)}, u32[]{:S(2)}) collective-permute-start(bf16[2,3,96,384]{3,2,1,0:T(8,128)(2,1)S(1)} %broadcast_select_fusion.3), channel_id=1, source_target_pairs={{0,16},{8,24},{16,0},{24,8},{1,17},{9,25},{17,1},{25,9},{2,18},{10... | collective-permute-start | bytes 1327112 | tf_op jit(solution)/shard_map/ppermute | solution.py:404
  56.5 13.2 %collective-permute-start.14 = (bf16[2,3,96,384]{3,2,1,0:T(8,128)(2,1)S(1)}, bf16[2,3,96,384]{3,2,1,0:T(8,128)(2,1)S(1)}, u32[]{:S(2)}, u32[]{:S(2)}) collective-permute-start(bf16[2,3,96,384]{3,2,1,0:T(8,128)(2,1)S(1)} %broadcast_select_fusion.1), channel_id=1, source_target_pairs={{0,8},{8,0},{16,24},{24,16},{1,9},{9,1},{17,25},{25,17},{2,10},{10... | collective-permute-start | bytes 1327112 | tf_op jit(solution)/shard_map/ppermute | solution.py:404
  57.8 23.3 %collective-permute-start.15 = (bf16[2,64,768]{2,1,0:T(8,128)(2,1)S(1)}, bf16[2,64,768]{2,1,0:T(8,128)(2,1)S(1)}, u32[]{:S(2)}, u32[]{:S(2)}) collective-permute-start(bf16[2,64,768]{2,1,0:T(8,128)(2,1)S(1)} %get-tuple-element.73), channel_id=1, source_target_pairs={{0,2},{1,3},{2,0},{3,1},{4,6},{5,7},{6,4},{7,5},{8,10},{9,11},{10,... | collective-permute-start | bytes 589832 | tf_op jit(solution)/shard_map/ppermute | solution.py:404
  68.6 2.4 %collective-permute-start.10 = (bf16[4,64,768]{2,1,0:T(8,128)(2,1)S(1)}, bf16[4,64,768]{2,1,0:T(8,128)(2,1)S(1)}, u32[]{:S(2)}, u32[]{:S(2)}) collective-permute-start(bf16[4,64,768]{2,1,0:T(8,128)(2,1)S(1)} %get-tuple-element.49), channel_id=1, source_target_pairs={{0,1},{1,0},{2,3},{3,2},{4,5},{5,4},{6,7},{7,6},{8,9},{9,8},{10,11... | collective-permute-start | bytes 1179656 | tf_op jit(solution)/shard_map/ppermute | solution.py:404
  68.7 15.3 %collective-permute-start.18 = (bf16[2,3,96,384]{3,2,1,0:T(8,128)(2,1)S(1)}, bf16[2,3,96,384]{3,2,1,0:T(8,128)(2,1)S(1)}, u32[]{:S(2)}, u32[]{:S(2)}) collective-permute-start(bf16[2,3,96,384]{3,2,1,0:T(8,128)(2,1)S(1)} %broadcast_select_fusion.2), channel_id=1, source_target_pairs={{0,8},{8,0},{16,24},{24,16},{1,9},{9,1},{17,25},{25,17},{2,10},{10... | collective-permute-start | bytes 1327112 | tf_op jit(solution)/shard_map/ppermute | solution.py:404
  69.8 14.2 %collective-permute-start.19 = (bf16[2,3,96,384]{3,2,1,0:T(8,128)(2,1)S(1)}, bf16[2,3,96,384]{3,2,1,0:T(8,128)(2,1)S(1)}, u32[]{:S(2)}, u32[]{:S(2)}) collective-permute-start(bf16[2,3,96,384]{3,2,1,0:T(8,128)(2,1)S(1)} %broadcast_select_fusion), channel_id=1, source_target_pairs={{0,16},{8,24},{16,0},{24,8},{1,17},{9,25},{17,1},{25,9},{2,18},{10... | collective-permute-start | bytes 1327112 | tf_op jit(solution)/shard_map/ppermute | solution.py:404
  71.1 10.1 %collective-permute-start.16 = (bf16[2,64,768]{2,1,0:T(8,128)(2,1)S(1)}, bf16[2,64,768]{2,1,0:T(8,128)(2,1)S(1)}, u32[]{:S(2)}, u32[]{:S(2)}) collective-permute-start(bf16[2,64,768]{2,1,0:T(8,128)(2,1)S(1)} %get-tuple-element.72), channel_id=1, source_target_pairs={{0,2},{1,3},{2,0},{3,1},{4,6},{5,7},{6,4},{7,5},{8,10},{9,11},{10,... | collective-permute-start | bytes 589832 | tf_op jit(solution)/shard_map/ppermute | solution.py:404
  81.0 1.8 %collective-permute-start.17 = (bf16[4,64,768]{2,1,0:T(8,128)(2,1)S(1)}, bf16[4,64,768]{2,1,0:T(8,128)(2,1)S(1)}, u32[]{:S(2)}, u32[]{:S(2)}) collective-permute-start(bf16[4,64,768]{2,1,0:T(8,128)(2,1)S(1)} %get-tuple-element.59), channel_id=1, source_target_pairs={{0,1},{1,0},{2,3},{3,2},{4,5},{5,4},{6,7},{7,6},{8,9},{9,8},{10,11... | collective-permute-start | bytes 1179656 | tf_op jit(solution)/shard_map/ppermute | solution.py:404
  81.3 12.5 %collective-permute-start.21 = (bf16[1,128,768]{2,1,0:T(8,128)(2,1)S(1)}, bf16[1,128,768]{2,1,0:T(8,128)(2,1)S(1)}, u32[]{:S(2)}, u32[]{:S(2)}) collective-permute-start(bf16[1,128,768]{2,1,0:T(8,128)(2,1)S(1)} %get-tuple-element.69), channel_id=1, source_target_pairs={{0,4},{1,5},{2,6},{3,7},{4,0},{5,1},{6,2},{7,3},{8,12},{9,13},{10,... | collective-permute-start | bytes 589832 | tf_op jit(solution)/shard_map/ppermute | solution.py:404
  82.9 10.1 %collective-permute-start.20 = (bf16[2,64,768]{2,1,0:T(8,128)(2,1)S(1)}, bf16[2,64,768]{2,1,0:T(8,128)(2,1)S(1)}, u32[]{:S(2)}, u32[]{:S(2)}) collective-permute-start(bf16[2,64,768]{2,1,0:T(8,128)(2,1)S(1)} %add_convert_fusion.7), channel_id=1, source_target_pairs={{0,2},{1,3},{2,0},{3,1},{4,6},{5,7},{6,4},{7,5},{8,10},{9,11},{10,... | collective-permute-start | bytes 589832 | tf_op jit(solution)/shard_map/ppermute | solution.py:404
  95.2 4.8 %collective-permute-start.23 = (bf16[4,128,768]{2,1,0:T(8,128)(2,1)S(1)}, bf16[4,128,768]{2,1,0:T(8,128)(2,1)S(1)}, u32[]{:S(2)}, u32[]{:S(2)}) collective-permute-start(bf16[4,128,768]{2,1,0:T(8,128)(2,1)S(1)} %screen.2), channel_id=1, source_target_pairs={{0,1},{1,0},{2,3},{3,2},{4,5},{5,4},{6,7},{7,6},{8,9},{9,8},{10,11... | collective-permute-start | bytes 2359304 | tf_op jit(solution)/shard_map/ppermute | solution.py:404
  95.2 2.8 %collective-permute-start.22 = (bf16[4,64,768]{2,1,0:T(8,128)(2,1)S(1)}, bf16[4,64,768]{2,1,0:T(8,128)(2,1)S(1)}, u32[]{:S(2)}, u32[]{:S(2)}) collective-permute-start(bf16[4,64,768]{2,1,0:T(8,128)(2,1)S(1)} %get-tuple-element.63), channel_id=1, source_target_pairs={{0,1},{1,0},{2,3},{3,2},{4,5},{5,4},{6,7},{7,6},{8,9},{9,8},{10,11... | collective-permute-start | bytes 1179656 | tf_op jit(solution)/shard_map/ppermute | solution.py:404
  95.7 14.5 %collective-permute-start.25 = (bf16[2,64,768]{2,1,0:T(8,128)(2,1)S(1)}, bf16[2,64,768]{2,1,0:T(8,128)(2,1)S(1)}, u32[]{:S(2)}, u32[]{:S(2)}) collective-permute-start(bf16[2,64,768]{2,1,0:T(8,128)(2,1)S(1)} %add_convert_fusion.5.refs_2_), channel_id=1, source_target_pairs={{0,4},{1,5},{2,6},{3,7},{4,0},{5,1},{6,2},{7,3},{8,12},{9,13},{10,... | collective-permute-start | bytes 589832 | tf_op jit(solution)/shard_map/ppermute | solution.py:404
  98.1 11.9 %collective-permute-start.26 = (bf16[2,64,768]{2,1,0:T(8,128)(2,1)S(1)}, bf16[2,64,768]{2,1,0:T(8,128)(2,1)S(1)}, u32[]{:S(2)}, u32[]{:S(2)}) collective-permute-start(bf16[2,64,768]{2,1,0:T(8,128)(2,1)S(1)} %add_convert_fusion.4), channel_id=1, source_target_pairs={{0,2},{1,3},{2,0},{3,1},{4,6},{5,7},{6,4},{7,5},{8,10},{9,11},{10,... | collective-permute-start | bytes 589832 | tf_op jit(solution)/shard_map/ppermute | solution.py:404
  100.1 21.8 %collective-permute-start.24 = (bf16[2,128,768]{2,1,0:T(8,128)(2,1)S(1)}, bf16[2,128,768]{2,1,0:T(8,128)(2,1)S(1)}, u32[]{:S(2)}, u32[]{:S(2)}) collective-permute-start(bf16[2,128,768]{2,1,0:T(8,128)(2,1)S(1)} %get-tuple-element.67), channel_id=1, source_target_pairs={{0,2},{1,3},{2,0},{3,1},{4,6},{5,7},{6,4},{7,5},{8,10},{9,11},{10,... | collective-permute-start | bytes 1179656 | tf_op jit(solution)/shard_map/ppermute | solution.py:404
  110.1 11.0 %collective-permute-start.27 = (bf16[2,64,768]{2,1,0:T(8,128)(2,1)S(1)}, bf16[2,64,768]{2,1,0:T(8,128)(2,1)S(1)}, u32[]{:S(2)}, u32[]{:S(2)}) collective-permute-start(bf16[2,64,768]{2,1,0:T(8,128)(2,1)S(1)} %add_convert_fusion.2.refs_4_), channel_id=1, source_target_pairs={{0,4},{1,5},{2,6},{3,7},{4,0},{5,1},{6,2},{7,3},{8,12},{9,13},{10,... | collective-permute-start | bytes 589832 | tf_op jit(solution)/shard_map/ppermute | solution.py:404
  122.9 1.2 collective-permute-start.28
  124.1 5.5 %collective-permute-start.31 = (f32[8,64]{1,0:T(8,128)S(1)}, f32[8,64]{1,0:T(8,128)S(1)}, u32[]{:S(2)}, u32[]{:S(2)}) collective-permute-start(f32[8,64]{1,0:T(8,128)S(1)} %get-tuple-element.76), channel_id=1, source_target_pairs={{0,6},{1,7},{2,4},{3,5},{4,2},{5,3},{6,0},{7,1},{8,14},{9,15},{10,... | collective-permute-start | bytes 6152 | tf_op jit(solution)/shard_map/ppermute | solution.py:404
  126.1 3.6 %collective-permute-start.30 = (f32[8,64]{1,0:T(8,128)S(1)}, f32[8,64]{1,0:T(8,128)S(1)}, u32[]{:S(2)}, u32[]{:S(2)}) collective-permute-start(f32[8,64]{1,0:T(8,128)S(1)} %get-tuple-element.77), channel_id=1, source_target_pairs={{0,2},{1,3},{2,0},{3,1},{4,6},{5,7},{6,4},{7,5},{8,10},{9,11},{10,... | collective-permute-start | bytes 6152 | tf_op jit(solution)/shard_map/ppermute | solution.py:404
  126.1 4.5 %collective-permute-start.29 = (f32[8,64]{1,0:T(8,128)S(1)}, f32[8,64]{1,0:T(8,128)S(1)}, u32[]{:S(2)}, u32[]{:S(2)}) collective-permute-start(f32[8,64]{1,0:T(8,128)S(1)} %get-tuple-element.75), channel_id=1, source_target_pairs={{0,4},{1,5},{2,6},{3,7},{4,0},{5,1},{6,2},{7,3},{8,12},{9,13},{10,... | collective-permute-start | bytes 6152 | tf_op jit(solution)/shard_map/ppermute | solution.py:404
  (15 other events, 171.0 us)

commit v4 on v3

--- a/solution.py
+++ b/solution.py
@@ -113,7 +113,7 @@
         in_specs=[pl.BlockSpec(memory_space=pl.ANY)],
         out_specs=[pl.BlockSpec(shape, lambda g, b: (0, 0, 0, 0))] * len(firsts),
         scratch_shapes=[
-            pltpu.VMEM((LANES // 128 * together, GRID_N // XG * functions, 128), F32),
+            pltpu.VMEM((LANES // 128 * together, (GRID_N // XG + 1) * functions, 128), F32),
             pltpu.VMEM((slab, functions, size), BF16),
             pltpu.SemaphoreType.DMA((groups,)),
         ],
@@ -193,8 +193,8 @@
                         mixed[kind, at:at + rows, half * LANES:half * LANES + LANES] = out[base:base + rows, i * LANES:i * LANES + LANES]
         for kind in range(classes):
             value = jnp.dot(mixed[kind], ztab[kind], preferred_element_type=F32)
-            section[now, 2 * kind] = value[:, :128]
-            section[now, 2 * kind + 1] = value[:, 128:]
+            section[now, 2 * kind, :value.shape[0], :] = value[:, :128]
+            section[now, 2 * kind + 1, :value.shape[0], :] = value[:, 128:]
         return carry
 
     lax.fori_loop(0, count, sections, 0)
@@ -283,7 +283,7 @@
         scratch_shapes=[
             pltpu.VMEM((count,) + cond.shape[1:], BF16),
             pltpu.VMEM((classes, groups * conds * KF // classes, 2 * LANES), BF16),
-            pltpu.VMEM((count, 2 * classes, groups * conds * KF // classes, XG * KF), F32),
+            pltpu.VMEM((count, 2 * classes, (groups * conds + 1) * KF // classes, XG * KF), F32),
             pltpu.SemaphoreType.DMA((count,)),
         ],
         out_shape=[shape, shape],

time: 132 us -> 132 us (level)
  starting transfers between devices: 31.6 us -> 39.2 us
  other arithmetic: 10.3 us -> 4.27 us
    ppermute x32, starting transfers between devices: 31.6 us -> 39.2 us  [swap(): return lax.ppermute(array, axis, [(i, i ^ mask) for i in range(size)])]
    select_n x8, other arithmetic: 8.31 us -> 2.24 us  [choose(): jnp.where(self.owner, self.own[q], a)]
  transfers between devices with their start and end apart: 32 -> 32, of which waited for: 13 -> 12; matrix products, arithmetic and copies ran while one was open for 8% -> 3% of each run, Pallas kernels for 35% -> 35%
where the time goes in v4:
time: 132 us
  Pallas kernels  54.1 us (41%)
  starting transfers between devices  39.2 us (30%)
  waiting for transfers between devices  27.8 us (21%)
  between operations  5.84 us (4%)
  other arithmetic  4.27 us (3%)
    ppermute x32, starting transfers between devices, swap(): return lax.ppermute(array, axis, [(i, i ^ mask) for i in range(size)])  39.2 us
    pallas_call x4, Pallas kernels, front(): pl.pallas_call(functools.partial(front_kernel, len(sources), find), in_sp...  35.9 us
    ppermute x32, waiting for transfers between devices, swap(): return lax.ppermute(array, axis, [(i, i ^ mask) for i in range(size)])  27.8 us
    pallas_call x3, Pallas kernels, planes(): pl.pallas_call(functools.partial(planes_kernel, firsts), grid_spec=spec,...  12.7 us
    pallas_call x2, Pallas kernels, screen(): pl.pallas_call(functools.partial(screen_kernel, [len(p) for p in parts],...  2.78 us
  transfers between devices with their start and end apart: 32, of which 12 were waited for; matrix products, arithmetic and copies ran while one was open for 3% of the time, Pallas kernels for 35%

profile of v4, /device:TPU:0, one launch (start us, length us, event | category | flops | bytes accessed | tf_op | source)
XLA Modules:
  0.0 131.9 jit_solution(14001450713455303744)
XLA Ops:
  0.0 5.0 %planes.4 = (bf16[2,3,96,384]{3,2,1,0:T(8,128)(2,1)}, bf16[2,3,96,384]{3,2,1,0:T(8,128)(2,1)}) custom-call(s32[2]{0:T(128)} %blocks.11, bf16[12,16,9216]{2,1,0:T(8,128)(2,1)} %bitcast.27), custom_call_target="tpu_custom_call" | custom-call | bytes 7077888 | tf_op jit(solution)/shard_map/planes/pallas_call | solution.py:121
  5.0 3.0 %collective-permute-start = (bf16[2,3,96,384]{3,2,1,0:T(8,128)(2,1)}, bf16[2,3,96,384]{3,2,1,0:T(8,128)(2,1)}, u32[]{:S(2)}, u32[]{:S(2)}) collective-permute-start(bf16[2,3,96,384]{3,2,1,0:T(8,128)(2,1)} %get-tuple-element.37.refs_0_), channel_id=1, source_target_pairs={{0,8},{8,0},{16,24},{24,16},{1,9},{9,1},{17,25},{25,17},{2,10},{10... | collective-permute-start | bytes 1327112 | tf_op jit(solution)/shard_map/ppermute | solution.py:404
  8.0 1.5 %collective-permute-start.2 = (bf16[2,3,96,384]{3,2,1,0:T(8,128)(2,1)}, bf16[2,3,96,384]{3,2,1,0:T(8,128)(2,1)}, u32[]{:S(2)}, u32[]{:S(2)}) collective-permute-start(bf16[2,3,96,384]{3,2,1,0:T(8,128)(2,1)} %get-tuple-element.39.refs_1_), channel_id=1, source_target_pairs={{0,16},{8,24},{16,0},{24,8},{1,17},{9,25},{17,1},{25,9},{2,18},{10... | collective-permute-start | bytes 1327112 | tf_op jit(solution)/shard_map/ppermute | solution.py:404
  9.5 5.5 %planes.3 = (bf16[2,3,96,384]{3,2,1,0:T(8,128)(2,1)}, bf16[2,3,96,384]{3,2,1,0:T(8,128)(2,1)}, bf16[2,3,96,384]{3,2,1,0:T(8,128)(2,1)S(1)}, bf16[2,3,96,384]{3,2...) custom-call(s32[2]{0:T(128)S(1)} %copy-done.3, ...), custom_call_target="tpu_custom_call" | custom-call | bytes 7077888 | tf_op jit(solution)/shard_map/planes/pallas_call | solution.py:121
  19.4 2.8 %collective-permute-start.1 = (bf16[2,3,96,384]{3,2,1,0:T(8,128)(2,1)}, bf16[2,3,96,384]{3,2,1,0:T(8,128)(2,1)}, u32[]{:S(2)}, u32[]{:S(2)}) collective-permute-start(bf16[2,3,96,384]{3,2,1,0:T(8,128)(2,1)} %broadcast_select_fusion.7), channel_id=1, source_target_pairs={{0,16},{8,24},{16,0},{24,8},{1,17},{9,25},{17,1},{25,9},{2,18},{10... | collective-permute-start | bytes 1327112 | tf_op jit(solution)/shard_map/ppermute | solution.py:404
  23.0 2.5 %collective-permute-start.3 = (bf16[2,3,96,384]{3,2,1,0:T(8,128)(2,1)}, bf16[2,3,96,384]{3,2,1,0:T(8,128)(2,1)}, u32[]{:S(2)}, u32[]{:S(2)}) collective-permute-start(bf16[2,3,96,384]{3,2,1,0:T(8,128)(2,1)} %broadcast_select_fusion.5), channel_id=1, source_target_pairs={{0,8},{8,0},{16,24},{24,16},{1,9},{9,1},{17,25},{25,17},{2,10},{10... | collective-permute-start | bytes 1327112 | tf_op jit(solution)/shard_map/ppermute | solution.py:404
  25.5 1.6 %collective-permute-start.5 = (s32[2,768]{1,0:T(2,128)S(1)}, s32[2,768]{1,0:T(2,128)S(1)}, u32[]{:S(2)}, u32[]{:S(2)}) collective-permute-start(s32[2,768]{1,0:T(2,128)S(1)} %pad_add_fusion.1), channel_id=1, source_target_pairs={{0,2},{1,3},{2,0},{3,1},{4,6},{5,7},{6,4},{7,5},{8,10},{9,11},{10,... | collective-permute-start | bytes 18440 | tf_op jit(solution)/shard_map/ppermute | solution.py:404
  27.2 2.0 %collective-permute-done.5 = s32[2,768]{1,0:T(2,128)S(1)} collective-permute-done((s32[2,768]{1,0:T(2,128)S(1)}, s32[2,768]{1,0:T(2,128)S(1)}, u32[]{:S(2)}, u32[]{:S(2)}) %collective-permute-start.5) | collective-permute-done | bytes 6176 | tf_op jit(solution)/shard_map/ppermute | solution.py:404
  29.9 2.7 %collective-permute-start.6 = (s32[4,768]{1,0:T(4,128)S(1)}, s32[4,768]{1,0:T(4,128)}, u32[]{:S(2)}, u32[]{:S(2)}) collective-permute-start(s32[4,768]{1,0:T(4,128)S(1)} %pad_add_fusion.refs_0_), channel_id=1, source_target_pairs={{0,4},{1,5},{2,6},{3,7},{4,0},{5,1},{6,2},{7,3},{8,12},{9,13},{10,... | collective-permute-start | bytes 36872 | tf_op jit(solution)/shard_map/ppermute | solution.py:404
  32.6 1.2 collective-permute-start.11
  37.0 2.2 %planes.5.refs_6_.refs_4_ = bf16[8,3,96,384]{3,2,1,0:T(8,128)(2,1)S(1)} custom-call(s32[2]{0:T(128)S(1)} %copy-done.3, bf16[12,8,9216]{2,1,0:T(8,128)(2,1)S(1)} %bitcast.29), custom_call_target="tpu_custom_call" | custom-call | bytes 3538944 | tf_op jit(solution)/shard_map/planes/pallas_call | solution.py:121
  39.3 1.7 %tables.1 = (bf16[8,128,768]{2,1,0:T(8,128)(2,1)S(1)}, f32[8,16,768]{2,1,0:T(8,128)S(1)}) custom-call(s32[4,768]{1,0:T(4,128)S(1)} %pad_add_fusion.refs_0_, s32[4,768]{1,0:T(4,128)} %collective-permute-done.6.refs_1_, bf16[8,2,16,32]{3,2,1,0:T(8,128)(2,1)S(1)} %copy-done.2), custom_call_target="tpu_custom_call" | custom-call | bytes 2359296 | tf_op jit(solution)/shard_map/tables/pallas_call | solution.py:149
  41.1 1.9 %collective-permute-start.8 = (bf16[2,3,96,384]{3,2,1,0:T(8,128)(2,1)S(1)}, bf16[2,3,96,384]{3,2,1,0:T(8,128)(2,1)S(1)}, u32[]{:S(2)}, u32[]{:S(2)}) collective-permute-start(bf16[2,3,96,384]{3,2,1,0:T(8,128)(2,1)S(1)} %broadcast_select_fusion.6), channel_id=1, source_target_pairs={{0,8},{8,0},{16,24},{24,16},{1,9},{9,1},{17,25},{25,17},{2,10},{10... | collective-permute-start | bytes 1327112 | tf_op jit(solution)/shard_map/ppermute | solution.py:404
  43.2 2.6 %collective-permute-start.9 = (bf16[2,3,96,384]{3,2,1,0:T(8,128)(2,1)S(1)}, bf16[2,3,96,384]{3,2,1,0:T(8,128)(2,1)S(1)}, u32[]{:S(2)}, u32[]{:S(2)}) collective-permute-start(bf16[2,3,96,384]{3,2,1,0:T(8,128)(2,1)S(1)} %broadcast_select_fusion.4), channel_id=1, source_target_pairs={{0,16},{8,24},{16,0},{24,8},{1,17},{9,25},{17,1},{25,9},{2,18},{10... | collective-permute-start | bytes 1327112 | tf_op jit(solution)/shard_map/ppermute | solution.py:404
  45.8 8.9 %front.4 = (bf16[4,64,768]{2,1,0:T(8,128)(2,1)S(1)}, bf16[4,64,768]{2,1,0:T(8,128)(2,1)S(1)}) custom-call(s32[2]{0:T(128)S(1)} %copy-done.3, s32[16]{0:T(128)S(1)} %copy-done.9, bf16[2,3,96,384]{3,2,1,0:T(8,128)(2,1)S(1)} %copy-done.5, bf16[2,3,96,384]{3,2,1,0:T(8,128)(2,1)S(1)} %copy-done.6, bf16[2,3,96,384]{3,2,1,0:T(8,128)(2,1)} %collective-permute-done.refs_2_, ...), custom_call_target="tpu_custom_call" | custom-call | flops 3600000000 | bytes 8000000 | tf_op jit(solution)/shard_map/front/pallas_call | solution.py:279
  55.8 2.2 %collective-permute-start.14 = (bf16[2,3,96,384]{3,2,1,0:T(8,128)(2,1)S(1)}, bf16[2,3,96,384]{3,2,1,0:T(8,128)(2,1)S(1)}, u32[]{:S(2)}, u32[]{:S(2)}) collective-permute-start(bf16[2,3,96,384]{3,2,1,0:T(8,128)(2,1)S(1)} %broadcast_select_fusion.1), channel_id=1, source_target_pairs={{0,8},{8,0},{16,24},{24,16},{1,9},{9,1},{17,25},{25,17},{2,10},{10... | collective-permute-start | bytes 1327112 | tf_op jit(solution)/shard_map/ppermute | solution.py:404
  58.2 1.6 %collective-permute-start.15 = (bf16[2,64,768]{2,1,0:T(8,128)(2,1)S(1)}, bf16[2,64,768]{2,1,0:T(8,128)(2,1)S(1)}, u32[]{:S(2)}, u32[]{:S(2)}) collective-permute-start(bf16[2,64,768]{2,1,0:T(8,128)(2,1)S(1)} %get-tuple-element.73), channel_id=1, source_target_pairs={{0,2},{1,3},{2,0},{3,1},{4,6},{5,7},{6,4},{7,5},{8,10},{9,11},{10,... | collective-permute-start | bytes 589832 | tf_op jit(solution)/shard_map/ppermute | solution.py:404
  59.8 9.1 %front.5 = (bf16[4,64,768]{2,1,0:T(8,128)(2,1)S(1)}, bf16[4,64,768]{2,1,0:T(8,128)(2,1)S(1)}) custom-call(s32[2]{0:T(128)S(1)} %copy-done.3, s32[16]{0:T(128)S(1)} %copy-done.9, bf16[2,3,96,384]{3,2,1,0:T(8,128)(2,1)S(1)} %get-tuple-element.38.refs_0_, bf16[2,3,96,384]{3,2,1,0:T(8,128)(2,1)S(1)} %get-tuple-element.36.refs_1_, ...), custom_call_target="tpu_custom_call" | custom-call | flops 3600000000 | bytes 8000000 | tf_op jit(solution)/shard_map/front/pallas_call | solution.py:279
  69.6 1.9 %collective-permute-start.19 = (bf16[2,3,96,384]{3,2,1,0:T(8,128)(2,1)S(1)}, bf16[2,3,96,384]{3,2,1,0:T(8,128)(2,1)S(1)}, u32[]{:S(2)}, u32[]{:S(2)}) collective-permute-start(bf16[2,3,96,384]{3,2,1,0:T(8,128)(2,1)S(1)} %broadcast_select_fusion), channel_id=1, source_target_pairs={{0,16},{8,24},{16,0},{24,8},{1,17},{9,25},{17,1},{25,9},{2,18},{10... | collective-permute-start | bytes 1327112 | tf_op jit(solution)/shard_map/ppermute | solution.py:404
  72.5 8.9 %front.6 = (bf16[4,64,768]{2,1,0:T(8,128)(2,1)S(1)}, bf16[4,64,768]{2,1,0:T(8,128)(2,1)S(1)}) custom-call(s32[2]{0:T(128)S(1)} %copy-done.3, s32[16]{0:T(128)S(1)} %copy-done.9, bf16[2,3,96,384]{3,2,1,0:T(8,128)(2,1)} %get-tuple-element.51.refs_0_, bf16[2,3,96,384]{3,2,1,0:T(8,128)(2,1)} %get-tuple-element.52.refs_1_, ...), custom_call_target="tpu_custom_call" | custom-call | flops 3600000000 | bytes 8000000 | tf_op jit(solution)/shard_map/front/pallas_call | solution.py:279
  82.0 1.1 collective-permute-done.17
  83.2 1.3 collective-permute-start.20
  84.5 8.9 %front.7 = (bf16[4,64,768]{2,1,0:T(8,128)(2,1)S(1)}, bf16[4,64,768]{2,1,0:T(8,128)(2,1)S(1)}) custom-call(s32[2]{0:T(128)S(1)} %copy-done.3, s32[16]{0:T(128)S(1)} %copy-done.9, bf16[2,3,96,384]{3,2,1,0:T(8,128)(2,1)S(1)} %get-tuple-element.54.refs_0_, bf16[2,3,96,384]{3,2,1,0:T(8,128)(2,1)S(1)} %get-tuple-element.50.refs_1_, ...), custom_call_target="tpu_custom_call" | custom-call | flops 3600000000 | bytes 8000000 | tf_op jit(solution)/shard_map/front/pallas_call | solution.py:279
  94.1 1.4 %screen.2 = bf16[4,128,768]{2,1,0:T(8,128)(2,1)S(1)} custom-call(bf16[128,768]{1,0:T(8,128)(2,1)S(1)} %get-tuple-element.64.refs_0_, bf16[128,768]{1,0:T(8,128)(2,1)S(1)} %bitcast.30, bf16[768,6144]{1,0:T(8,128)(2,1)S(1)} %bitcast.26), custom_call_target="tpu_custom_call" | custom-call | flops 603979776 | bytes 4718592 | tf_op jit(solution)/shard_map/screen/pallas_call | solution.py:330
  96.1 1.4 %collective-permute-start.25 = (bf16[2,64,768]{2,1,0:T(8,128)(2,1)S(1)}, bf16[2,64,768]{2,1,0:T(8,128)(2,1)S(1)}, u32[]{:S(2)}, u32[]{:S(2)}) collective-permute-start(bf16[2,64,768]{2,1,0:T(8,128)(2,1)S(1)} %add_convert_fusion.5.refs_2_), channel_id=1, source_target_pairs={{0,4},{1,5},{2,6},{3,7},{4,0},{5,1},{6,2},{7,3},{8,12},{9,13},{10,... | collective-permute-start | bytes 589832 | tf_op jit(solution)/shard_map/ppermute | solution.py:404
  99.1 1.4 %screen.3 = bf16[4,128,768]{2,1,0:T(8,128)(2,1)S(1)} custom-call(bf16[128,768]{1,0:T(8,128)(2,1)S(1)} %get-tuple-element.64.refs_0_, bf16[128,768]{1,0:T(8,128)(2,1)S(1)} %bitcast.31, bf16[768,6144]{1,0:T(8,128)(2,1)S(1)} %bitcast.26), custom_call_target="tpu_custom_call" | custom-call | flops 603979776 | bytes 4718592 | tf_op jit(solution)/shard_map/screen/pallas_call | solution.py:330
  100.7 1.6 %collective-permute-start.24 = (bf16[2,128,768]{2,1,0:T(8,128)(2,1)S(1)}, bf16[2,128,768]{2,1,0:T(8,128)(2,1)S(1)}, u32[]{:S(2)}, u32[]{:S(2)}) collective-permute-start(bf16[2,128,768]{2,1,0:T(8,128)(2,1)S(1)} %get-tuple-element.67), channel_id=1, source_target_pairs={{0,2},{1,3},{2,0},{3,1},{4,6},{5,7},{6,4},{7,5},{8,10},{9,11},{10,... | collective-permute-start | bytes 1179656 | tf_op jit(solution)/shard_map/ppermute | solution.py:404
  102.2 8.1 %collective-permute-done.26 = bf16[2,64,768]{2,1,0:T(8,128)(2,1)S(1)} collective-permute-done((bf16[2,64,768]{2,1,0:T(8,128)(2,1)S(1)}, bf16[2,64,768]{2,1,0:T(8,128)(2,1)S(1)}, u32[]{:S(2)}, u32[]{:S(2)}) %collective-permute-start.26) | collective-permute-done | bytes 196640 | tf_op jit(solution)/shard_map/ppermute | solution.py:404
  110.9 10.5 %collective-permute-done.27 = bf16[2,64,768]{2,1,0:T(8,128)(2,1)S(1)} collective-permute-done((bf16[2,64,768]{2,1,0:T(8,128)(2,1)S(1)}, bf16[2,64,768]{2,1,0:T(8,128)(2,1)S(1)}, u32[]{:S(2)}, u32[]{:S(2)}) %collective-permute-start.27) | collective-permute-done | bytes 196640 | tf_op jit(solution)/shard_map/ppermute | solution.py:404
  123.3 1.2 collective-permute-done.28
  124.5 2.3 %collective-permute-start.31 = (f32[8,64]{1,0:T(8,128)S(1)}, f32[8,64]{1,0:T(8,128)S(1)}, u32[]{:S(2)}, u32[]{:S(2)}) collective-permute-start(f32[8,64]{1,0:T(8,128)S(1)} %get-tuple-element.76), channel_id=1, source_target_pairs={{0,6},{1,7},{2,4},{3,5},{4,2},{5,3},{6,0},{7,1},{8,14},{9,15},{10,... | collective-permute-start | bytes 6152 | tf_op jit(solution)/shard_map/ppermute | solution.py:404
  126.8 2.1 %collective-permute-start.29 = (f32[8,64]{1,0:T(8,128)S(1)}, f32[8,64]{1,0:T(8,128)S(1)}, u32[]{:S(2)}, u32[]{:S(2)}) collective-permute-start(f32[8,64]{1,0:T(8,128)S(1)} %get-tuple-element.75), channel_id=1, source_target_pairs={{0,4},{1,5},{2,6},{3,7},{4,0},{5,1},{6,2},{7,3},{8,12},{9,13},{10,... | collective-permute-start | bytes 6152 | tf_op jit(solution)/shard_map/ppermute | solution.py:404
  (101 shorter events, 15.8 us)
Async XLA Ops:
  5.0 13.5 %collective-permute-start = (bf16[2,3,96,384]{3,2,1,0:T(8,128)(2,1)}, bf16[2,3,96,384]{3,2,1,0:T(8,128)(2,1)}, u32[]{:S(2)}, u32[]{:S(2)}) collective-permute-start(bf16[2,3,96,384]{3,2,1,0:T(8,128)(2,1)} %get-tuple-element.37.refs_0_), channel_id=1, source_target_pairs={{0,8},{8,0},{16,24},{24,16},{1,9},{9,1},{17,25},{25,17},{2,10},{10... | collective-permute-start | bytes 1327112 | tf_op jit(solution)/shard_map/ppermute | solution.py:404
  8.0 14.2 %collective-permute-start.2 = (bf16[2,3,96,384]{3,2,1,0:T(8,128)(2,1)}, bf16[2,3,96,384]{3,2,1,0:T(8,128)(2,1)}, u32[]{:S(2)}, u32[]{:S(2)}) collective-permute-start(bf16[2,3,96,384]{3,2,1,0:T(8,128)(2,1)} %get-tuple-element.39.refs_1_), channel_id=1, source_target_pairs={{0,16},{8,24},{16,0},{24,8},{1,17},{9,25},{17,1},{25,9},{2,18},{10... | collective-permute-start | bytes 1327112 | tf_op jit(solution)/shard_map/ppermute | solution.py:404
  19.4 21.7 %collective-permute-start.1 = (bf16[2,3,96,384]{3,2,1,0:T(8,128)(2,1)}, bf16[2,3,96,384]{3,2,1,0:T(8,128)(2,1)}, u32[]{:S(2)}, u32[]{:S(2)}) collective-permute-start(bf16[2,3,96,384]{3,2,1,0:T(8,128)(2,1)} %broadcast_select_fusion.7), channel_id=1, source_target_pairs={{0,16},{8,24},{16,0},{24,8},{1,17},{9,25},{17,1},{25,9},{2,18},{10... | collective-permute-start | bytes 1327112 | tf_op jit(solution)/shard_map/ppermute | solution.py:404
  23.0 2.5 %collective-permute-start.4 = (s32[1,768]{1,0:T(1,128)S(1)}, s32[1,768]{1,0:T(1,128)S(1)}, u32[]{:S(2)}, u32[]{:S(2)}) collective-permute-start(s32[1,768]{1,0:T(1,128)S(1)} %reshape.3), channel_id=1, source_target_pairs={{0,1},{1,0},{2,3},{3,2},{4,5},{5,4},{6,7},{7,6},{8,9},{9,8},{10,11... | collective-permute-start | bytes 9224 | tf_op jit(solution)/shard_map/ppermute | solution.py:404
  23.0 20.1 %collective-permute-start.3 = (bf16[2,3,96,384]{3,2,1,0:T(8,128)(2,1)}, bf16[2,3,96,384]{3,2,1,0:T(8,128)(2,1)}, u32[]{:S(2)}, u32[]{:S(2)}) collective-permute-start(bf16[2,3,96,384]{3,2,1,0:T(8,128)(2,1)} %broadcast_select_fusion.5), channel_id=1, source_target_pairs={{0,8},{8,0},{16,24},{24,16},{1,9},{9,1},{17,25},{25,17},{2,10},{10... | collective-permute-start | bytes 1327112 | tf_op jit(solution)/shard_map/ppermute | solution.py:404
  25.5 3.7 %collective-permute-start.5 = (s32[2,768]{1,0:T(2,128)S(1)}, s32[2,768]{1,0:T(2,128)S(1)}, u32[]{:S(2)}, u32[]{:S(2)}) collective-permute-start(s32[2,768]{1,0:T(2,128)S(1)} %pad_add_fusion.1), channel_id=1, source_target_pairs={{0,2},{1,3},{2,0},{3,1},{4,6},{5,7},{6,4},{7,5},{8,10},{9,11},{10,... | collective-permute-start | bytes 18440 | tf_op jit(solution)/shard_map/ppermute | solution.py:404
  29.9 9.4 %collective-permute-start.6 = (s32[4,768]{1,0:T(4,128)S(1)}, s32[4,768]{1,0:T(4,128)}, u32[]{:S(2)}, u32[]{:S(2)}) collective-permute-start(s32[4,768]{1,0:T(4,128)S(1)} %pad_add_fusion.refs_0_), channel_id=1, source_target_pairs={{0,4},{1,5},{2,6},{3,7},{4,0},{5,1},{6,2},{7,3},{8,12},{9,13},{10,... | collective-permute-start | bytes 36872 | tf_op jit(solution)/shard_map/ppermute | solution.py:404
  32.6 22.2 %collective-permute-start.11 = (bf16[2,3,96,384]{3,2,1,0:T(8,128)(2,1)}, bf16[2,3,96,384]{3,2,1,0:T(8,128)(2,1)}, u32[]{:S(2)}, u32[]{:S(2)}) collective-permute-start(bf16[2,3,96,384]{3,2,1,0:T(8,128)(2,1)} %get-tuple-element.51.refs_0_), channel_id=1, source_target_pairs={{0,8},{8,0},{16,24},{24,16},{1,9},{9,1},{17,25},{25,17},{2,10},{10... | collective-permute-start | bytes 1327112 | tf_op jit(solution)/shard_map/ppermute | solution.py:404
  33.7 21.1 %collective-permute-start.12 = (bf16[2,3,96,384]{3,2,1,0:T(8,128)(2,1)}, bf16[2,3,96,384]{3,2,1,0:T(8,128)(2,1)}, u32[]{:S(2)}, u32[]{:S(2)}) collective-permute-start(bf16[2,3,96,384]{3,2,1,0:T(8,128)(2,1)} %get-tuple-element.52.refs_1_), channel_id=1, source_target_pairs={{0,16},{8,24},{16,0},{24,8},{1,17},{9,25},{17,1},{25,9},{2,18},{10... | collective-permute-start | bytes 1327112 | tf_op jit(solution)/shard_map/ppermute | solution.py:404
  41.1 18.7 %collective-permute-start.8 = (bf16[2,3,96,384]{3,2,1,0:T(8,128)(2,1)S(1)}, bf16[2,3,96,384]{3,2,1,0:T(8,128)(2,1)S(1)}, u32[]{:S(2)}, u32[]{:S(2)}) collective-permute-start(bf16[2,3,96,384]{3,2,1,0:T(8,128)(2,1)S(1)} %broadcast_select_fusion.6), channel_id=1, source_target_pairs={{0,8},{8,0},{16,24},{24,16},{1,9},{9,1},{17,25},{25,17},{2,10},{10... | collective-permute-start | bytes 1327112 | tf_op jit(solution)/shard_map/ppermute | solution.py:404
  43.2 16.6 %collective-permute-start.9 = (bf16[2,3,96,384]{3,2,1,0:T(8,128)(2,1)S(1)}, bf16[2,3,96,384]{3,2,1,0:T(8,128)(2,1)S(1)}, u32[]{:S(2)}, u32[]{:S(2)}) collective-permute-start(bf16[2,3,96,384]{3,2,1,0:T(8,128)(2,1)S(1)} %broadcast_select_fusion.4), channel_id=1, source_target_pairs={{0,16},{8,24},{16,0},{24,8},{1,17},{9,25},{17,1},{25,9},{2,18},{10... | collective-permute-start | bytes 1327112 | tf_op jit(solution)/shard_map/ppermute | solution.py:404
  54.7 3.3 %collective-permute-start.7 = (bf16[4,64,768]{2,1,0:T(8,128)(2,1)S(1)}, bf16[4,64,768]{2,1,0:T(8,128)(2,1)S(1)}, u32[]{:S(2)}, u32[]{:S(2)}) collective-permute-start(bf16[4,64,768]{2,1,0:T(8,128)(2,1)S(1)} %get-tuple-element.46), channel_id=1, source_target_pairs={{0,1},{1,0},{2,3},{3,2},{4,5},{5,4},{6,7},{7,6},{8,9},{9,8},{10,11... | collective-permute-start | bytes 1179656 | tf_op jit(solution)/shard_map/ppermute | solution.py:404
  54.9 14.1 %collective-permute-start.13 = (bf16[2,3,96,384]{3,2,1,0:T(8,128)(2,1)S(1)}, bf16[2,3,96,384]{3,2,1,0:T(8,128)(2,1)S(1)}, u32[]{:S(2)}, u32[]{:S(2)}) collective-permute-start(bf16[2,3,96,384]{3,2,1,0:T(8,128)(2,1)S(1)} %broadcast_select_fusion.3), channel_id=1, source_target_pairs={{0,16},{8,24},{16,0},{24,8},{1,17},{9,25},{17,1},{25,9},{2,18},{10... | collective-permute-start | bytes 1327112 | tf_op jit(solution)/shard_map/ppermute | solution.py:404
  55.8 13.7 %collective-permute-start.14 = (bf16[2,3,96,384]{3,2,1,0:T(8,128)(2,1)S(1)}, bf16[2,3,96,384]{3,2,1,0:T(8,128)(2,1)S(1)}, u32[]{:S(2)}, u32[]{:S(2)}) collective-permute-start(bf16[2,3,96,384]{3,2,1,0:T(8,128)(2,1)S(1)} %broadcast_select_fusion.1), channel_id=1, source_target_pairs={{0,8},{8,0},{16,24},{24,16},{1,9},{9,1},{17,25},{25,17},{2,10},{10... | collective-permute-start | bytes 1327112 | tf_op jit(solution)/shard_map/ppermute | solution.py:404
  58.2 23.3 %collective-permute-start.15 = (bf16[2,64,768]{2,1,0:T(8,128)(2,1)S(1)}, bf16[2,64,768]{2,1,0:T(8,128)(2,1)S(1)}, u32[]{:S(2)}, u32[]{:S(2)}) collective-permute-start(bf16[2,64,768]{2,1,0:T(8,128)(2,1)S(1)} %get-tuple-element.73), channel_id=1, source_target_pairs={{0,2},{1,3},{2,0},{3,1},{4,6},{5,7},{6,4},{7,5},{8,10},{9,11},{10,... | collective-permute-start | bytes 589832 | tf_op jit(solution)/shard_map/ppermute | solution.py:404
  68.9 2.5 %collective-permute-start.10 = (bf16[4,64,768]{2,1,0:T(8,128)(2,1)S(1)}, bf16[4,64,768]{2,1,0:T(8,128)(2,1)S(1)}, u32[]{:S(2)}, u32[]{:S(2)}) collective-permute-start(bf16[4,64,768]{2,1,0:T(8,128)(2,1)S(1)} %get-tuple-element.49), channel_id=1, source_target_pairs={{0,1},{1,0},{2,3},{3,2},{4,5},{5,4},{6,7},{7,6},{8,9},{9,8},{10,11... | collective-permute-start | bytes 1179656 | tf_op jit(solution)/shard_map/ppermute | solution.py:404
  69.1 15.4 %collective-permute-start.18 = (bf16[2,3,96,384]{3,2,1,0:T(8,128)(2,1)S(1)}, bf16[2,3,96,384]{3,2,1,0:T(8,128)(2,1)S(1)}, u32[]{:S(2)}, u32[]{:S(2)}) collective-permute-start(bf16[2,3,96,384]{3,2,1,0:T(8,128)(2,1)S(1)} %broadcast_select_fusion.2), channel_id=1, source_target_pairs={{0,8},{8,0},{16,24},{24,16},{1,9},{9,1},{17,25},{25,17},{2,10},{10... | collective-permute-start | bytes 1327112 | tf_op jit(solution)/shard_map/ppermute | solution.py:404
  69.6 14.9 %collective-permute-start.19 = (bf16[2,3,96,384]{3,2,1,0:T(8,128)(2,1)S(1)}, bf16[2,3,96,384]{3,2,1,0:T(8,128)(2,1)S(1)}, u32[]{:S(2)}, u32[]{:S(2)}) collective-permute-start(bf16[2,3,96,384]{3,2,1,0:T(8,128)(2,1)S(1)} %broadcast_select_fusion), channel_id=1, source_target_pairs={{0,16},{8,24},{16,0},{24,8},{1,17},{9,25},{17,1},{25,9},{2,18},{10... | collective-permute-start | bytes 1327112 | tf_op jit(solution)/shard_map/ppermute | solution.py:404
  71.6 9.9 %collective-permute-start.16 = (bf16[2,64,768]{2,1,0:T(8,128)(2,1)S(1)}, bf16[2,64,768]{2,1,0:T(8,128)(2,1)S(1)}, u32[]{:S(2)}, u32[]{:S(2)}) collective-permute-start(bf16[2,64,768]{2,1,0:T(8,128)(2,1)S(1)} %get-tuple-element.72), channel_id=1, source_target_pairs={{0,2},{1,3},{2,0},{3,1},{4,6},{5,7},{6,4},{7,5},{8,10},{9,11},{10,... | collective-permute-start | bytes 589832 | tf_op jit(solution)/shard_map/ppermute | solution.py:404
  81.4 1.8 %collective-permute-start.17 = (bf16[4,64,768]{2,1,0:T(8,128)(2,1)S(1)}, bf16[4,64,768]{2,1,0:T(8,128)(2,1)S(1)}, u32[]{:S(2)}, u32[]{:S(2)}) collective-permute-start(bf16[4,64,768]{2,1,0:T(8,128)(2,1)S(1)} %get-tuple-element.59), channel_id=1, source_target_pairs={{0,1},{1,0},{2,3},{3,2},{4,5},{5,4},{6,7},{7,6},{8,9},{9,8},{10,11... | collective-permute-start | bytes 1179656 | tf_op jit(solution)/shard_map/ppermute | solution.py:404
  81.6 12.5 %collective-permute-start.21 = (bf16[1,128,768]{2,1,0:T(8,128)(2,1)S(1)}, bf16[1,128,768]{2,1,0:T(8,128)(2,1)S(1)}, u32[]{:S(2)}, u32[]{:S(2)}) collective-permute-start(bf16[1,128,768]{2,1,0:T(8,128)(2,1)S(1)} %get-tuple-element.69), channel_id=1, source_target_pairs={{0,4},{1,5},{2,6},{3,7},{4,0},{5,1},{6,2},{7,3},{8,12},{9,13},{10,... | collective-permute-start | bytes 589832 | tf_op jit(solution)/shard_map/ppermute | solution.py:404
  83.2 10.3 %collective-permute-start.20 = (bf16[2,64,768]{2,1,0:T(8,128)(2,1)S(1)}, bf16[2,64,768]{2,1,0:T(8,128)(2,1)S(1)}, u32[]{:S(2)}, u32[]{:S(2)}) collective-permute-start(bf16[2,64,768]{2,1,0:T(8,128)(2,1)S(1)} %add_convert_fusion.7), channel_id=1, source_target_pairs={{0,2},{1,3},{2,0},{3,1},{4,6},{5,7},{6,4},{7,5},{8,10},{9,11},{10,... | collective-permute-start | bytes 589832 | tf_op jit(solution)/shard_map/ppermute | solution.py:404
  95.5 5.0 %collective-permute-start.23 = (bf16[4,128,768]{2,1,0:T(8,128)(2,1)S(1)}, bf16[4,128,768]{2,1,0:T(8,128)(2,1)S(1)}, u32[]{:S(2)}, u32[]{:S(2)}) collective-permute-start(bf16[4,128,768]{2,1,0:T(8,128)(2,1)S(1)} %screen.2), channel_id=1, source_target_pairs={{0,1},{1,0},{2,3},{3,2},{4,5},{5,4},{6,7},{7,6},{8,9},{9,8},{10,11... | collective-permute-start | bytes 2359304 | tf_op jit(solution)/shard_map/ppermute | solution.py:404
  95.6 2.8 %collective-permute-start.22 = (bf16[4,64,768]{2,1,0:T(8,128)(2,1)S(1)}, bf16[4,64,768]{2,1,0:T(8,128)(2,1)S(1)}, u32[]{:S(2)}, u32[]{:S(2)}) collective-permute-start(bf16[4,64,768]{2,1,0:T(8,128)(2,1)S(1)} %get-tuple-element.63), channel_id=1, source_target_pairs={{0,1},{1,0},{2,3},{3,2},{4,5},{5,4},{6,7},{7,6},{8,9},{9,8},{10,11... | collective-permute-start | bytes 1179656 | tf_op jit(solution)/shard_map/ppermute | solution.py:404
  96.1 14.8 %collective-permute-start.25 = (bf16[2,64,768]{2,1,0:T(8,128)(2,1)S(1)}, bf16[2,64,768]{2,1,0:T(8,128)(2,1)S(1)}, u32[]{:S(2)}, u32[]{:S(2)}) collective-permute-start(bf16[2,64,768]{2,1,0:T(8,128)(2,1)S(1)} %add_convert_fusion.5.refs_2_), channel_id=1, source_target_pairs={{0,4},{1,5},{2,6},{3,7},{4,0},{5,1},{6,2},{7,3},{8,12},{9,13},{10,... | collective-permute-start | bytes 589832 | tf_op jit(solution)/shard_map/ppermute | solution.py:404
  98.5 11.9 %collective-permute-start.26 = (bf16[2,64,768]{2,1,0:T(8,128)(2,1)S(1)}, bf16[2,64,768]{2,1,0:T(8,128)(2,1)S(1)}, u32[]{:S(2)}, u32[]{:S(2)}) collective-permute-start(bf16[2,64,768]{2,1,0:T(8,128)(2,1)S(1)} %add_convert_fusion.4), channel_id=1, source_target_pairs={{0,2},{1,3},{2,0},{3,1},{4,6},{5,7},{6,4},{7,5},{8,10},{9,11},{10,... | collective-permute-start | bytes 589832 | tf_op jit(solution)/shard_map/ppermute | solution.py:404
  100.7 21.6 %collective-permute-start.24 = (bf16[2,128,768]{2,1,0:T(8,128)(2,1)S(1)}, bf16[2,128,768]{2,1,0:T(8,128)(2,1)S(1)}, u32[]{:S(2)}, u32[]{:S(2)}) collective-permute-start(bf16[2,128,768]{2,1,0:T(8,128)(2,1)S(1)} %get-tuple-element.67), channel_id=1, source_target_pairs={{0,2},{1,3},{2,0},{3,1},{4,6},{5,7},{6,4},{7,5},{8,10},{9,11},{10,... | collective-permute-start | bytes 1179656 | tf_op jit(solution)/shard_map/ppermute | solution.py:404
  110.5 11.0 %collective-permute-start.27 = (bf16[2,64,768]{2,1,0:T(8,128)(2,1)S(1)}, bf16[2,64,768]{2,1,0:T(8,128)(2,1)S(1)}, u32[]{:S(2)}, u32[]{:S(2)}) collective-permute-start(bf16[2,64,768]{2,1,0:T(8,128)(2,1)S(1)} %add_convert_fusion.2.refs_4_), channel_id=1, source_target_pairs={{0,4},{1,5},{2,6},{3,7},{4,0},{5,1},{6,2},{7,3},{8,12},{9,13},{10,... | collective-permute-start | bytes 589832 | tf_op jit(solution)/shard_map/ppermute | solution.py:404
  123.2 1.2 collective-permute-start.28
  124.5 5.5 %collective-permute-start.31 = (f32[8,64]{1,0:T(8,128)S(1)}, f32[8,64]{1,0:T(8,128)S(1)}, u32[]{:S(2)}, u32[]{:S(2)}) collective-permute-start(f32[8,64]{1,0:T(8,128)S(1)} %get-tuple-element.76), channel_id=1, source_target_pairs={{0,6},{1,7},{2,4},{3,5},{4,2},{5,3},{6,0},{7,1},{8,14},{9,15},{10,... | collective-permute-start | bytes 6152 | tf_op jit(solution)/shard_map/ppermute | solution.py:404
  126.8 3.6 %collective-permute-start.30 = (f32[8,64]{1,0:T(8,128)S(1)}, f32[8,64]{1,0:T(8,128)S(1)}, u32[]{:S(2)}, u32[]{:S(2)}) collective-permute-start(f32[8,64]{1,0:T(8,128)S(1)} %get-tuple-element.77), channel_id=1, source_target_pairs={{0,2},{1,3},{2,0},{3,1},{4,6},{5,7},{6,4},{7,5},{8,10},{9,11},{10,... | collective-permute-start | bytes 6152 | tf_op jit(solution)/shard_map/ppermute | solution.py:404
  126.8 4.5 %collective-permute-start.29 = (f32[8,64]{1,0:T(8,128)S(1)}, f32[8,64]{1,0:T(8,128)S(1)}, u32[]{:S(2)}, u32[]{:S(2)}) collective-permute-start(f32[8,64]{1,0:T(8,128)S(1)} %get-tuple-element.75), channel_id=1, source_target_pairs={{0,4},{1,5},{2,6},{3,7},{4,0},{5,1},{6,2},{7,3},{8,12},{9,13},{10,... | collective-permute-start | bytes 6152 | tf_op jit(solution)/shard_map/ppermute | solution.py:404
  (15 other events, 170.8 us)
